TPU v7x, 32 devices: a whole 2x2x4 slice. The times are simulated.
32 devices in a mesh: dp: 4 (over y, x), head: 8 (over z, core).
Axes of the slice: x: 2, y: 2, z: 4, core: 2. Of those that a mesh axis runs over, the one named last changes fastest.
Arguments:
- stream: bfloat16 [8192, 2048], P(('dp', 'head')), may hold values from -4 to 4
- doc_lengths: int32 [4, 8], P('dp'), may hold values from 1 to 1024, 2048 in all within a row
- premix_gain: bfloat16 [2048], replicated, may hold values from 0.099609375 to 1.8984375
- branch_weight: bfloat16 [2048, 2736], P(None, 'head'), may hold values from -0.125 to 0.125
- input_weight: bfloat16 [2048, 2736], P(None, 'head'), may hold values from -0.125 to 0.125
- conv_kernel: bfloat16 [4, 2736], P(None, 'head'), may hold values from -3 to 3
- conv_bias: bfloat16 [2736], P('head'), may hold values from -3 to 3
- rate_weight: bfloat16 [16, 171, 171], P('head'), may hold values from -0.4375 to 0.4375
- rate_bias: bfloat16 [16, 171], P('head'), may hold values from -3 to 3
- entry_weight: bfloat16 [16, 171, 171], P('head'), may hold values from -0.4375 to 0.4375
- entry_bias: bfloat16 [16, 171], P('head'), may hold values from -3 to 3
- decay_param: bfloat16 [2736], P('head'), may hold values from -9 to -3
- output_weight: bfloat16 [2736, 2048], P('head'), may hold values from -0.625 to 0.625
- preffn_gain: bfloat16 [2048], replicated, may hold values from 0.099609375 to 1.8984375
- ffn_gate: bfloat16 [2048, 6144], P(None, 'head'), may hold values from -0.125 to 0.125
- ffn_upward: bfloat16 [2048, 6144], P(None, 'head'), may hold values from -1 to 1
- ffn_down: bfloat16 [2048, 6144], P(None, 'head'), may hold values from -1 to 1
- cotangent: bfloat16 [8192, 2048], P(('dp', 'head')), may hold values from -4 to 4
Outputs:
- layer_out: bfloat16 [8192, 2048], P(('dp', 'head'))
- stream_grad: bfloat16 [8192, 2048], P(('dp', 'head'))
- premix_grad: float32 [2048], replicated
- branch_grad: float32 [2048, 2736], P(None, 'head')
- input_grad: float32 [2048, 2736], P(None, 'head')
- kernel_grad: float32 [4, 2736], P(None, 'head')
- convbias_grad: float32 [2736], P('head')
- rate_grad: float32 [16, 171, 171], P('head')
- ratebias_grad: float32 [16, 171], P('head')
- entry_grad: float32 [16, 171, 171], P('head')
- entrybias_grad: float32 [16, 171], P('head')
- decay_grad: float32 [2736], P('head')
- output_grad: float32 [2736, 2048], P('head')
- preffn_grad: float32 [2048], replicated
- ffngate_grad: float32 [2048, 6144], P('dp', 'head')
- ffnupward_grad: float32 [2048, 6144], P('dp', 'head')
- ffndown_grad: float32 [2048, 6144], P('dp', 'head')
Inputs may be any that keep to these rules, and one draw needn't show every extreme that they name: `doc_lengths`: each row's 8 document lengths add up to 2048, and the longest is exactly 1024.
All inputs are finite; a program needn't handle non-finite values.
Results may differ from a plain program's by a relative error of at most 0.025.
Values may be sent and summed in bfloat16 or wider, within the bound.
A program may use at most 576 MiB of HBM per device.

v0:
```python
import jax
import jax.numpy as jnp
from jax import lax
from jax.sharding import PartitionSpec as P

CONVW = 4
SEQ = 2048


EPSILON = 1e-06
HIGHEST = lax.Precision.HIGHEST
DECAY_SCALE = 8.0


def rms_norm(values, scales):
    return values * lax.rsqrt(jnp.mean(values * values, axis=-1, keepdims=True) + EPSILON) * scales


def gated_unit(gate_pre, upward_pre):
    return jax.nn.gelu(gate_pre) * upward_pre


def doc_masks(lengths, length):
    starts = jnp.cumsum(lengths, axis=1) - lengths
    places = jnp.arange(length, dtype=jnp.int32)
    resets = jnp.any(starts[:, :, None] == places[None, None, :], axis=1)
    earlier = jnp.where(starts[:, :, None] <= places[None, None, :], starts[:, :, None], 0)
    begins = jnp.max(earlier, axis=1)
    shifts = jnp.arange(CONVW, dtype=jnp.int32)
    inside = places[None, :, None] - shifts[None, None, :] >= begins[:, :, None]
    return (resets, inside.astype(jnp.float32))


def block_states(log_decay, driven, resets):
    row_count, length, width = driven.shape
    span = min(128, length)
    count = length // span
    places = jnp.arange(span, dtype=jnp.int32)
    lower = places[:, None] >= places[None, :]

    def one_block(carry, index):
        first = index * span
        decay_part = lax.dynamic_slice_in_dim(log_decay, first, span, 1)
        driven_part = lax.dynamic_slice_in_dim(driven, first, span, 1)
        reset_part = lax.dynamic_slice_in_dim(resets, first, span, 1).astype(jnp.int32)
        segment = jnp.cumsum(reset_part, axis=1)
        summed = jnp.cumsum(decay_part, axis=1)
        same = (segment[:, :, None] == segment[:, None, :]) & lower[None, :, :]
        spread = summed[:, :, None, :] - summed[:, None, :, :]
        factors = jnp.where(
            same[:, :, :, None], jnp.exp(jnp.where(same[:, :, :, None], spread, 0.0)), 0.0
        )
        inner = jnp.einsum("rtjc,rjc->rtc", factors, driven_part, precision=HIGHEST)
        leading = (segment == 0)[:, :, None]
        states = inner + jnp.where(leading, jnp.exp(summed), 0.0) * carry[:, None, :]
        return (states[:, -1, :], states)

    start = jnp.zeros((row_count, width), jnp.float32)
    _, pieces = lax.scan(jax.checkpoint(one_block), start, jnp.arange(count, dtype=jnp.int32))
    return jnp.moveaxis(pieces, 0, 1).reshape(row_count, length, width)


def recurrence(
    branch_pre,
    input_pre,
    kernel,
    kernel_bias,
    rate_weight,
    rate_bias,
    entry_weight,
    entry_bias,
    decay_param,
    resets,
    inside,
):
    length = input_pre.shape[1]
    convolved = kernel_bias + kernel[0] * input_pre
    for offset in range(1, kernel.shape[0]):
        shifted = jnp.pad(input_pre, ((0, 0), (offset, 0), (0, 0)))[:, :length]
        convolved = convolved + kernel[offset] * shifted * inside[:, :, offset : offset + 1]
    blocks = convolved.reshape(
        convolved.shape[0], length, rate_weight.shape[0], rate_weight.shape[1]
    )
    rate_gate = jax.nn.sigmoid(
        jnp.einsum("rthc,hcd->rthd", blocks, rate_weight, precision=HIGHEST) + rate_bias
    ).reshape(convolved.shape)
    entry_gate = jax.nn.sigmoid(
        jnp.einsum("rthc,hcd->rthd", blocks, entry_weight, precision=HIGHEST) + entry_bias
    ).reshape(convolved.shape)
    log_decay = -DECAY_SCALE * jax.nn.softplus(decay_param) * rate_gate
    scaling = jnp.where(resets[:, :, None], 1.0, jnp.sqrt(-jnp.expm1(2.0 * log_decay)))
    states = block_states(log_decay, scaling * entry_gate * convolved, resets)
    return states * jax.nn.gelu(branch_pre)


def contract_cols(leading, trailing):
    return lax.dot_general(
        leading, trailing, (((1,), (1,)), ((), ())), preferred_element_type=jnp.float32
    )


def contract_rows(leading, trailing):
    return lax.dot_general(
        leading, trailing, (((0,), (0,)), ((), ())), preferred_element_type=jnp.float32
    )


def shards(
    stream,
    doc_lengths,
    premix_gain,
    branch_weight,
    input_weight,
    conv_kernel,
    conv_bias,
    rate_weight,
    rate_bias,
    entry_weight,
    entry_bias,
    decay_param,
    output_weight,
    preffn_gain,
    ffn_gate,
    ffn_upward,
    ffn_down,
    cotangent,
):
    resets, inside = doc_masks(doc_lengths, SEQ)
    row_count = doc_lengths.shape[0]
    chan_width = branch_weight.shape[1]
    inflow = stream.astype(jnp.float32)
    normed, premix_back = jax.vjp(rms_norm, inflow, premix_gain.astype(jnp.float32))
    normed_low = normed.astype(jnp.bfloat16)
    normed_rows = lax.all_gather(normed_low, "head", axis=0, tiled=True)
    branch_pre = jnp.dot(normed_rows, branch_weight, preferred_element_type=jnp.float32).reshape(
        row_count, SEQ, chan_width
    )
    input_pre = jnp.dot(normed_rows, input_weight, preferred_element_type=jnp.float32).reshape(
        row_count, SEQ, chan_width
    )

    def mixer_core(
        branch_part, input_part, kernel, kernel_bias, rate_w, rate_b, entry_w, entry_b, decay_part
    ):
        return recurrence(
            branch_part,
            input_part,
            kernel,
            kernel_bias,
            rate_w,
            rate_b,
            entry_w,
            entry_b,
            decay_part,
            resets,
            inside,
        )

    gated_out, mixer_back = jax.vjp(
        mixer_core,
        branch_pre,
        input_pre,
        conv_kernel.astype(jnp.float32),
        conv_bias.astype(jnp.float32),
        rate_weight.astype(jnp.float32),
        rate_bias.astype(jnp.float32),
        entry_weight.astype(jnp.float32),
        entry_bias.astype(jnp.float32),
        decay_param.astype(jnp.float32),
    )
    gated_low = gated_out.reshape(-1, chan_width).astype(jnp.bfloat16)
    mixer_out = lax.psum_scatter(
        jnp.dot(gated_low, output_weight, preferred_element_type=jnp.float32).astype(jnp.bfloat16),
        "head",
        scatter_dimension=0,
        tiled=True,
    ).astype(jnp.float32)
    hidden_in = inflow + mixer_out
    ffn_normed, preffn_back = jax.vjp(rms_norm, hidden_in, preffn_gain.astype(jnp.float32))
    ffn_low = ffn_normed.astype(jnp.bfloat16)
    upstream = cotangent.astype(jnp.float32)
    gate_piece = lax.all_gather(ffn_gate, "head", axis=1, tiled=True)
    upward_piece = lax.all_gather(ffn_upward, "head", axis=1, tiled=True)
    down_piece = lax.all_gather(ffn_down, "head", axis=1, tiled=True)
    gate_pre = jnp.dot(ffn_low, gate_piece, preferred_element_type=jnp.float32)
    upward_pre = jnp.dot(ffn_low, upward_piece, preferred_element_type=jnp.float32)
    hidden_part = gated_unit(gate_pre, upward_pre).astype(jnp.bfloat16)
    running = contract_cols(hidden_part, down_piece)
    ffn_out = running
    layer_out = (hidden_in + ffn_out).astype(jnp.bfloat16)
    gate_piece = lax.all_gather(ffn_gate, "head", axis=1, tiled=True)
    upward_piece = lax.all_gather(ffn_upward, "head", axis=1, tiled=True)
    down_piece = lax.all_gather(ffn_down, "head", axis=1, tiled=True)
    hidden_grad = jnp.dot(cotangent, down_piece, preferred_element_type=jnp.float32)
    _, unit_back = jax.vjp(gated_unit, gate_pre, upward_pre)
    gate_grad, upward_grad = unit_back(hidden_grad)
    gate_low = gate_grad.astype(jnp.bfloat16)
    upward_low = upward_grad.astype(jnp.bfloat16)
    running = contract_cols(gate_low, gate_piece) + contract_cols(upward_low, upward_piece)
    hidden_part = gated_unit(gate_pre, upward_pre).astype(jnp.bfloat16)
    weight_terms = lax.psum_scatter(
        jnp.stack(
            [
                contract_rows(gate_low, ffn_low),
                contract_rows(upward_low, ffn_low),
                contract_rows(hidden_part, cotangent),
            ],
            axis=1,
        ).astype(jnp.bfloat16),
        "head",
        scatter_dimension=0,
        tiled=True,
    )
    weight_sums = lax.psum_scatter(weight_terms, "dp", scatter_dimension=2, tiled=True).astype(
        jnp.float32
    )
    hidden_back, preffn_scale_grad = preffn_back(running)
    resid_grad = upstream + hidden_back
    resid_low = resid_grad.astype(jnp.bfloat16)
    grad_rows = lax.all_gather(resid_low, "head", axis=0, tiled=True)
    gated_grad = contract_cols(grad_rows, output_weight)
    output_weight_grad = contract_rows(gated_low, grad_rows)
    mixer_grads = mixer_back(gated_grad.reshape(row_count, SEQ, chan_width))
    branch_low = mixer_grads[0].reshape(-1, chan_width).astype(jnp.bfloat16)
    input_low = mixer_grads[1].reshape(-1, chan_width).astype(jnp.bfloat16)
    branch_weight_grad = contract_rows(normed_rows, branch_low)
    input_weight_grad = contract_rows(normed_rows, input_low)
    branch_part = branch_low
    input_part = input_low
    normed_first_grad = lax.psum_scatter(
        (
            contract_cols(branch_part, branch_weight) + contract_cols(input_part, input_weight)
        ).astype(jnp.bfloat16),
        "head",
        scatter_dimension=0,
        tiled=True,
    ).astype(jnp.float32)
    stream_back, premix_scale_grad = premix_back(normed_first_grad)
    stream_grad = (resid_grad + stream_back).astype(jnp.bfloat16)
    summed = (
        lax.psum(branch_weight_grad.astype(jnp.bfloat16), "dp").astype(jnp.float32),
        lax.psum(input_weight_grad.astype(jnp.bfloat16), "dp").astype(jnp.float32),
        lax.psum(mixer_grads[2].astype(jnp.bfloat16), "dp").astype(jnp.float32),
        lax.psum(mixer_grads[3].astype(jnp.bfloat16), "dp").astype(jnp.float32),
        lax.psum(mixer_grads[4].astype(jnp.bfloat16), "dp").astype(jnp.float32),
        lax.psum(mixer_grads[5].astype(jnp.bfloat16), "dp").astype(jnp.float32),
        lax.psum(mixer_grads[6].astype(jnp.bfloat16), "dp").astype(jnp.float32),
        lax.psum(mixer_grads[7].astype(jnp.bfloat16), "dp").astype(jnp.float32),
        lax.psum(mixer_grads[8].astype(jnp.bfloat16), "dp").astype(jnp.float32),
        lax.psum(output_weight_grad.astype(jnp.bfloat16), "dp").astype(jnp.float32),
    )
    gain_sums = lax.psum((premix_scale_grad, preffn_scale_grad), ("dp", "head"))
    return (
        layer_out,
        stream_grad,
        gain_sums[0],
        summed[0],
        summed[1],
        summed[2],
        summed[3],
        summed[4],
        summed[5],
        summed[6],
        summed[7],
        summed[8],
        summed[9],
        gain_sums[1],
        weight_sums[:, 0, :].T,
        weight_sums[:, 1, :].T,
        weight_sums[:, 2, :].T,
    )


def solution(mesh):
    placed = (
        P(("dp", "head"), None),
        P("dp", None),
        P(),
        P(None, "head"),
        P(None, "head"),
        P(None, "head"),
        P("head"),
        P("head", None, None),
        P("head", None),
        P("head", None, None),
        P("head", None),
        P("head"),
        P("head", None),
        P(),
        P(None, "head"),
        P(None, "head"),
        P(None, "head"),
        P(("dp", "head"), None),
    )
    return jax.shard_map(
        shards,
        mesh=mesh,
        in_specs=placed,
        out_specs=(
            P(("dp", "head"), None),
            P(("dp", "head"), None),
            P(),
            P(None, "head"),
            P(None, "head"),
            P(None, "head"),
            P("head"),
            P("head", None, None),
            P("head", None),
            P("head", None, None),
            P("head", None),
            P("head"),
            P("head", None),
            P(),
            P("dp", "head"),
            P("dp", "head"),
            P("dp", "head"),
        ),
        check_vma=False,
    )
```

profile of v0, /device:TPU:0, one launch (start us, length us, event | category | flops | bytes accessed | tf_op | source)
XLA Modules:
  0.0 2573.4 jit_solution(12147986305082307592)
XLA Ops:
  14.1 84.1 %all-gather.6.cloned.1.call-done = bf16[2048,2048]{1,0:T(8,128)(2,1)} async-done(((bf16[256,2048]{1,0:T(8,128)(2,1)}), bf16[2048,2048]{1,0:T(8,128)(2,1)}) %all-gather.6.cloned.1.call-update) | async-done | bytes 8388624 | tf_op jit(solution)/shard_map/all_gather | solution.py:134
  143.2 328.7 %while.36 = (s32[]{:T(128)}, f32[1,342]{1,0:T(1,128)S(1)}, f32[16,1,128,342]{3,2,1,0:T(8,128)}, f32[16,1,342]{2,1,0:T(1,128)}, s32[16]{0:T(128)S(1)}, /*index=5*...) while((s32[]{:T(128)}, f32[1,342]{1,0:T(1,128)S(1)}, ...), condition=%wide.region_7.8_spmd.clone, body=%wide.region_4.7_spmd.clone.sunk | while | flops 33729412 | bytes 3046011 | solution.py:59
  148.0 15.0 multiply_reduce_fusion.14
  168.5 15.0 multiply_reduce_fusion.14
  189.0 15.0 multiply_reduce_fusion.14
  209.6 15.0 multiply_reduce_fusion.14
  230.1 15.0 multiply_reduce_fusion.14
  250.6 15.0 multiply_reduce_fusion.14
  271.2 15.0 multiply_reduce_fusion.14
  291.7 15.0 multiply_reduce_fusion.14
  312.2 15.0 multiply_reduce_fusion.14
  332.7 15.0 multiply_reduce_fusion.14
  353.3 15.0 multiply_reduce_fusion.14
  373.8 15.0 multiply_reduce_fusion.14
  394.3 15.0 multiply_reduce_fusion.14
  414.9 15.0 multiply_reduce_fusion.14
  435.4 15.0 multiply_reduce_fusion.14
  456.0 15.0 multiply_reduce_fusion.14
  496.9 86.3 %reduce-scatter.5.cloned.1.call-done = bf16[256,2048]{1,0:T(8,128)(2,1)} async-done(((bf16[2048,2048]{1,0:T(8,128)(2,1)}), bf16[256,2048]{1,0:T(8,128)(2,1)}) %reduce-scatter.5.cloned.1.call-update) | async-done | bytes 1048592 | tf_op jit(solution)/shard_map/reduce_scatter | solution.py:172
  586.4 216.6 %all-gather.10.cloned.1.call-done = bf16[2048,6144]{1,0:T(8,128)(2,1)} async-done(((bf16[2048,768]{1,0:T(8,128)(2,1)}), bf16[2048,6144]{1,0:T(8,128)(2,1)}) %all-gather.10.cloned.1.call-update) | async-done | bytes 25165840 | tf_op jit(solution)/shard_map/all_gather | solution.py:183
  803.1 15.9 fusion.92
  819.0 203.6 %all-gather.8.cloned.1.call-done = bf16[2048,6144]{1,0:T(8,128)(2,1)} async-done(((bf16[2048,768]{1,0:T(8,128)(2,1)}), bf16[2048,6144]{1,0:T(8,128)(2,1)}) %all-gather.8.cloned.1.call-update) | async-done | bytes 25165840 | tf_op jit(solution)/shard_map/all_gather | solution.py:182
  1022.6 15.5 fusion.91
  1038.2 204.0 %all-gather.12.cloned.1.call-done = bf16[2048,6144]{1,0:T(8,128)(2,1)} async-done(((bf16[2048,768]{1,0:T(8,128)(2,1)}), bf16[2048,6144]{1,0:T(8,128)(2,1)}) %all-gather.12.cloned.1.call-update) | async-done | bytes 25165840 | tf_op jit(solution)/shard_map/all_gather | solution.py:184
  1242.2 20.8 multiply_convert_fusion
  1276.7 14.9 multiply_reduce_fusion.8
  1296.0 14.8 convert_bitcast_fusion.1
  1338.7 50.1 %pad_maximum_fusion = bf16[6144,3,2048]{2,0,1:T(8,128)(2,1)} fusion(bf16[6144,1,2048]{2,0,1:T(8,128)(2,1)} %convert_bitcast_fusion, bf16[6144,1,2048]{2,0,1:T(8,128)(2,1)} %convert_bitcast_fusion.1, bf16[6144,1,2048]{2,0,1:T(8,128)(2,1)} %convert_bitcast_fusion.2), kind=kLoop, calls=%fused_computation.42 | loop fusion | flops 75497472 | bytes 150994944 | tf_op jit(solution)/shard_map/stack | solution.py:202
  1409.1 773.4 %while.37 = (s32[]{:T(128)}, f32[1,2048,342]{1,2,0:T(8,128)}, f32[1,2048,342]{1,2,0:T(8,128)}, f32[1,342]{1,0:T(1,128)S(1)}, f32[16,1,342]{2,1,0:T(1,128)}, /*in...) while((s32[]{:T(128)}, f32[1,2048,342]{1,2,0:T(8,128)}, ...), condition=%wide.region_18.19_spmd.clone, body=%wide.region_11.18_spmd.clone.sunk | while | flops 84465456 | bytes 10083847 | solution.py:59
  1417.7 14.2 multiply_reduce_fusion.15
  1431.9 20.5 fusion.144
  1466.0 14.2 multiply_reduce_fusion.15
  1480.2 20.5 fusion.144
  1514.4 14.2 multiply_reduce_fusion.15
  1528.6 20.5 fusion.144
  1562.7 14.2 multiply_reduce_fusion.15
  1576.9 20.5 fusion.144
  1611.0 14.2 multiply_reduce_fusion.15
  1625.2 20.5 fusion.144
  1659.3 14.2 multiply_reduce_fusion.15
  1673.5 20.5 fusion.144
  1707.6 14.2 multiply_reduce_fusion.15
  1721.9 20.5 fusion.144
  1756.1 14.2 multiply_reduce_fusion.15
  1770.3 20.5 fusion.144
  1804.4 14.2 multiply_reduce_fusion.15
  1818.6 20.5 fusion.144
  1852.7 14.2 multiply_reduce_fusion.15
  1866.9 20.5 fusion.144
  1901.0 14.2 multiply_reduce_fusion.15
  1915.2 20.5 fusion.144
  1949.3 14.2 multiply_reduce_fusion.15
  1963.6 20.5 fusion.144
  1997.6 14.2 multiply_reduce_fusion.15
  2011.9 20.5 fusion.144
  2045.9 14.2 multiply_reduce_fusion.15
  2060.2 20.5 fusion.144
  2108.5 20.5 fusion.144
  2142.6 14.2 multiply_reduce_fusion.15
  2156.8 20.5 fusion.144
  2308.8 55.8 %all-reduce.16.cloned.1.call-done = (bf16[2,171,171]{2,1,0:T(8,128)(2,1)}, bf16[2,171,171]{2,1,0:T(8,128)(2,1)}, bf16[2048,342]{0,1:T(8,128)(2,1)}, bf16[2048,342]{0,1:T(8,128)(2,1)}, bf16[342,2048]{1,0:T(8,128)(2,1)}) async-done(((bf16[2,171,171]{2,1,0:T(8,128)(2,1)}, bf16[2,171,171]{2,1,0:T(8,128)(2,1)}, bf16[2048,342]{0,1:T(8,128)(2,1)}, bf16[2048,342]{0,1:T(8,128)(2,1)}, bf16[342,2048]{1,0:T(8,128)(2,1)}), ...) | async-done | bytes 4436440 | tf_op jit(solution)/shard_map/psum | solution.py:245
  2375.5 81.1 %reduce-scatter.7.cloned.1.call-done = bf16[256,2048]{1,0:T(8,128)(2,1)} async-done(((bf16[2048,2048]{1,0:T(8,128)(2,1)}), bf16[256,2048]{1,0:T(8,128)(2,1)}) %reduce-scatter.7.cloned.1.call-update) | async-done | bytes 1048592 | tf_op jit(solution)/shard_map/reduce_scatter | solution.py:230
  2458.8 38.4 %all-reduce.11 = (f32[2048]{0:T(1024)}, f32[2048]{0:T(1024)}) all-reduce(f32[2048]{0:T(1024)S(1)} %get-tuple-element.556, f32[2048]{0:T(1024)S(1)} %copy-done.58), channel_id=1, replica_groups=mesh['dp'=4,'head'=8] {'dp','head'}, use_global_device_ids=true, to_apply=%region_22.23 | all-reduce | flops 4096 | bytes 32768 | tf_op jit(solution)/shard_map/psum | solution.py:252
  2501.8 52.3 %reduce-scatter.11.cloned.1.call-done = bf16[768,3,512]{2,0,1:T(8,128)(2,1)} async-done(((bf16[768,3,2048]{2,0,1:T(8,128)(2,1)}), bf16[768,3,512]{2,0,1:T(8,128)(2,1)}) %reduce-scatter.11.cloned.1.call-update) | async-done | bytes 2359312 | tf_op jit(solution)/shard_map/reduce_scatter | solution.py:214
  (1026 shorter events, 597.1 us)
Async XLA Ops:
  7.2 480.9 %copy-start = (bf16[342,2048]{1,0:T(8,128)(2,1)S(1)}, bf16[342,2048]{1,0:T(8,128)(2,1)}, u32[]{:S(2)}) copy-start(bf16[342,2048]{1,0:T(8,128)(2,1)} %param.34) | copy-start | bytes 4202500
  7.2 6.2 copy-start.66
  7.2 6.4 copy-start.63
  7.2 6.4 copy-start.64
  7.2 6.4 copy-start.65
  7.2 6.4 copy-start.62
  7.3 6.8 copy-start.60
  7.3 91.0 %copy-start.21 = (bf16[2048,342]{0,1:T(8,128)(2,1)S(1)}, bf16[2048,342]{0,1:T(8,128)(2,1)}, u32[]{:S(2)}) copy-start(bf16[2048,342]{0,1:T(8,128)(2,1)} %param.26) | copy-start | bytes 4202500
  7.3 91.0 %all-gather.6.cloned.1.call-start = ((), (), s32[]{:S(2)}) async-start(), calls=%async_computation.4 | async-start | bytes 9437184 | tf_op jit(solution)/shard_map/all_gather | solution.py:134
  13.4 569.8 %reduce-scatter.5.cloned.1.call-start = ((), (), s32[]{:S(2)}) async-start(), calls=%async_computation.5 | async-start | bytes 9437184 | tf_op jit(solution)/shard_map/reduce_scatter | solution.py:172
  13.8 117.8 %copy-start.37 = (pred[2048]{0:T(1024)(128)(4,1)}, pred[2048]{0:T(1024)(128)(4,1)S(1)}, u32[]{:S(2)}) copy-start(pred[2048]{0:T(1024)(128)(4,1)S(1)} %fusion.70) | copy-start | bytes 6148
  13.9 90.0 %copy-start.41 = (f32[342]{0:T(512)}, f32[342]{0:T(512)S(1)}, u32[]{:S(2)}) copy-start(f32[342]{0:T(512)S(1)} %get-tuple-element.559) | copy-start | bytes 4108
  13.9 90.0 %copy-start.43 = (f32[342]{0:T(512)}, f32[342]{0:T(512)S(1)}, u32[]{:S(2)}) copy-start(f32[342]{0:T(512)S(1)} %get-tuple-element.560) | copy-start | bytes 4108
  13.9 90.0 %copy-start.45 = (f32[342]{0:T(512)}, f32[342]{0:T(512)S(1)}, u32[]{:S(2)}) copy-start(f32[342]{0:T(512)S(1)} %get-tuple-element.561) | copy-start | bytes 4108
  13.9 90.0 %copy-start.47 = (f32[342]{0:T(512)}, f32[342]{0:T(512)S(1)}, u32[]{:S(2)}) copy-start(f32[342]{0:T(512)S(1)} %get-tuple-element.558) | copy-start | bytes 4108
  14.0 117.5 %copy-start.39 = (f32[342]{0:T(512)}, f32[342]{0:T(512)S(1)}, u32[]{:S(2)}) copy-start(f32[342]{0:T(512)S(1)} %broadcast_multiply_fusion.2) | copy-start | bytes 4108
  14.1 89.8 %copy-start.29 = (f32[1,2048,1]{1,2,0:T(1,128)}, f32[1,2048,1]{1,2,0:T(1,128)S(1)}, u32[]{:S(2)}) copy-start(f32[1,2048,1]{1,2,0:T(1,128)S(1)} %get-tuple-element.633) | copy-start | bytes 24580
  14.1 89.8 %copy-start.31 = (f32[1,2048,1]{1,2,0:T(1,128)}, f32[1,2048,1]{1,2,0:T(1,128)S(1)}, u32[]{:S(2)}) copy-start(f32[1,2048,1]{1,2,0:T(1,128)S(1)} %get-tuple-element.634) | copy-start | bytes 24580
  14.1 89.8 %copy-start.33 = (f32[1,2048,1]{1,2,0:T(1,128)}, f32[1,2048,1]{1,2,0:T(1,128)S(1)}, u32[]{:S(2)}) copy-start(f32[1,2048,1]{1,2,0:T(1,128)S(1)} %get-tuple-element.635) | copy-start | bytes 24580
  494.9 308.1 %all-gather.10.cloned.1.call-start = ((), (), s32[]{:S(2)}) async-start(), calls=%async_computation.7 | async-start | bytes 28311552 | tf_op jit(solution)/shard_map/all_gather | solution.py:183
  495.7 87.5 %copy-start.2 = (bf16[256,2048]{1,0:T(8,128)(2,1)S(1)}, bf16[256,2048]{1,0:T(8,128)(2,1)}, u32[]{:S(2)}) copy-start(bf16[256,2048]{1,0:T(8,128)(2,1)} %param.22) | copy-start | bytes 3145732
  495.7 526.9 %all-gather.8.cloned.1.call-start = ((), (), s32[]{:S(2)}) async-start(), calls=%async_computation.6 | async-start | bytes 28311552 | tf_op jit(solution)/shard_map/all_gather | solution.py:182
  496.3 745.9 %all-gather.12.cloned.1.call-start = ((), (), s32[]{:S(2)}) async-start(), calls=%async_computation.8 | async-start | bytes 28311552 | tf_op jit(solution)/shard_map/all_gather | solution.py:184
  496.9 892.1 %all-gather.14.cloned.1.call-start = ((), (), s32[]{:S(2)}) async-start(), calls=%async_computation.9 | async-start | bytes 9437184 | tf_op jit(solution)/shard_map/all_gather | solution.py:220
  496.9 794.7 %copy-start.35 = (f32[2048]{0:T(1024)}, f32[2048]{0:T(1024)S(1)}, u32[]{:S(2)}) copy-start(f32[2048]{0:T(1024)S(1)} %convert_element_type.182) | copy-start | bytes 24580
  585.0 706.7 %copy-start.51 = (f32[256]{0:T(256)}, f32[256]{0:T(256)S(1)}, u32[]{:S(2)}) copy-start(f32[256]{0:T(256)S(1)} %fusion.81) | copy-start | bytes 3076
  1296.0 14.9 copy-start.15
  1296.0 977.9 %reduce-scatter.9.cloned.1.call-start = ((), (), s32[]{:S(2)}) async-start(), calls=%async_computation.11 | async-start | bytes 84934656 | tf_op jit(solution)/shard_map/reduce_scatter | solution.py:201
  1310.9 13.9 copy-start.16
  1388.8 975.7 %all-reduce.16.cloned.1.call-start = ((), (), s32[]{:S(2)}) async-start(), calls=%async_computation.13 | async-start | bytes 9175040 | tf_op jit(solution)/shard_map/psum | solution.py:245
  1409.1 773.4 %copy-start.38 = (pred[2048]{0:T(1024)(128)(4,1)S(1)}, pred[2048]{0:T(1024)(128)(4,1)}, u32[]{:S(2)}) copy-start(pred[2048]{0:T(1024)(128)(4,1)} %copy-done.37) | copy-start | bytes 6148
  2182.5 10.4 copy-start.40
  2198.3 3.7 copy-start.24
  2202.0 4.8 copy-start.6
  2202.0 4.8 copy-start.7
  2202.0 4.8 copy-start.26
  2214.2 7.4 copy-start.4
  2214.2 7.4 copy-start.5
  2214.2 13.5 copy-start.12
  2221.6 6.1 copy-start.8
  2221.6 6.1 copy-start.9
  2221.6 6.1 copy-start.11
  2221.6 6.1 copy-start.30
  2221.7 6.1 copy-start.32
  2221.7 6.1 copy-start.34
  2227.8 5.7 copy-start.42
  2227.8 5.7 copy-start.44
  2227.8 5.7 copy-start.46
  2234.5 10.2 slice-start
  2236.9 7.7 slice-start.1
  2253.2 203.4 %reduce-scatter.7.cloned.1.call-start = ((), (), s32[]{:S(2)}) async-start(), calls=%async_computation.10 | async-start | bytes 9437184 | tf_op jit(solution)/shard_map/reduce_scatter | solution.py:230
  2253.3 9.7 copy-start.22
  2273.8 280.3 %reduce-scatter.11.cloned.1.call-start = ((), (), s32[]{:S(2)}) async-start(), calls=%async_computation.12 | async-start | bytes 11796480 | tf_op jit(solution)/shard_map/reduce_scatter | solution.py:214
  2275.5 13.7 copy-start.61
  2364.5 6.9 copy-start.19
  2373.5 83.1 %copy-start.28 = (f32[2048]{0:T(1024)S(1)}, f32[2048]{0:T(1024)}, u32[]{:S(2)}) copy-start(f32[2048]{0:T(1024)} %copy-done.27) | copy-start | bytes 24580
  2373.5 83.1 %copy-start.50 = (f32[256]{0:T(256)S(1)}, f32[256]{0:T(256)}, u32[]{:S(2)}) copy-start(f32[256]{0:T(256)} %copy-done.49) | copy-start | bytes 3076
  2373.5 85.3 %copy-start.58 = (f32[2048]{0:T(1024)S(1)}, f32[2048]{0:T(1024)}, u32[]{:S(2)}) copy-start(f32[2048]{0:T(1024)} %get-tuple-element.552) | copy-start | bytes 24580
  2373.5 123.7 %copy-start.56 = (f32[256]{0:T(256)S(1)}, f32[256]{0:T(256)}, u32[]{:S(2)}) copy-start(f32[256]{0:T(256)} %copy-done.55) | copy-start | bytes 3076
  2373.5 123.7 %copy-start.17 = (bf16[256,2048]{1,0:T(8,128)(2,1)S(1)}, bf16[256,2048]{1,0:T(8,128)(2,1)}, u32[]{:S(2)}) copy-start(bf16[256,2048]{1,0:T(8,128)(2,1)} %param.39) | copy-start | bytes 3145732
  2373.5 123.7 %copy-start.36 = (f32[2048]{0:T(1024)S(1)}, f32[2048]{0:T(1024)}, u32[]{:S(2)}) copy-start(f32[2048]{0:T(1024)} %copy-done.35) | copy-start | bytes 24580
  2373.5 123.7 %copy-start.52 = (f32[256]{0:T(256)S(1)}, f32[256]{0:T(256)}, u32[]{:S(2)}) copy-start(f32[256]{0:T(256)} %copy-done.51) | copy-start | bytes 3076
  2373.6 123.7 %copy-start.54 = (f32[256]{0:T(256)S(1)}, f32[256]{0:T(256)}, u32[]{:S(2)}) copy-start(f32[256]{0:T(256)} %copy-done.53) | copy-start | bytes 3076
  2561.6 4.7 copy-start.1
  (17 other events, 31.1 us)
Sparse Core Ops, SparseCore 0:
  13.5 84.7 all-gather.5
  495.0 88.1 reduce-scatter.4
  584.8 218.2 all-gather.9
  804.5 218.0 all-gather.7
  1024.1 218.0 all-gather.11
  1296.1 80.2 all-gather.13
  1389.0 717.6 reduce-scatter.8
  2253.3 111.1 all-reduce.15
  2366.9 89.5 reduce-scatter.6
  2459.8 94.2 reduce-scatter.10
where the time goes:
time: 2590 us; the launch traced here: 2570 us
  other arithmetic  1020 us (39%)
  waiting for transfers between devices  986 us (38%)
  matrix products  244 us (9%)
  local copies, waits for them, and re-layouts  238 us (9%)
  blocking collectives  49.1 us (2%)
    while x32, other arithmetic  468 us
    reduce_sum x16, other arithmetic, one_block(): spread = summed[:, :, None, :] - summed[:, None, :, :]  329 us
    all_gather x1, waiting for transfers between devices, shards(): upward_piece = lax.all_gather(ffn_upward, 'head', axis=1, tiled=True)  217 us
    all_gather x1, waiting for transfers between devices, shards(): down_piece = lax.all_gather(ffn_down, 'head', axis=1, tiled=True)  204 us
    all_gather x1, waiting for transfers between devices, shards(): gate_piece = lax.all_gather(ffn_gate, 'head', axis=1, tiled=True)  204 us
    reduce_scatter x1, waiting for transfers between devices, shards(): lax.psum_scatter(jnp.dot(gated_low, output_weight, preferred_element_type...  86.3 us
    all_gather x1, waiting for transfers between devices, shards(): normed_rows = lax.all_gather(normed_low, 'head', axis=0, tiled=True)  84.1 us
    reduce_scatter x1, waiting for transfers between devices, shards(): lax.psum_scatter((contract_cols(branch_part, branch_weight) + contract_co...  81.1 us
  transfers between devices with their start and end apart: 10, of which 8 were waited for; matrix products, arithmetic and copies ran while one was open for 40% of the time, Pallas kernels for 0%

commit v1 on v0

v1 whole, which is shorter than its diff:
```python
import functools
import math

import jax
import jax.numpy as jnp
from jax import lax
from jax.experimental import pallas as pl
from jax.experimental.pallas import tpu as pltpu
from jax.sharding import PartitionSpec as P

CONVW = 4
SEQ = 2048
CHUNK = 256
BLOCK = 64
LANES = 128
HALO = 8

EPSILON = 1e-06
DECAY_SCALE = 8.0
GELU_A = math.sqrt(2.0 / math.pi)
GELU_B = 0.044715

BIAS, TAP, RATE_B, ENTRY_B, DECAY = 0, 1, 5, 6, 7
PARAMS = 8
G_BIAS, G_TAP, G_RATE, G_ENTRY, G_DECAY = 0, 1, 5, 6, 7


def rms_parts(values):
    rinv = lax.rsqrt(jnp.mean(values * values, axis=-1, keepdims=True) + EPSILON)
    return rinv, values * rinv


def norm_back(unit, rinv, gain, grad):
    q = gain * grad
    return rinv * (q - unit * jnp.mean(q * unit, axis=-1, keepdims=True))


def contract_cols(leading, trailing):
    return lax.dot_general(
        leading, trailing, (((1,), (1,)), ((), ())), preferred_element_type=jnp.float32
    )


def contract_rows(leading, trailing):
    return lax.dot_general(
        leading, trailing, (((0,), (0,)), ((), ())), preferred_element_type=jnp.float32
    )


def gelu_pair(v):
    sq = v * v
    th = jnp.tanh(GELU_A * v * (1.0 + GELU_B * sq))
    half = 0.5 * (1.0 + th)
    slope = half + 0.5 * v * (1.0 - th * th) * (GELU_A * (1.0 + 3.0 * GELU_B * sq))
    return v * half, slope


def gelu(v):
    return v * (0.5 * (1.0 + jnp.tanh(GELU_A * v * (1.0 + GELU_B * v * v))))


def decay_terms(rate_gate, slope, fresh):
    log_decay = slope * rate_gate
    c = jnp.exp(log_decay)
    y = 2.0 * log_decay
    series = 1.0 + y * (1.0 / 7.0)
    for n in (6, 5, 4, 3, 2):
        series = 1.0 + (y * (1.0 / n)) * series
    sq = c * c
    q = jnp.where(y > -0.5, -y * series, 1.0 - sq)
    rsq = lax.rsqrt(jnp.maximum(q, 1e-37))
    return (
        jnp.where(fresh, 0.0, c),
        jnp.where(fresh, 1.0, q * rsq),
        jnp.where(fresh, 0.0, sq * rsq),
    )


def rec_fwd_kernel(pre, pos, wg, par, u_out, r_out, e_out, h_out, gated, xbuf, z, carry):
    width = u_out.shape[1]
    tiles = width // LANES

    @pl.when(pl.program_id(0) == 0)
    def _():
        xbuf[0:HALO, :] = jnp.zeros((HALO, width), jnp.float32)
        carry[...] = jnp.zeros_like(carry)

    @pl.when(pl.program_id(0) > 0)
    def _():
        xbuf[0:HALO, :] = xbuf[CHUNK : CHUNK + HALO, :]

    xbuf[HALO : HALO + CHUNK, :] = pre[:, width:]

    def conv_step(i, _):
        row = pl.multiple_of(i * BLOCK, BLOCK)
        place = pos[pl.ds(row, BLOCK), :]
        for t in range(tiles):
            cols = pl.ds(t * LANES, LANES)
            xs = xbuf[pl.ds(row, BLOCK + HALO), cols]
            total = par[BIAS : BIAS + 1, cols] + par[TAP : TAP + 1, cols] * xs[HALO:]
            for k in range(1, CONVW):
                term = par[TAP + k : TAP + k + 1, cols] * xs[HALO - k : HALO - k + BLOCK]
                total = total + jnp.where(place >= k, term, 0.0)
            u_out[pl.ds(row, BLOCK), cols] = total
        return 0

    lax.fori_loop(0, CHUNK // BLOCK, conv_step, 0)
    z[...] = jnp.dot(u_out[...].astype(jnp.bfloat16), wg[...], preferred_element_type=jnp.float32)

    def scan_step(i, _):
        row = pl.multiple_of(i * BLOCK, BLOCK)
        rows = pl.ds(row, BLOCK)
        fresh = pos[rows, :] == 0
        inner = lax.broadcasted_iota(jnp.int32, (BLOCK, LANES), 0) % 8
        for t in range(tiles):
            cols = pl.ds(t * LANES, LANES)
            other = pl.ds(width + t * LANES, LANES)
            r = jax.nn.sigmoid(z[rows, cols] + par[RATE_B : RATE_B + 1, cols])
            e = jax.nn.sigmoid(z[rows, other] + par[ENTRY_B : ENTRY_B + 1, cols])
            u = u_out[rows, cols]
            c, m, _ = decay_terms(r, par[DECAY : DECAY + 1, cols], fresh)
            r_out[rows, cols] = r
            e_out[rows, cols] = e
            b = m * e * u
            for d in (1, 2, 4):
                near = inner >= d
                b = b + c * jnp.where(near, pltpu.roll(b, d, 0), 0.0)
                c = c * jnp.where(near, pltpu.roll(c, d, 0), 1.0)
            last = carry[0:1, cols]
            pieces = []
            for g in range(BLOCK // 8):
                part = slice(g * 8, g * 8 + 8)
                state = b[part] + c[part] * last
                last = state[7:8]
                pieces.append(state)
            carry[0:1, cols] = last
            h = jnp.concatenate(pieces, axis=0)
            h_out[rows, cols] = h
            gated[rows, cols] = (h * gelu(pre[rows, cols])).astype(jnp.bfloat16)
        return 0

    lax.fori_loop(0, CHUNK // BLOCK, scan_step, 0)


def rec_fwd(pre, pos, wg, par):
    length, width = pre.shape[0], pre.shape[1] // 2
    rows = lambda cols: pl.BlockSpec((CHUNK, cols), lambda i: (i, 0))
    whole = lambda a: pl.BlockSpec(a.shape, lambda i: (0,) * a.ndim)
    wide = jax.ShapeDtypeStruct((length, width), jnp.float32)
    return pl.pallas_call(
        rec_fwd_kernel,
        grid=(length // CHUNK,),
        out_shape=(wide, wide, wide, wide, jax.ShapeDtypeStruct((length, width), jnp.bfloat16)),
        in_specs=[rows(2 * width), rows(LANES), whole(wg), whole(par)],
        out_specs=[rows(width)] * 5,
        scratch_shapes=[
            pltpu.VMEM((CHUNK + HALO, width), jnp.float32),
            pltpu.VMEM((CHUNK, 2 * width), jnp.float32),
            pltpu.VMEM((8, width), jnp.float32),
        ],
        compiler_params=pltpu.CompilerParams(vmem_limit_bytes=40 * 2**20),
        name="recurrence_forward",
    )(pre, pos, wg, par)


def rec_bwd_kernel(
    gg, pre, pre_halo, pos, u_in, r_in, e_in, h_in, h_halo, wg, par,
    dpre, dgate, dpar, dz, du, pbuf, carry,
):
    width = u_in.shape[1]
    tiles = width // LANES
    step = pl.program_id(0)

    @pl.when(step == 0)
    def _():
        du[CHUNK:, :] = jnp.zeros((HALO, width), jnp.float32)
        pbuf[CHUNK:, :] = jnp.zeros((HALO, LANES), jnp.int32)
        carry[...] = jnp.zeros_like(carry)
        dgate[...] = jnp.zeros_like(dgate)
        dpar[...] = jnp.zeros_like(dpar)

    @pl.when(step > 0)
    def _():
        du[CHUNK:, :] = du[0:HALO, :]
        pbuf[CHUNK:, :] = pbuf[0:HALO, :]

    pbuf[0:CHUNK, :] = pos[...]

    def total(v):
        return jnp.sum(v, axis=0, keepdims=True)

    def scan_step(j, _):
        i = CHUNK // BLOCK - 1 - j
        row = pl.multiple_of(i * BLOCK, BLOCK)
        rows = pl.ds(row, BLOCK)
        fresh = pos[rows, :] == 0
        place = lax.broadcasted_iota(jnp.int32, (BLOCK, LANES), 0)
        inner = place % 8
        before = pl.multiple_of(jnp.maximum(row - 8, 0), 8)
        for t in range(tiles):
            cols = pl.ds(t * LANES, LANES)
            other = pl.ds(width + t * LANES, LANES)
            r, e, u, h = r_in[rows, cols], e_in[rows, cols], u_in[rows, cols], h_in[rows, cols]
            grad = gg[rows, cols]
            act, slope = gelu_pair(pre[rows, cols])
            dpre[rows, cols] = (grad * h * slope).astype(jnp.bfloat16)
            dh = grad * act
            decay = par[DECAY : DECAY + 1, cols]
            c, m, ratio = decay_terms(r, decay, fresh)
            b, a = c * dh, c
            for d in (1, 2, 4):
                near = inner < 8 - d
                b = b + a * jnp.where(near, pltpu.roll(b, BLOCK - d, 0), 0.0)
                a = a * jnp.where(near, pltpu.roll(a, BLOCK - d, 0), 1.0)
            later = carry[0:1, cols]
            pieces = []
            first = later
            for g in reversed(range(BLOCK // 8)):
                part = slice(g * 8, g * 8 + 8)
                state = b[part] + a[part] * first
                first = state[0:1]
                pieces.append(state)
            carry[0:1, cols] = first
            mu = jnp.concatenate(pieces[::-1], axis=0)
            adj = dh + jnp.where(place == BLOCK - 1, later, pltpu.roll(mu, BLOCK - 1, 0))
            edge = jnp.where(i == 0, h_halo[7:8, cols], h_in[pl.ds(before, 8), cols][7:8])
            prior = jnp.where(place == 0, edge, pltpu.roll(h, 1, 0))
            eu = e * u
            dlog = adj * (prior * c - eu * ratio)
            dpar[G_DECAY : G_DECAY + 1, cols] += total(dlog * r)
            dzr = decay * dlog * (r * (1.0 - r))
            dze = adj * m * eu * (1.0 - e)
            dpar[G_RATE : G_RATE + 1, cols] += total(dzr)
            dpar[G_ENTRY : G_ENTRY + 1, cols] += total(dze)
            dz[rows, cols] = dzr.astype(jnp.bfloat16)
            dz[rows, other] = dze.astype(jnp.bfloat16)
            du[rows, cols] = adj * m * e
        return 0

    lax.fori_loop(0, CHUNK // BLOCK, scan_step, 0)
    du[0:CHUNK, :] += contract_cols(dz[...], wg[...])
    dgate[...] += contract_rows(u_in[...].astype(jnp.bfloat16), dz[...])

    def conv_step(i, _):
        row = pl.multiple_of(i * BLOCK, BLOCK)
        rows = pl.ds(row, BLOCK)
        before = pl.multiple_of(jnp.maximum(row - 8, 0), 8)
        place = pbuf[pl.ds(row, BLOCK + HALO), :]
        for t in range(tiles):
            cols = pl.ds(t * LANES, LANES)
            other = pl.ds(width + t * LANES, LANES)
            ds = du[pl.ds(row, BLOCK + HALO), cols]
            near = ds[0:BLOCK]
            x = pre[rows, other]
            head = jnp.where(i == 0, pre_halo[:, other], pre[pl.ds(before, 8), other])
            xs = jnp.concatenate([head, x], axis=0)
            dx = par[TAP : TAP + 1, cols] * near
            dpar[G_BIAS : G_BIAS + 1, cols] += total(near)
            dpar[G_TAP : G_TAP + 1, cols] += total(near * x)
            for k in range(1, CONVW):
                inside = jnp.where(place >= k, ds, 0.0)
                dx = dx + par[TAP + k : TAP + k + 1, cols] * inside[k : k + BLOCK]
                dpar[G_TAP + k : G_TAP + k + 1, cols] += total(
                    inside[0:BLOCK] * xs[HALO - k : HALO - k + BLOCK]
                )
            dpre[rows, other] = dx.astype(jnp.bfloat16)
        return 0

    lax.fori_loop(0, CHUNK // BLOCK, conv_step, 0)


def rec_bwd(gg, pre, pos, u, r, e, h, wg, par):
    length, width = u.shape
    count = length // CHUNK
    rows = lambda cols: pl.BlockSpec((CHUNK, cols), lambda i: (count - 1 - i, 0))
    halo = lambda cols: pl.BlockSpec(
        (HALO, cols), lambda i: (jnp.maximum((count - 1 - i) * (CHUNK // HALO) - 1, 0), 0)
    )
    whole = lambda shape: pl.BlockSpec(shape, lambda i: (0,) * len(shape))
    return pl.pallas_call(
        rec_bwd_kernel,
        grid=(count,),
        out_shape=(
            jax.ShapeDtypeStruct((length, 2 * width), jnp.bfloat16),
            jax.ShapeDtypeStruct((width, 2 * width), jnp.float32),
            jax.ShapeDtypeStruct((PARAMS, width), jnp.float32),
        ),
        in_specs=[
            rows(width), rows(2 * width), halo(2 * width), rows(LANES),
            rows(width), rows(width), rows(width), rows(width), halo(width),
            whole(wg.shape), whole(par.shape),
        ],
        out_specs=[rows(2 * width), whole((width, 2 * width)), whole((PARAMS, width))],
        scratch_shapes=[
            pltpu.VMEM((CHUNK, 2 * width), jnp.bfloat16),
            pltpu.VMEM((CHUNK + HALO, width), jnp.float32),
            pltpu.VMEM((CHUNK + HALO, LANES), jnp.int32),
            pltpu.VMEM((8, width), jnp.float32),
        ],
        compiler_params=pltpu.CompilerParams(vmem_limit_bytes=40 * 2**20),
        name="recurrence_backward",
    )(gg, pre, pre, pos, u, r, e, h, h, wg, par)


def places(lengths):
    starts = jnp.cumsum(lengths, axis=1) - lengths
    spots = jnp.arange(SEQ, dtype=jnp.int32)
    earlier = jnp.where(starts[:, :, None] <= spots[None, None, :], starts[:, :, None], 0)
    return (spots[None, :] - jnp.max(earlier, axis=1))[0]


def widen(values, width):
    return jnp.pad(values, ((0, 0), (0, width - values.shape[1])))


def block_diagonal(weights, width):
    heads, size = weights.shape[0], weights.shape[1]
    placed = [
        jnp.pad(weights[i], ((i * size, width - (i + 1) * size),) * 2) for i in range(heads)
    ]
    return functools.reduce(jnp.add, placed)


def diagonal_blocks(dense, heads, size):
    return jnp.stack(
        [dense[i * size : (i + 1) * size, i * size : (i + 1) * size] for i in range(heads)]
    )


def shards(
    stream, doc_lengths, premix_gain, branch_weight, input_weight, conv_kernel, conv_bias,
    rate_weight, rate_bias, entry_weight, entry_bias, decay_param, output_weight, preffn_gain,
    ffn_gate, ffn_upward, ffn_down, cotangent,
):
    f32, bf16 = jnp.float32, jnp.bfloat16
    heads, size = rate_bias.shape
    chans = branch_weight.shape[1]
    width = -(-chans // LANES) * LANES
    group = lax.axis_size("dp")

    pos = jnp.broadcast_to(places(doc_lengths)[:, None], (SEQ, LANES))
    slope = -DECAY_SCALE * jax.nn.softplus(decay_param.astype(f32))
    par = jnp.concatenate(
        [
            conv_bias[None].astype(f32),
            conv_kernel.astype(f32),
            rate_bias.reshape(1, -1).astype(f32),
            entry_bias.reshape(1, -1).astype(f32),
            slope[None],
        ]
    )
    par = jnp.pad(par, ((0, 0), (0, width - chans)), constant_values=-1.0)
    par = jnp.where((jnp.arange(width)[None] < chans) | (jnp.arange(PARAMS)[:, None] == DECAY), par, 0.0)
    wg = jnp.concatenate(
        [block_diagonal(rate_weight, width), block_diagonal(entry_weight, width)], axis=1
    )
    wbi = jnp.concatenate([widen(branch_weight, width), widen(input_weight, width)], axis=1)
    wo = jnp.pad(output_weight, ((0, width - chans), (0, 0)))

    inflow = stream.astype(f32)
    premix = premix_gain.astype(f32)
    rinv1, unit1 = rms_parts(inflow)
    normed = (unit1 * premix).astype(bf16)
    normed_rows = lax.all_gather(normed, "head", axis=0, tiled=True)
    pre = jnp.dot(normed_rows, wbi, preferred_element_type=f32)
    u, r, e, h, gated = rec_fwd(pre, pos, wg, par)
    mixer_out = lax.psum_scatter(
        jnp.dot(gated, wo, preferred_element_type=f32).astype(bf16),
        "head", scatter_dimension=0, tiled=True,
    )
    hidden_in = inflow + mixer_out.astype(f32)

    preffn = preffn_gain.astype(f32)
    rinv2, unit2 = rms_parts(hidden_in)
    ffn_low = (unit2 * preffn).astype(bf16)
    cot_rows = lax.all_gather(cotangent, "head", axis=0, tiled=True)
    ffn_rows = lax.all_gather(ffn_low, "head", axis=0, tiled=True)
    gate_pre = jnp.dot(ffn_rows, ffn_gate, preferred_element_type=f32)
    upward_pre = jnp.dot(ffn_rows, ffn_upward, preferred_element_type=f32)
    hidden_grad = jnp.dot(cot_rows, ffn_down, preferred_element_type=f32)
    act, act_slope = gelu_pair(gate_pre)
    hidden_low = (act * upward_pre).astype(bf16)
    gate_low = (hidden_grad * upward_pre * act_slope).astype(bf16)
    upward_low = (hidden_grad * act).astype(bf16)
    back = contract_cols(gate_low, ffn_gate) + contract_cols(upward_low, ffn_upward)
    ffn_grad = lax.psum_scatter(
        back.astype(bf16), "head", scatter_dimension=0, tiled=True
    ).astype(f32)
    ffn_out = lax.psum_scatter(
        contract_cols(hidden_low, ffn_down).astype(bf16), "head", scatter_dimension=0, tiled=True
    )
    layer_out = (hidden_in + ffn_out.astype(f32)).astype(bf16)
    terms = jnp.stack(
        [
            contract_rows(gate_low, ffn_rows),
            contract_rows(upward_low, ffn_rows),
            contract_rows(hidden_low, cot_rows),
        ]
    ).astype(bf16)
    terms = jnp.moveaxis(terms.reshape(3, terms.shape[1], group, -1), 2, 0)
    ffn_sums = lax.psum_scatter(terms, "dp", scatter_dimension=0, tiled=False).astype(f32)

    preffn_grad = jnp.sum(ffn_grad * unit2, axis=0)
    resid_grad = cotangent.astype(f32) + norm_back(unit2, rinv2, preffn, ffn_grad)
    resid_low = resid_grad.astype(bf16)

    grad_rows = lax.all_gather(resid_low, "head", axis=0, tiled=True)
    gated_grad = contract_cols(grad_rows, wo)
    output_grad = contract_rows(gated, grad_rows)[:chans]
    dpre, dgate, dpar = rec_bwd(gated_grad, pre, pos, u, r, e, h, wg, par)
    normed_grad = lax.psum_scatter(
        contract_cols(dpre, wbi).astype(bf16), "head", scatter_dimension=0, tiled=True
    ).astype(f32)
    dwbi = contract_rows(normed_rows, dpre)
    premix_grad = jnp.sum(normed_grad * unit1, axis=0)
    stream_grad = (resid_grad + norm_back(unit1, rinv1, premix, normed_grad)).astype(bf16)

    sums = lax.psum(
        tuple(
            v.astype(bf16)
            for v in (
                dwbi[:, :chans],
                dwbi[:, width : width + chans],
                output_grad,
                diagonal_blocks(dgate[:, :width], heads, size),
                diagonal_blocks(dgate[:, width:], heads, size),
                dpar[:, :chans],
            )
        ),
        "dp",
    )
    branch_grad, input_grad, output_grad, rate_grad, entry_grad, dpar = (
        v.astype(f32) for v in sums
    )
    premix_grad, preffn_grad = lax.psum((premix_grad, preffn_grad), ("dp", "head"))
    decay_grad = dpar[G_DECAY] * (-DECAY_SCALE * jax.nn.sigmoid(decay_param.astype(f32)))
    return (
        layer_out,
        stream_grad,
        premix_grad,
        branch_grad,
        input_grad,
        dpar[G_TAP : G_TAP + CONVW],
        dpar[G_BIAS],
        rate_grad,
        dpar[G_RATE].reshape(heads, size),
        entry_grad,
        dpar[G_ENTRY].reshape(heads, size),
        decay_grad,
        output_grad,
        preffn_grad,
        ffn_sums[0].T,
        ffn_sums[1].T,
        ffn_sums[2].T,
    )


def solution(mesh):
    placed = (
        P(("dp", "head"), None),
        P("dp", None),
        P(),
        P(None, "head"),
        P(None, "head"),
        P(None, "head"),
        P("head"),
        P("head", None, None),
        P("head", None),
        P("head", None, None),
        P("head", None),
        P("head"),
        P("head", None),
        P(),
        P(None, "head"),
        P(None, "head"),
        P(None, "head"),
        P(("dp", "head"), None),
    )
    return jax.shard_map(
        shards,
        mesh=mesh,
        in_specs=placed,
        out_specs=(
            P(("dp", "head"), None),
            P(("dp", "head"), None),
            P(),
            P(None, "head"),
            P(None, "head"),
            P(None, "head"),
            P("head"),
            P("head", None, None),
            P("head", None),
            P("head", None, None),
            P("head", None),
            P("head"),
            P("head", None),
            P(),
            P("dp", "head"),
            P("dp", "head"),
            P("dp", "head"),
        ),
        check_vma=False,
    )
```

time: 2590 us -> 1030 us (0.40)
  other arithmetic: 1020 us -> 46.4 us
  waiting for transfers between devices: 986 us -> 676 us
  local copies, waits for them, and re-layouts: 238 us -> 34.4 us
  matrix products: 244 us -> 156 us
  Pallas kernels: 0 us -> 42.9 us
    all_gather x4 -> x3, waiting for transfers between devices: 708 us -> 224 us  [the longest x1 82.5 us: shards(): normed_rows = lax.all_gather(normed, 'head', axis=0, tiled=True)]
    while x32 -> x0, other arithmetic: 468 us -> none
    reduce_sum x38 -> x4, other arithmetic: 359 us -> 8.99 us  [the longest x2 3.66 us: rms_parts(): jnp.mean(values * values, axis=-1, keepdims=True) + EPSILON]
    another operation x178 -> x4, other arithmetic: 130 us -> 1.94 us  [the longest x2 1.69 us: diagonal_blocks(): jnp.stack([dense[i * size:(i + 1) * size, i * size:(i + 1) * size] for i...]
    reduce_scatter x4, waiting for transfers between devices: 220 us -> 306 us  [the longest x1 88.3 us: shards(): lax.psum_scatter(back.astype(bf16), 'head', scatter_dimension=0, tiled=True)]
    dot_general x12 -> x5, matrix products: 109 us -> 55.7 us  [the longest x1 17 us: shards(): hidden_grad = jnp.dot(cot_rows, ffn_down, preferred_element_type=f32)]
    dynamic_slice x64 -> x0, local copies, waits for them, and re-layouts: 49 us -> none  [the longest x32 30.4 us: one_block(): decay_part = lax.dynamic_slice_in_dim(log_decay, first, span, 1)]
    another operation x133 -> x6, local copies, waits for them, and re-layouts: 62.3 us -> 15.7 us  [the longest x3 14.2 us: shards(): jnp.stack([contract_rows(gate_low, ffn_rows), contract_rows(upward_low, f...]
  transfers between devices with their start and end apart: 10 -> 10, of which waited for: 8 -> 10; matrix products, arithmetic and copies ran while one was open for 40% -> 15% of each run, Pallas kernels for 0% -> 2%
where the time goes in v1:
time: 1030 us; the launch traced here: 1020 us
  waiting for transfers between devices  676 us (66%)
  matrix products  156 us (15%)
  blocking collectives  49 us (5%)
  other arithmetic  46.4 us (5%)
  Pallas kernels  42.9 us (4%)
  local copies, waits for them, and re-layouts  34.4 us (3%)
  between operations  14.8 us (1%)
    psum x1, waiting for transfers between devices, shards(): lax.psum(tuple((v.astype(bf16) for v in (dwbi[:, :chans], dwbi[:, width:w...  100 us
    reduce_scatter x1, waiting for transfers between devices, shards(): lax.psum_scatter(back.astype(bf16), 'head', scatter_dimension=0, tiled=True)  88.3 us
    reduce_scatter x1, waiting for transfers between devices, shards(): lax.psum_scatter(jnp.dot(gated, wo, preferred_element_type=f32).astype(bf...  87.6 us
    all_gather x1, waiting for transfers between devices, shards(): normed_rows = lax.all_gather(normed, 'head', axis=0, tiled=True)  82.5 us
    reduce_scatter x1, waiting for transfers between devices, shards(): lax.psum_scatter(contract_cols(dpre, wbi).astype(bf16), 'head', scatter_d...  81.1 us
    all_gather x1, waiting for transfers between devices, shards(): ffn_rows = lax.all_gather(ffn_low, 'head', axis=0, tiled=True)  79.4 us
    all_gather x1, waiting for transfers between devices, shards(): cot_rows = lax.all_gather(cotangent, 'head', axis=0, tiled=True)  61.8 us
    dot_general x5, matrix products, contract_rows(): lax.dot_general(leading, trailing, (((0,), (0,)), ((), ())), preferred_el...  50.9 us
  transfers between devices with their start and end apart: 10, of which 10 were waited for; matrix products, arithmetic and copies ran while one was open for 15% of the time, Pallas kernels for 2%

profile of v1, /device:TPU:0, one launch (start us, length us, event | category | flops | bytes accessed | tf_op | source)
XLA Modules:
  0.0 1020.8 jit_solution(12650399317963039903)
XLA Ops:
  7.3 1.7 fusion.21
  9.1 0.7 convert_element_type.143
  9.8 0.6 copy-done.18
  10.4 2.5 fusion.18
  14.3 0.9 pad_maximum_fusion.wg
  15.3 82.5 %all-gather.5.cloned.1.call-done = bf16[2048,2048]{1,0:T(8,128)(2,1)} async-done(((bf16[256,2048]{1,0:T(8,128)(2,1)}), bf16[2048,2048]{1,0:T(8,128)(2,1)}) %all-gather.5.cloned.1.call-update) | async-done | bytes 8388624 | tf_op jit(solution)/shard_map/all_gather | solution.py:364
  97.8 11.6 %fusion.27.pre.pre_halo = f32[2048,768]{1,0:T(8,128)} fusion(bf16[2048,2048]{1,0:T(8,128)(2,1)} %all-gather.5.cloned.1.call-done, bf16[2048,342]{0,1:T(8,128)(2,1)} %param.22, bf16[2048,342]{0,1:T(8,128)(2,1)} %param.21), kind=kOutput, calls=%fused_computation.55 | convolution fusion | flops 6455033856 | bytes 17481728 | tf_op jit(solution)/shard_map/dot_general | solution.py:365
  109.8 17.8 %recurrence_forward.1 = (f32[2048,384]{1,0:T(8,128)S(1)}, f32[2048,384]{1,0:T(8,128)S(1)}, f32[2048,384]{1,0:T(8,128)S(1)}, f32[2048,384]{1,0:T(8,128)}, bf16[2048,384]{1,0:T(8,128)(2,1)S(1)}) custom-call(f32[2048,768]{1,0:T(8,128)} %fusion.27.pre.pre_halo, s32[2048,128]{1,0:T(8,128)S(1)} %broadcast_in_dim.18.pos, bf16[384,768]{1,0:T(8,128)(2,1)S(1)} %copy-done.3, ...), custom_call_target="tpu_custom_call" | custom-call | tf_op jit(solution)/shard_map/recurrence_forward/pallas_call | solution.py:150
  127.6 1.7 copy-done.5
  129.4 1.6 copy-done.7
  131.0 1.7 copy-done.8
  132.6 1.1 copy-done.10
  133.8 6.8 convolution_convert_fusion.2
  140.6 0.6 copy-done.22
  141.3 87.6 %reduce-scatter.8.cloned.1.call-done = bf16[256,2048]{1,0:T(8,128)(2,1)} async-done(((bf16[2048,2048]{1,0:T(8,128)(2,1)}), bf16[256,2048]{1,0:T(8,128)(2,1)}) %reduce-scatter.8.cloned.1.call-update) | async-done | bytes 1048592 | tf_op jit(solution)/shard_map/reduce_scatter | solution.py:367
  228.9 2.0 multiply_reduce_fusion
  230.9 2.9 multiply_convert_fusion.3
  235.0 79.4 %all-gather.7.cloned.1.call-done = bf16[2048,2048]{1,0:T(8,128)(2,1)} async-done(((bf16[256,2048]{1,0:T(8,128)(2,1)}), bf16[2048,2048]{1,0:T(8,128)(2,1)}) %all-gather.7.cloned.1.call-update) | async-done | bytes 8388624 | tf_op jit(solution)/shard_map/all_gather | solution.py:377
  314.4 11.8 %fusion.52 = f32[2048,768]{1,0:T(8,128)} fusion(bf16[2048,2048]{1,0:T(8,128)(2,1)} %all-gather.7.cloned.1.call-done, bf16[2048,768]{1,0:T(8,128)(2,1)} %param.33), kind=kOutput, calls=%fused_computation.112 | convolution fusion | flops 6442450944 | bytes 17825792 | tf_op jit(solution)/shard_map/dot_general | solution.py:379
  326.2 8.5 fusion.51
  334.7 61.8 %all-gather.9.cloned.1.call-done = bf16[2048,2048]{1,0:T(8,128)(2,1)} async-done(((bf16[256,2048]{1,0:T(8,128)(2,1)}), bf16[2048,2048]{1,0:T(8,128)(2,1)}) %all-gather.9.cloned.1.call-update) | async-done | bytes 8388624 | tf_op jit(solution)/shard_map/all_gather | solution.py:376
  396.4 17.0 %multiply_convert_fusion = (bf16[2048,768]{1,0:T(8,128)(2,1)S(1)}, bf16[2048,768]{1,0:T(8,128)(2,1)S(1)}, bf16[2048,768]{1,0:T(8,128)(2,1)}) fusion(f32[2048,768]{1,0:T(8,128)} %fusion.51, f32[2048,768]{1,0:T(8,128)} %fusion.52, bf16[2048,2048]{1,0:T(8,128)(2,1)} %all-gather.9.cloned.1.call-done, bf16[2048,768]{1,0:T(8,128)(2,1)S(1)} %copy-done), kind=kOutput, calls=%fused_computation.7 | convolution fusion | flops 6480199680 | bytes 33554432 | tf_op jit(solution)/shard_map/dot_general | solution.py:380
  413.5 9.6 fusion.53
  423.1 12.6 %add_convert_fusion = bf16[2048,2048]{1,0:T(8,128)(2,1)} fusion(f32[2048,2048]{1,0:T(8,128)} %fusion.53, bf16[2048,768]{1,0:T(8,128)(2,1)S(1)} %get-tuple-element.99, bf16[2048,768]{1,0:T(8,128)(2,1)S(1)} %copy-done.33), kind=kOutput, calls=%fused_computation | convolution fusion | flops 6450839552 | bytes 31457280 | tf_op jit(solution)/shard_map/dot_general | solution.py:39
  435.7 88.3 %reduce-scatter.12.cloned.1.call-done = bf16[256,2048]{1,0:T(8,128)(2,1)} async-done(((bf16[2048,2048]{1,0:T(8,128)(2,1)}), bf16[256,2048]{1,0:T(8,128)(2,1)}) %reduce-scatter.12.cloned.1.call-update) | async-done | bytes 1048592 | tf_op jit(solution)/shard_map/reduce_scatter | solution.py:386
  524.0 3.0 fusion.17
  527.0 3.3 fusion.47
  530.3 12.0 %convolution_convert_fusion.3 = bf16[768,2048]{1,0:T(8,128)(2,1)} fusion(bf16[2048,768]{1,0:T(8,128)(2,1)} %get-tuple-element.101, bf16[2048,2048]{1,0:T(8,128)(2,1)} %all-gather.9.cloned.1.call-done), kind=kOutput, calls=%fused_computation.15 | convolution fusion | flops 6444023808 | bytes 14680064 | tf_op jit(solution)/shard_map/dot_general | solution.py:45
  542.4 4.7 copy.64
  547.1 12.1 %convolution_convert_fusion.5 = bf16[768,2048]{1,0:T(8,128)(2,1)} fusion(bf16[2048,768]{1,0:T(8,128)(2,1)} %copy-done.38, bf16[2048,2048]{1,0:T(8,128)(2,1)} %all-gather.7.cloned.1.call-done), kind=kOutput, calls=%fused_computation.17 | convolution fusion | flops 6444023808 | bytes 14680064 | tf_op jit(solution)/shard_map/dot_general | solution.py:45
  559.2 4.8 copy.62
  563.9 12.1 %convolution_convert_fusion.4 = bf16[768,2048]{1,0:T(8,128)(2,1)} fusion(bf16[2048,768]{1,0:T(8,128)(2,1)} %copy-done.37, bf16[2048,2048]{1,0:T(8,128)(2,1)} %all-gather.7.cloned.1.call-done), kind=kOutput, calls=%fused_computation.16 | convolution fusion | flops 6444023808 | bytes 14680064 | tf_op jit(solution)/shard_map/dot_general | solution.py:45
  576.1 4.8 copy.63
  580.8 9.2 maximum_bitcast_fusion
  590.3 20.5 %all-gather.11.cloned.1.call-done = bf16[2048,2048]{1,0:T(8,128)(2,1)} async-done(((bf16[256,2048]{1,0:T(8,128)(2,1)}), bf16[2048,2048]{1,0:T(8,128)(2,1)}) %all-gather.11.cloned.1.call-update) | async-done | bytes 8388624 | tf_op jit(solution)/shard_map/all_gather | solution.py:407
  610.8 7.5 fusion.54
  618.3 1.2 slice.126
  619.5 4.5 fusion.23.gg
  624.1 25.1 %recurrence_backward.1 = (bf16[2048,768]{1,0:T(8,128)(2,1)S(1)}, f32[384,768]{1,0:T(8,128)S(1)}, f32[8,384]{1,0:T(8,128)S(1)}) custom-call(f32[2048,384]{1,0:T(8,128)S(1)} %fusion.23.gg, f32[2048,768]{1,0:T(8,128)} %fusion.27.pre.pre_halo, f32[2048,768]{1,0:T(8,128)} %fusion.27.pre.pre_halo, s32[2048,128]{1,0:T(8,128)S(1)} %copy-done.2, ...), custom_call_target="tpu_custom_call" | custom-call | tf_op jit(solution)/shard_map/recurrence_backward/pallas_call | solution.py:280
  649.5 1.0 pad_maximum_fusion.2
  650.5 0.7 pad_maximum_fusion.1
  651.2 7.1 convolution_convert_fusion.6
  658.3 1.7 fusion.48
  660.2 11.5 %convolution_convert_fusion = bf16[2048,2048]{1,0:T(8,128)(2,1)} fusion(bf16[2048,768]{1,0:T(8,128)(2,1)} %copy-done.9, bf16[2048,342]{0,1:T(8,128)(2,1)} %param.22, bf16[2048,342]{0,1:T(8,128)(2,1)} %param.21), kind=kOutput, calls=%fused_computation.2 | convolution fusion | flops 6459228160 | bytes 14336000 | tf_op jit(solution)/shard_map/dot_general | solution.py:39
  671.7 11.0 %convolution_convert_fusion.1 = bf16[2048,2048]{1,0:T(8,128)(2,1)} fusion(bf16[2048,768]{1,0:T(8,128)(2,1)} %get-tuple-element.101, bf16[2048,768]{1,0:T(8,128)(2,1)S(1)} %copy-done), kind=kOutput, calls=%fused_computation.3 | convolution fusion | flops 6446645248 | bytes 14680064 | tf_op jit(solution)/shard_map/dot_general | solution.py:39
  682.7 24.8 %reduce-scatter.16.cloned.1.call-done = bf16[1,3,768,512]{2,3,1,0:T(8,128)(2,1)} async-done(((bf16[4,3,768,512]{2,3,1,0:T(8,128)(2,1)}), bf16[1,3,768,512]{2,3,1,0:T(8,128)(2,1)}) %reduce-scatter.16.cloned.1.call-update) | async-done | bytes 2359312
  707.5 2.1 convert_element_type.176
  709.6 2.3 slice_bitcast_fusion
  711.9 9.3 psum.59
  721.2 0.6 slice.100
  721.8 0.6 slice_reduce_fusion
  722.4 0.7 reshape_squeeze.7
  723.1 0.7 reshape_squeeze.6
  724.4 100.5 %all-reduce.13.cloned.1.call-done = (bf16[2,171,171]{2,1,0:T(8,128)(2,1)}, bf16[2,171,171]{2,1,0:T(8,128)(2,1)}, bf16[2048,342]{0,1:T(8,128)(2,1)}, bf16[2048,342]{0,1:T(8,128)(2,1)}, bf16[342,2048]{1,0:T(8,128)(2,1)}) async-done(((bf16[2,171,171]{2,1,0:T(8,128)(2,1)}, bf16[2,171,171]{2,1,0:T(8,128)(2,1)}, bf16[2048,342]{0,1:T(8,128)(2,1)}, bf16[2048,342]{0,1:T(8,128)(2,1)}, bf16[342,2048]{1,0:T(8,128)(2,1)}), ...) | async-done | bytes 4436440 | tf_op jit(solution)/shard_map/psum | solution.py:418
  824.8 1.9 copy.60
  826.7 1.8 copy.61
  828.5 3.2 convert_element_type.170
  831.8 2.0 convert_element_type.171
  833.7 1.9 convert_element_type.175
  835.6 81.1 %reduce-scatter.14.cloned.1.call-done = bf16[256,2048]{1,0:T(8,128)(2,1)} async-done(((bf16[2048,2048]{1,0:T(8,128)(2,1)}), bf16[256,2048]{1,0:T(8,128)(2,1)}) %reduce-scatter.14.cloned.1.call-update) | async-done | bytes 1048592 | tf_op jit(solution)/shard_map/reduce_scatter | solution.py:411
  916.8 2.4 fusion.20
  919.1 39.7 %all-reduce.9 = (f32[2048]{0:T(1024)}, f32[2048]{0:T(1024)}) all-reduce(f32[2048]{0:T(1024)S(1)} %get-tuple-element.86, f32[2048]{0:T(1024)S(1)} %get-tuple-element.84), channel_id=1, replica_groups=mesh['dp'=4,'head'=8] {'dp','head'}, use_global_device_ids=true, to_apply=%region_11.12 | all-reduce | flops 4096 | bytes 32768 | tf_op jit(solution)/shard_map/psum | solution.py:435
  958.8 49.1 %reduce-scatter.10.cloned.1.call-done = bf16[256,2048]{1,0:T(8,128)(2,1)} async-done(((bf16[2048,2048]{1,0:T(8,128)(2,1)}), bf16[256,2048]{1,0:T(8,128)(2,1)}) %reduce-scatter.10.cloned.1.call-update) | async-done | bytes 1048592 | tf_op jit(solution)/shard_map/reduce_scatter | solution.py:389
  1007.9 5.8 fusion.13
  (127 shorter events, 4.5 us)
Async XLA Ops:
  7.2 389.2 %copy-start = (bf16[2048,768]{1,0:T(8,128)(2,1)S(1)}, bf16[2048,768]{1,0:T(8,128)(2,1)}, u32[]{:S(2)}) copy-start(bf16[2048,768]{1,0:T(8,128)(2,1)} %param.34) | copy-start | bytes 9437188
  7.2 5.7 copy-start.26
  7.2 5.7 copy-start.27
  7.2 5.8 copy-start.28
  7.2 5.9 copy-start.23
  7.2 5.9 copy-start.36
  7.3 6.1 copy-start.25
  7.3 6.3 copy-start.16
  7.3 6.7 copy-start.17
  7.3 90.5 %all-gather.5.cloned.1.call-start = ((), (), s32[]{:S(2)}) async-start(), calls=%async_computation.5 | async-start | bytes 9437184 | tf_op jit(solution)/shard_map/all_gather | solution.py:364
  9.0 0.7 copy-start.20
  9.8 0.6 copy-start.18
  12.9 216.0 %reduce-scatter.8.cloned.1.call-start = ((), (), s32[]{:S(2)}) async-start(), calls=%async_computation.6 | async-start | bytes 9437184 | tf_op jit(solution)/shard_map/reduce_scatter | solution.py:367
  97.8 12.0 %copy-start.3 = (bf16[384,768]{1,0:T(8,128)(2,1)S(1)}, bf16[384,768]{1,0:T(8,128)(2,1)}, u32[]{:S(2)}) copy-start(bf16[384,768]{1,0:T(8,128)(2,1)} %pad_maximum_fusion.wg) | copy-start | bytes 1769476
  109.8 17.8 %copy-start.1 = (s32[2048,128]{1,0:T(8,128)}, s32[2048,128]{1,0:T(8,128)S(1)}, u32[]{:S(2)}) copy-start(s32[2048,128]{1,0:T(8,128)S(1)} %broadcast_in_dim.18.pos) | copy-start | bytes 3145732
  109.8 24.0 %copy-start.34 = (bf16[342,2048]{1,0:T(8,128)(2,1)S(1)}, bf16[342,2048]{1,0:T(8,128)(2,1)}, u32[]{:S(2)}) copy-start(bf16[342,2048]{1,0:T(8,128)(2,1)} %param.30) | copy-start | bytes 4202500
  127.6 1.7 copy-start.5
  129.4 1.6 copy-start.7
  131.0 1.7 copy-start.8
  132.6 1.1 copy-start.10
  140.6 0.7 copy-start.22
  140.6 173.8 %all-gather.7.cloned.1.call-start = ((), (), s32[]{:S(2)}) async-start(), calls=%async_computation.7 | async-start | bytes 9437184 | tf_op jit(solution)/shard_map/all_gather | solution.py:377
  233.8 162.6 %all-gather.9.cloned.1.call-start = ((), (), s32[]{:S(2)}) async-start(), calls=%async_computation.9 | async-start | bytes 9437184 | tf_op jit(solution)/shard_map/all_gather | solution.py:376
  234.4 289.6 %reduce-scatter.12.cloned.1.call-start = ((), (), s32[]{:S(2)}) async-start(), calls=%async_computation.10 | async-start | bytes 9437184 | tf_op jit(solution)/shard_map/reduce_scatter | solution.py:386
  314.4 11.8 %copy-start.29 = (bf16[2048,2048]{1,0:T(8,128)(2,1)S(1)}, bf16[2048,2048]{1,0:T(8,128)(2,1)}, u32[]{:S(2)}) copy-start(bf16[2048,2048]{1,0:T(8,128)(2,1)} %all-gather.7.cloned.1.call-done) | copy-start | bytes 25165828
  314.4 11.8 %copy-start.31 = (bf16[2048,768]{1,0:T(8,128)(2,1)S(1)}, bf16[2048,768]{1,0:T(8,128)(2,1)}, u32[]{:S(2)}) copy-start(bf16[2048,768]{1,0:T(8,128)(2,1)} %param.32) | copy-start | bytes 9437188
  396.4 17.0 %copy-start.32 = (bf16[2048,768]{1,0:T(8,128)(2,1)S(1)}, bf16[2048,768]{1,0:T(8,128)(2,1)}, u32[]{:S(2)}) copy-start(bf16[2048,768]{1,0:T(8,128)(2,1)} %param.32) | copy-start | bytes 9437188
  413.4 9.6 copy-start.38
  413.4 9.6 copy-start.37
  413.5 9.6 copy-start.33
  435.7 175.2 %all-gather.11.cloned.1.call-start = ((), (), s32[]{:S(2)}) async-start(), calls=%async_computation.11 | async-start | bytes 9437184 | tf_op jit(solution)/shard_map/all_gather | solution.py:407
  524.0 3.0 copy-start.11
  524.0 3.0 copy-start.12
  524.0 3.0 copy-start.13
  530.3 177.2 %reduce-scatter.16.cloned.1.call-start = ((), (), s32[]{:S(2)}) async-start(), calls=%async_computation.13 | async-start | bytes 11796480
  590.1 234.7 %all-reduce.13.cloned.1.call-start = ((), (), s32[]{:S(2)}) async-start(), calls=%async_computation.14 | async-start | bytes 9175040 | tf_op jit(solution)/shard_map/psum | solution.py:418
  610.8 8.7 copy-start.30
  610.8 8.7 copy-start.35
  619.5 4.6 copy-start.2
  619.5 4.6 copy-start.4
  619.5 4.6 copy-start.6
  619.5 31.7 %slice-start = ((s8[8388608]{0:T(1024)(128)(4,1)}), s8[4194304]{0:T(1024)(128)(4,1)S(1)}, s32[]{:S(2)}) async-start(s8[8388608]{0:T(1024)(128)(4,1)} %bitcast.65), calls=%async_computation.15 | async-start | bytes 8388608
  624.1 27.1 %slice-start.1 = ((s8[8388608]{0:T(1024)(128)(4,1)}), s8[4194304]{0:T(1024)(128)(4,1)S(1)}, s32[]{:S(2)}) async-start(s8[8388608]{0:T(1024)(128)(4,1)} %bitcast.65), calls=%async_computation.16 | async-start | bytes 8388608
  649.3 9.1 copy-start.9
  660.1 256.6 %reduce-scatter.14.cloned.1.call-start = ((), (), s32[]{:S(2)}) async-start(), calls=%async_computation.12 | async-start | bytes 9437184 | tf_op jit(solution)/shard_map/reduce_scatter | solution.py:411
  671.7 336.2 %reduce-scatter.10.cloned.1.call-start = ((), (), s32[]{:S(2)}) async-start(), calls=%async_computation.8 | async-start | bytes 9437184 | tf_op jit(solution)/shard_map/reduce_scatter | solution.py:389
  709.6 14.2 %copy-start.24 = (bf16[342]{0:T(512)(128)(2,1)S(1)}, bf16[342]{0:T(512)(128)(2,1)}, u32[]{:S(2)}) copy-start(bf16[342]{0:T(512)(128)(2,1)} %param.29) | copy-start | bytes 2056
  824.8 6.9 copy-start.15
  831.7 2.0 copy-start.14
  833.7 83.0 %copy-start.19 = (f32[2048]{0:T(1024)S(1)}, f32[2048]{0:T(1024)}, u32[]{:S(2)}) copy-start(f32[2048]{0:T(1024)} %copy-done.18) | copy-start | bytes 24580
  833.7 83.0 %copy-start.21 = (f32[256]{0:T(256)S(1)}, f32[256]{0:T(256)}, u32[]{:S(2)}) copy-start(f32[256]{0:T(256)} %copy-done.20) | copy-start | bytes 3076
Sparse Core Ops, SparseCore 0:
  13.0 84.7 all-gather.4
  140.7 88.1 reduce-scatter.7
  233.9 80.3 all-gather.6
  315.8 80.5 all-gather.8
  435.8 88.1 reduce-scatter.11
  530.4 80.3 all-gather.10
  613.9 93.5 reduce-scatter.15
  712.9 111.8 all-reduce.12
  827.1 89.5 reduce-scatter.13
  918.9 88.9 reduce-scatter.9

commit v2 on v1

--- a/solution.py
+++ b/solution.py
@@ -14,6 +14,8 @@
 BLOCK = 64
 LANES = 128
 HALO = 8
+PARTS = 2
+VMEM_BYTES = 62 * 2**20
 
 EPSILON = 1e-06
 DECAY_SCALE = 8.0
@@ -301,6 +303,617 @@
         name="recurrence_backward",
     )(gg, pre, pre, pos, u, r, e, h, h, wg, par)
 
+def each(count, body):
+    def step(i, _):
+        body(i)
+        return 0
+
+    lax.fori_loop(0, count, step, 0)
+
+
+def line_place():
+    return lax.axis_index("head"), lax.axis_size("head")
+
+
+def line_barrier(j, n):
+    barrier = pltpu.get_barrier_semaphore()
+    for side in (-1, 1):
+
+        @pl.when((j + side >= 0) & (j + side < n))
+        def _():
+            pl.semaphore_signal(
+                barrier, inc=1, device_id={"head": j + side}, device_id_type=pl.DeviceIdType.MESH
+            )
+
+    inside = (j > 0) & (j < n - 1)
+
+    @pl.when(inside)
+    def _():
+        pl.semaphore_wait(barrier, 2)
+
+    @pl.when(jnp.logical_not(inside))
+    def _():
+        pl.semaphore_wait(barrier, 1)
+
+
+class Gather:
+    def __init__(self, j, n, buf, send, recv):
+        self.j, self.n, self.buf, self.send, self.recv = j, n, buf, send, recv
+        self.span = buf.shape[1] // PARTS
+
+    def copy(self, block, s, side, source=None):
+        part = pl.ds(s * self.span, self.span)
+        target = self.buf.at[block, part]
+        return pltpu.make_async_remote_copy(
+            src_ref=target if source is None else source.at[part],
+            dst_ref=target,
+            send_sem=self.send.at[(side + 1) // 2, block, s],
+            recv_sem=self.recv.at[block, s],
+            device_id={"head": self.j + side},
+            device_id_type=pl.DeviceIdType.MESH,
+        )
+
+    def there(self, side):
+        return (self.j + side >= 0) & (self.j + side < self.n)
+
+    def flows(self, t):
+        for side in (1, -1):
+            block = self.j - side * t
+            yield side, block, (block >= 0) & (block < self.n)
+
+    def start(self, source):
+        for s in range(PARTS):
+            for side in (1, -1):
+
+                @pl.when(self.there(side))
+                def _():
+                    self.copy(self.j, s, side, source).start()
+
+    def step(self, t):
+        for s in range(PARTS):
+            for side, block, live in self.flows(t):
+
+                @pl.when(live)
+                def _():
+                    self.copy(block, s, -side).wait_recv()
+
+                @pl.when(live & self.there(side))
+                def _():
+                    self.copy(block, s, side).start()
+
+    def finish(self):
+        def drain(t):
+            for s in range(PARTS):
+                for side, block, live in self.flows(t):
+
+                    @pl.when(live & self.there(side))
+                    def _():
+                        self.copy(block, s, side).wait_send()
+
+        each(self.n, drain)
+
+
+class Scatter:
+    def __init__(self, j, n, own, held, send, recv):
+        self.j, self.n, self.own, self.held, self.send, self.recv = j, n, own, held, send, recv
+        self.span = own.shape[1] // PARTS
+
+    def rows(self, s):
+        return pl.ds(s * self.span, self.span)
+
+    def slot(self, block, side, at):
+        return block if side == 1 else jnp.where(block == at, self.n, block)
+
+    def arrival(self, slot, s):
+        return pltpu.make_async_copy(
+            self.held.at[slot, self.rows(s)], self.held.at[slot, self.rows(s)], self.recv.at[slot, s]
+        )
+
+    def flows(self, t):
+        for side in (1, -1):
+            lag = self.j if side == 1 else self.n - 1 - self.j
+            block = self.n - 1 - (t - lag) if side == 1 else t - lag
+            yield side, block, (t >= lag) & (t <= self.n - 2)
+
+    def copy(self, source, block, s, side):
+        slot = self.slot(block, side, self.j + side)
+        return pltpu.make_async_remote_copy(
+            src_ref=source.at[block, self.rows(s)],
+            dst_ref=self.held.at[slot, self.rows(s)],
+            send_sem=self.send.at[block, s],
+            recv_sem=self.recv.at[slot, s],
+            device_id={"head": self.j + side},
+            device_id_type=pl.DeviceIdType.MESH,
+        )
+
+    def step(self, t):
+        for s in range(PARTS):
+            for side, block, live in self.flows(t):
+                behind = (self.j - side >= 0) & (self.j - side < self.n)
+
+                @pl.when(live & jnp.logical_not(behind))
+                def _():
+                    self.copy(self.own, block, s, side).start()
+
+                @pl.when(live & behind)
+                def _():
+                    self.arrival(block, s).wait()
+                    self.add(block, s)
+                    self.copy(self.held, block, s, side).start()
+
+    def add(self, block, s):
+        def add_rows(i):
+            rows = pl.ds(pl.multiple_of(s * self.span + i * 16, 16), 16)
+            total = self.own[block, rows, :].astype(jnp.float32) + self.held[
+                block, rows, :
+            ].astype(jnp.float32)
+            self.held[block, rows, :] = total.astype(jnp.bfloat16)
+
+        each(self.span // 16, add_rows)
+
+    def arrive(self):
+        for s in range(PARTS):
+
+            @pl.when(self.j > 0)
+            def _():
+                self.arrival(self.j, s).wait()
+
+            @pl.when(self.j < self.n - 1)
+            def _():
+                self.arrival(self.n, s).wait()
+
+    def result(self, rows):
+        total = self.own[self.j, rows, :].astype(jnp.float32)
+        left = self.held[self.j, rows, :].astype(jnp.float32)
+        right = self.held[self.n, rows, :].astype(jnp.float32)
+        total = total + jnp.where(self.j > 0, left, 0.0)
+        return total + jnp.where(self.j < self.n - 1, right, 0.0)
+
+    def finish(self):
+        def drain(t):
+            for s in range(PARTS):
+                for side, block, live in self.flows(t):
+
+                    @pl.when(live)
+                    def _():
+                        self.copy(self.own, block, s, side).wait_send()
+
+        each(self.n - 1, drain)
+
+
+def gather_sems(n):
+    return [pltpu.SemaphoreType.DMA((2, n, PARTS)), pltpu.SemaphoreType.DMA((n, PARTS))]
+
+
+def scatter_sems(n):
+    return [pltpu.SemaphoreType.DMA((n, PARTS)), pltpu.SemaphoreType.DMA((n + 1, PARTS))]
+
+
+def line_call(kernel, ident, name, out_shape, in_specs, out_specs, scratch, cost=None):
+    return pl.pallas_call(
+        kernel,
+        out_shape=out_shape,
+        in_specs=in_specs,
+        out_specs=out_specs,
+        scratch_shapes=scratch,
+        compiler_params=pltpu.CompilerParams(
+            collective_id=ident, has_side_effects=True, vmem_limit_bytes=VMEM_BYTES
+        ),
+        name=name,
+    )
+
+
+IN_VMEM = pl.BlockSpec(memory_space=pltpu.VMEM)
+IN_ANY = pl.BlockSpec(memory_space=pl.ANY)
+STRIP = 16
+
+
+def strips(rows, body):
+    each(rows // STRIP, lambda i: body(pl.ds(pl.multiple_of(i * STRIP, STRIP), STRIP)))
+
+
+def project_kernel(
+    stream, gain, wbi, rows_out, pre, normed, rows, send, recv, keep_sem
+):
+    j, n = line_place()
+    line_barrier(j, n)
+    local = stream.shape[0]
+
+    def norm(part):
+        _, unit = rms_parts(stream[part, :].astype(jnp.float32))
+        normed[part, :] = (unit * gain[...]).astype(jnp.bfloat16)
+
+    strips(local, norm)
+    gather = Gather(j, n, rows, send, recv)
+    gather.start(normed)
+
+    def project(block, source):
+        part = pl.ds(pl.multiple_of(block * local, local), local)
+        pre[part, :] = jnp.dot(source, wbi[...], preferred_element_type=jnp.float32)
+
+    def keep(source, block):
+        return pltpu.make_async_copy(source, rows_out.at[block], keep_sem.at[block])
+
+    keep(normed, j).start()
+    project(j, normed[...])
+
+    def visit(v):
+        t = v // 2 + 1
+        block = jnp.where(v % 2 == 0, j - t, j + t)
+
+        @pl.when(v % 2 == 0)
+        def _():
+            gather.step(t)
+
+        @pl.when((block >= 0) & (block < n))
+        def _():
+            keep(rows.at[block], block).start()
+            project(block, rows[block])
+
+    each(2 * (n - 1), visit)
+    gather.finish()
+    keep(normed, j).wait()
+    for k in range(1, n):
+        other = lax.rem(j + k, n)
+        keep(rows.at[other], other).wait()
+
+
+def project(stream, gain, wbi):
+    n = lax.axis_size("head")
+    local, depth = stream.shape
+    return line_call(
+        project_kernel, 0, "gather_project",
+        (
+            jax.ShapeDtypeStruct((n, local, depth), jnp.bfloat16),
+            jax.ShapeDtypeStruct((n * local, wbi.shape[1]), jnp.float32),
+        ),
+        [IN_VMEM] * 3,
+        [IN_ANY, IN_VMEM],
+        [
+            pltpu.VMEM((local, depth), jnp.bfloat16),
+            pltpu.VMEM((n, local, depth), jnp.bfloat16),
+            *gather_sems(n),
+            pltpu.SemaphoreType.DMA((n,)),
+        ],
+    )(stream, gain, wbi)
+
+
+def mixer_out_kernel(
+    gated, wo, stream, gain, cot, cot_rows, hidden, low_out, own, held,
+    send, recv, gsend, grecv, sem,
+):
+    j, n = line_place()
+    line_barrier(j, n)
+    local = stream.shape[0]
+    gather = Gather(j, n, cot_rows, gsend, grecv)
+    scatter = Scatter(j, n, own, held, send, recv)
+
+    def compute(block):
+        part = pl.ds(pl.multiple_of(block * local, local), local)
+        own[block] = jnp.dot(
+            gated[part, :], wo[...], preferred_element_type=jnp.float32
+        ).astype(jnp.bfloat16)
+
+    def ahead(t):
+        for _, block, live in scatter.flows(t):
+            pl.when(live)(lambda: compute(block))
+
+    ahead(0)
+    mine = pltpu.make_async_copy(cot, cot_rows.at[j], sem)
+    mine.start()
+
+    def step(t):
+        scatter.step(t)
+
+        @pl.when(t == 0)
+        def _():
+            gather.start(cot)
+
+        ahead(t + 1)
+
+        @pl.when(t == 0)
+        def _():
+            compute(j)
+
+        @pl.when(t > 0)
+        def _():
+            gather.step(t)
+
+    each(n - 1, step)
+    scatter.arrive()
+
+    def settle(part):
+        total = stream[part, :].astype(jnp.float32) + scatter.result(part)
+        hidden[part, :] = total
+        _, unit = rms_parts(total)
+        low_out[part, :] = (unit * gain[...]).astype(jnp.bfloat16)
+
+    strips(local, settle)
+    gather.step(n - 1)
+    scatter.finish()
+    gather.finish()
+    mine.wait()
+
+
+def mixer_out(gated, wo, stream, gain, cot):
+    n = lax.axis_size("head")
+    local, depth = stream.shape
+    return line_call(
+        mixer_out_kernel, 1, "mixer_out",
+        (
+            jax.ShapeDtypeStruct((n, local, depth), jnp.bfloat16),
+            jax.ShapeDtypeStruct((local, depth), jnp.float32),
+            jax.ShapeDtypeStruct((local, depth), jnp.bfloat16),
+        ),
+        [IN_VMEM] * 4 + [IN_ANY],
+        [IN_ANY, IN_VMEM, IN_VMEM],
+        [
+            pltpu.VMEM((n, local, depth), jnp.bfloat16),
+            pltpu.VMEM((n + 1, local, depth), jnp.bfloat16),
+            *scatter_sems(n),
+            *gather_sems(n),
+            pltpu.SemaphoreType.DMA,
+        ],
+    )(gated, wo, stream, gain, cot)
+
+
+def ffn_kernel(
+    low, cot_rows, cot, hidden, gain, wg, wu, wd,
+    out_part, terms, resid, resid_low, gain_grad,
+    rows, cot_unit, kept, own, held, stage, wstage, cot_cols,
+    gsend, grecv, send, recv, cot_sem, out_sem, col_sem, term_sem,
+):
+    j, n = line_place()
+    line_barrier(j, n)
+    f32, bf16 = jnp.float32, jnp.bfloat16
+    local, depth = low.shape
+    units = wg.shape[1]
+    fstep = 256 if units % 256 == 0 else LANES
+    dstep = 512
+    gather = Gather(j, n, rows, gsend, grecv)
+    scatter = Scatter(j, n, own, held, send, recv)
+    gather.start(low)
+    rows[j] = low[...]
+
+    def fetch(block):
+        return pltpu.make_async_copy(cot_rows.at[block], cot_unit, cot_sem)
+
+    def put(block):
+        return pltpu.make_async_copy(stage, out_part.at[block], out_sem)
+
+    def unit(block):
+        span = pl.ds(pl.multiple_of(block * local, local), local)
+        x = rows.at[block]
+        for f in range(0, units, fstep):
+            cols = slice(f, f + fstep)
+            gate = jnp.dot(x[...], wg[:, cols], preferred_element_type=f32)
+            act, slope = gelu_pair(gate)
+            up = jnp.dot(x[...], wu[:, cols], preferred_element_type=f32)
+            kept[2, span, cols] = (act * up).astype(bf16)
+            grad = jnp.dot(cot_unit[...], wd[:, cols], preferred_element_type=f32)
+            kept[0, span, cols] = (grad * up * slope).astype(bf16)
+            kept[1, span, cols] = (grad * act).astype(bf16)
+        for d in range(0, depth, dstep):
+            cols = slice(d, d + dstep)
+            own[block, :, cols] = (
+                contract_cols(kept[0, span, :], wg[cols, :])
+                + contract_cols(kept[1, span, :], wu[cols, :])
+            ).astype(bf16)
+            stage[:, cols] = contract_cols(kept[2, span, :], wd[cols, :]).astype(bf16)
+
+    def visit(v):
+        t = (v + 1) // 2
+        block = jnp.where(v % 2 == 1, j - t, j + t)
+        live = (block >= 0) & (block < n)
+
+        @pl.when(live)
+        def _():
+            fetch(block).start()
+
+        @pl.when(v % 2 == 1)
+        def _():
+            gather.step(t)
+
+        @pl.when(live)
+        def _():
+            fetch(block).wait()
+
+            @pl.when(v > 0)
+            def _():
+                put(block).wait()
+
+            unit(block)
+            put(block).start()
+
+    each(2 * n - 1, visit)
+    put(j).wait()
+
+    width = depth // n
+    per = depth // terms.shape[0] // width
+
+    def take(b):
+        cols = pl.ds(pl.multiple_of(b * width, width), width)
+        return pltpu.make_async_copy(cot_rows.at[:, :, cols], cot_cols, col_sem)
+
+    def give(b):
+        spot = pl.ds(pl.multiple_of(lax.rem(b, per) * width, width), width)
+        return pltpu.make_async_copy(wstage, terms.at[b // per, :, spot, :], term_sem)
+
+    def weights(b):
+        cols = pl.ds(pl.multiple_of(b * width, width), width)
+        xs = rows[:, :, cols].reshape(n * local, width)
+        take(b).wait()
+
+        @pl.when(b > 0)
+        def _():
+            give(b).wait()
+
+        wstage[0] = contract_rows(xs, kept[0]).astype(bf16)
+        wstage[1] = contract_rows(xs, kept[1]).astype(bf16)
+        wstage[2] = contract_rows(
+            cot_cols[...].reshape(n * local, width), kept[2]
+        ).astype(bf16)
+        give(b).start()
+
+        @pl.when(b + 1 < n)
+        def _():
+            take(b + 1).start()
+
+    take(0).start()
+
+    def step(t):
+        pl.when(t < n - 1)(lambda: scatter.step(t))
+        weights(t)
+
+    each(n, step)
+    scatter.arrive()
+    gain_grad[...] = jnp.zeros_like(gain_grad)
+
+    def settle(part):
+        rinv, u = rms_parts(hidden[part, :])
+        grad = scatter.result(part)
+        gain_grad[...] += jnp.sum(grad * u, axis=0, keepdims=True)
+        total = cot[part, :].astype(f32) + norm_back(u, rinv, gain[...], grad)
+        resid[part, :] = total
+        resid_low[part, :] = total.astype(bf16)
+
+    strips(local, settle)
+    give(0).wait()
+    gather.finish()
+    scatter.finish()
+
+
+def feed_forward(low, cot_rows, cot, hidden, gain, wg, wu, wd):
+    n, group = lax.axis_size("head"), lax.axis_size("dp")
+    local, depth = low.shape
+    units = wg.shape[1]
+    bf16 = jnp.bfloat16
+    return line_call(
+        ffn_kernel, 2, "feed_forward",
+        (
+            jax.ShapeDtypeStruct((n, local, depth), bf16),
+            jax.ShapeDtypeStruct((group, 3, depth // group, units), bf16),
+            jax.ShapeDtypeStruct((local, depth), jnp.float32),
+            jax.ShapeDtypeStruct((local, depth), bf16),
+            jax.ShapeDtypeStruct((1, depth), jnp.float32),
+        ),
+        [IN_VMEM, IN_ANY] + [IN_VMEM] * 6,
+        [IN_ANY, IN_ANY, IN_VMEM, IN_VMEM, IN_VMEM],
+        [
+            pltpu.VMEM((n, local, depth), bf16),
+            pltpu.VMEM((local, depth), bf16),
+            pltpu.VMEM((3, n * local, units), bf16),
+            pltpu.VMEM((n, local, depth), bf16),
+            pltpu.VMEM((n + 1, local, depth), bf16),
+            pltpu.VMEM((local, depth), bf16),
+            pltpu.VMEM((3, depth // n, units), bf16),
+            pltpu.VMEM((n, local, depth // n), bf16),
+            *gather_sems(n),
+            *scatter_sems(n),
+            *[pltpu.SemaphoreType.DMA] * 4,
+        ],
+    )(low, cot_rows, cot, hidden, gain, wg, wu, wd)
+
+
+def resid_kernel(
+    low, out_part, hidden, grad_rows, layer_out, held, send, recv, gsend, grecv, sem
+):
+    j, n = line_place()
+    line_barrier(j, n)
+    gather = Gather(j, n, grad_rows, gsend, grecv)
+    scatter = Scatter(j, n, out_part, held, send, recv)
+    gather.start(low)
+    mine = pltpu.make_async_copy(low, grad_rows.at[j], sem)
+    mine.start()
+
+    def step(t):
+        pl.when(t > 0)(lambda: gather.step(t))
+        pl.when(t < n - 1)(lambda: scatter.step(t))
+
+    each(n, step)
+    scatter.arrive()
+
+    def settle(part):
+        layer_out[part, :] = (hidden[part, :] + scatter.result(part)).astype(jnp.bfloat16)
+
+    strips(low.shape[0], settle)
+    gather.finish()
+    scatter.finish()
+    mine.wait()
+
+
+def gather_resid(low, out_part, hidden):
+    n = lax.axis_size("head")
+    local, depth = low.shape
+    bf16 = jnp.bfloat16
+    return line_call(
+        resid_kernel, 3, "gather_resid",
+        (jax.ShapeDtypeStruct((n, local, depth), bf16), jax.ShapeDtypeStruct((local, depth), bf16)),
+        [IN_VMEM] * 3,
+        [IN_ANY, IN_VMEM],
+        [
+            pltpu.VMEM((n + 1, local, depth), bf16),
+            *scatter_sems(n),
+            *gather_sems(n),
+            pltpu.SemaphoreType.DMA,
+        ],
+    )(low, out_part, hidden)
+
+
+def stream_kernel(dpre, wbi, stream, gain, resid, stream_grad, gain_grad, own, held, send, recv):
+    j, n = line_place()
+    line_barrier(j, n)
+    local = stream.shape[0]
+    scatter = Scatter(j, n, own, held, send, recv)
+
+    def compute(block):
+        part = pl.ds(pl.multiple_of(block * local, local), local)
+        own[block] = contract_cols(dpre[part, :], wbi[...]).astype(jnp.bfloat16)
+
+    def ahead(t):
+        for _, block, live in scatter.flows(t):
+            pl.when(live)(lambda: compute(block))
+
+    ahead(0)
+
+    def step(t):
+        scatter.step(t)
+        ahead(t + 1)
+        pl.when(t == 0)(lambda: compute(j))
+
+    each(n - 1, step)
+    scatter.arrive()
+    gain_grad[...] = jnp.zeros_like(gain_grad)
+
+    def settle(part):
+        rinv, u = rms_parts(stream[part, :].astype(jnp.float32))
+        grad = scatter.result(part)
+        gain_grad[...] += jnp.sum(grad * u, axis=0, keepdims=True)
+        total = resid[part, :] + norm_back(u, rinv, gain[...], grad)
+        stream_grad[part, :] = total.astype(jnp.bfloat16)
+
+    strips(local, settle)
+    scatter.finish()
+
+
+def stream_back(dpre, wbi, stream, gain, resid):
+    n = lax.axis_size("head")
+    local, depth = stream.shape
+    return line_call(
+        stream_kernel, 4, "stream_back",
+        (
+            jax.ShapeDtypeStruct((local, depth), jnp.bfloat16),
+            jax.ShapeDtypeStruct((1, depth), jnp.float32),
+        ),
+        [IN_VMEM] * 5,
+        [IN_VMEM, IN_VMEM],
+        [
+            pltpu.VMEM((n, local, depth), jnp.bfloat16),
+            pltpu.VMEM((n + 1, local, depth), jnp.bfloat16),
+            *scatter_sems(n),
+        ],
+    )(dpre, wbi, stream, gain, resid)
+
 
 def places(lengths):
     starts = jnp.cumsum(lengths, axis=1) - lengths
@@ -336,7 +949,6 @@
     heads, size = rate_bias.shape
     chans = branch_weight.shape[1]
     width = -(-chans // LANES) * LANES
-    group = lax.axis_size("dp")
 
     pos = jnp.broadcast_to(places(doc_lengths)[:, None], (SEQ, LANES))
     slope = -DECAY_SCALE * jax.nn.softplus(decay_param.astype(f32))
@@ -357,63 +969,24 @@
     wbi = jnp.concatenate([widen(branch_weight, width), widen(input_weight, width)], axis=1)
     wo = jnp.pad(output_weight, ((0, width - chans), (0, 0)))
 
-    inflow = stream.astype(f32)
-    premix = premix_gain.astype(f32)
-    rinv1, unit1 = rms_parts(inflow)
-    normed = (unit1 * premix).astype(bf16)
-    normed_rows = lax.all_gather(normed, "head", axis=0, tiled=True)
-    pre = jnp.dot(normed_rows, wbi, preferred_element_type=f32)
+    premix = premix_gain.astype(f32)[None]
+    preffn = preffn_gain.astype(f32)[None]
+    normed_rows, pre = project(stream, premix, wbi)
     u, r, e, h, gated = rec_fwd(pre, pos, wg, par)
-    mixer_out = lax.psum_scatter(
-        jnp.dot(gated, wo, preferred_element_type=f32).astype(bf16),
-        "head", scatter_dimension=0, tiled=True,
-    )
-    hidden_in = inflow + mixer_out.astype(f32)
-
-    preffn = preffn_gain.astype(f32)
-    rinv2, unit2 = rms_parts(hidden_in)
-    ffn_low = (unit2 * preffn).astype(bf16)
-    cot_rows = lax.all_gather(cotangent, "head", axis=0, tiled=True)
-    ffn_rows = lax.all_gather(ffn_low, "head", axis=0, tiled=True)
-    gate_pre = jnp.dot(ffn_rows, ffn_gate, preferred_element_type=f32)
-    upward_pre = jnp.dot(ffn_rows, ffn_upward, preferred_element_type=f32)
-    hidden_grad = jnp.dot(cot_rows, ffn_down, preferred_element_type=f32)
-    act, act_slope = gelu_pair(gate_pre)
-    hidden_low = (act * upward_pre).astype(bf16)
-    gate_low = (hidden_grad * upward_pre * act_slope).astype(bf16)
-    upward_low = (hidden_grad * act).astype(bf16)
-    back = contract_cols(gate_low, ffn_gate) + contract_cols(upward_low, ffn_upward)
-    ffn_grad = lax.psum_scatter(
-        back.astype(bf16), "head", scatter_dimension=0, tiled=True
-    ).astype(f32)
-    ffn_out = lax.psum_scatter(
-        contract_cols(hidden_low, ffn_down).astype(bf16), "head", scatter_dimension=0, tiled=True
-    )
-    layer_out = (hidden_in + ffn_out.astype(f32)).astype(bf16)
-    terms = jnp.stack(
-        [
-            contract_rows(gate_low, ffn_rows),
-            contract_rows(upward_low, ffn_rows),
-            contract_rows(hidden_low, cot_rows),
-        ]
-    ).astype(bf16)
-    terms = jnp.moveaxis(terms.reshape(3, terms.shape[1], group, -1), 2, 0)
+    cot_rows, hidden_in, ffn_low = mixer_out(gated, wo, stream, preffn, cotangent)
+
+    out_part, terms, resid_grad, resid_low, preffn_grad = feed_forward(
+        ffn_low, cot_rows, cotangent, hidden_in, preffn, ffn_gate, ffn_upward, ffn_down
+    )
     ffn_sums = lax.psum_scatter(terms, "dp", scatter_dimension=0, tiled=False).astype(f32)
 
-    preffn_grad = jnp.sum(ffn_grad * unit2, axis=0)
-    resid_grad = cotangent.astype(f32) + norm_back(unit2, rinv2, preffn, ffn_grad)
-    resid_low = resid_grad.astype(bf16)
-
-    grad_rows = lax.all_gather(resid_low, "head", axis=0, tiled=True)
+    grad_rows, layer_out = gather_resid(resid_low, out_part, hidden_in)
+    grad_rows = grad_rows.reshape(SEQ, -1)
     gated_grad = contract_cols(grad_rows, wo)
     output_grad = contract_rows(gated, grad_rows)[:chans]
     dpre, dgate, dpar = rec_bwd(gated_grad, pre, pos, u, r, e, h, wg, par)
-    normed_grad = lax.psum_scatter(
-        contract_cols(dpre, wbi).astype(bf16), "head", scatter_dimension=0, tiled=True
-    ).astype(f32)
-    dwbi = contract_rows(normed_rows, dpre)
-    premix_grad = jnp.sum(normed_grad * unit1, axis=0)
-    stream_grad = (resid_grad + norm_back(unit1, rinv1, premix, normed_grad)).astype(bf16)
+    dwbi = contract_rows(normed_rows.reshape(SEQ, -1), dpre)
+    stream_grad, premix_grad = stream_back(dpre, wbi, stream, premix, resid_grad)
 
     sums = lax.psum(
         tuple(
@@ -432,7 +1005,7 @@
     branch_grad, input_grad, output_grad, rate_grad, entry_grad, dpar = (
         v.astype(f32) for v in sums
     )
-    premix_grad, preffn_grad = lax.psum((premix_grad, preffn_grad), ("dp", "head"))
+    premix_grad, preffn_grad = lax.psum((premix_grad[0], preffn_grad[0]), ("dp", "head"))
     decay_grad = dpar[G_DECAY] * (-DECAY_SCALE * jax.nn.sigmoid(decay_param.astype(f32)))
     return (
         layer_out,
@@ -449,9 +1022,9 @@
         decay_grad,
         output_grad,
         preffn_grad,
-        ffn_sums[0].T,
-        ffn_sums[1].T,
-        ffn_sums[2].T,
+        ffn_sums[0],
+        ffn_sums[1],
+        ffn_sums[2],
     )
 
 

time: 1030 us -> 794 us (0.77)
  waiting for transfers between devices: 676 us -> 66.8 us
  Pallas kernels: 42.9 us -> 577 us
  matrix products: 156 us -> 19.4 us
  other arithmetic: 46.4 us -> 18.4 us
  blocking collectives: 49 us -> 64.6 us
    pallas_call x0 -> x5, Pallas kernels: none -> 535 us  [the longest x1 167 us: feed_forward(): line_call(ffn_kernel, 2, 'feed_forward', (jax.ShapeDtypeStruct((n, local,...]
    reduce_scatter x4 -> x0, waiting for transfers between devices: 306 us -> none  [the longest x1 88.3 us: shards(): lax.psum_scatter(back.astype(bf16), 'head', scatter_dimension=0, tiled=True)]
    all_gather x4 -> x0, waiting for transfers between devices: 244 us -> none  [the longest x1 82.5 us: shards(): normed_rows = lax.all_gather(normed, 'head', axis=0, tiled=True)]
    psum x1, waiting for transfers between devices: 100 us -> 0.01 us  [shards(): lax.psum(tuple((v.astype(bf16) for v in (dwbi[:, :chans], dwbi[:, width:w...]
    dot_general x5 -> x0, matrix products: 55.7 us -> none  [the longest x1 17 us: shards(): hidden_grad = jnp.dot(cot_rows, ffn_down, preferred_element_type=f32)]
    dot_general x5 -> x1, matrix products: 49.2 us -> 4.55 us  [contract_cols(): lax.dot_general(leading, trailing, (((1,), (1,)), ((), ())), preferred_el...]
    unnamed x11 -> x3, waiting for transfers between devices: 25.5 us -> 66.8 us
    dot_general x5 -> x2, matrix products: 50.9 us -> 14.9 us  [contract_rows(): lax.dot_general(leading, trailing, (((0,), (0,)), ((), ())), preferred_el...]
  transfers between devices with their start and end apart: 10 -> 2, of which waited for: 10 -> 1; matrix products, arithmetic and copies ran while one was open for 15% -> 2% of each run, Pallas kernels for 2% -> 10%
where the time goes in v2:
time: 794 us; the launch traced here: 793 us
  Pallas kernels  577 us (73%)
  waiting for transfers between devices  66.8 us (8%)
  blocking collectives  64.6 us (8%)
  local copies, waits for them, and re-layouts  32 us (4%)
  matrix products  19.4 us (2%)
  other arithmetic  18.4 us (2%)
  between operations  14.4 us (2%)
    pallas_call x1, Pallas kernels, feed_forward(): line_call(ffn_kernel, 2, 'feed_forward', (jax.ShapeDtypeStruct((n, local,...  167 us
    pallas_call x1, Pallas kernels, gather_resid(): line_call(resid_kernel, 3, 'gather_resid', (jax.ShapeDtypeStruct((n, loca...  106 us
    pallas_call x1, Pallas kernels, mixer_out(): line_call(mixer_out_kernel, 1, 'mixer_out', (jax.ShapeDtypeStruct((n, loc...  103 us
    pallas_call x1, Pallas kernels, project(): line_call(project_kernel, 0, 'gather_project', (jax.ShapeDtypeStruct((n,...  81.5 us
    pallas_call x1, Pallas kernels, stream_back(): line_call(stream_kernel, 4, 'stream_back', (jax.ShapeDtypeStruct((local,...  76.8 us
    unnamed x3, waiting for transfers between devices  66.8 us
    psum x1, blocking collectives, shards(): lax.psum((premix_grad[0], preffn_grad[0]), ('dp', 'head'))  54.5 us
    pallas_call x1, Pallas kernels, rec_bwd(): pl.pallas_call(rec_bwd_kernel, grid=(count,), out_shape=(jax.ShapeDtypeSt...  24.9 us
  transfers between devices with their start and end apart: 2, of which 1 were waited for; matrix products, arithmetic and copies ran while one was open for 2% of the time, Pallas kernels for 10%

profile of v2, /device:TPU:0, one launch (start us, length us, event | category | flops | bytes accessed | tf_op | source)
XLA Modules:
  0.0 792.6 jit_solution(14616209661378465992)
XLA Ops:
  7.2 0.0 all-reduce.13.cloned.1.call-start
  7.3 0.9 reduce_window_sum.11
  8.2 0.7 subtract_bitcast_fusion
  8.9 0.7 reshape.170
  9.5 0.8 reshape.171
  10.3 0.8 reshape.172
  11.1 0.7 fusion.12
  11.8 0.1 select_reduce_fusion
  11.9 1.3 broadcast_in_dim.47
  13.2 1.3 broadcast_in_dim.48
  14.5 1.3 fusion.16
  15.8 1.3 fusion.17
  17.1 2.6 copy.51
  19.6 1.6 copy.52
  21.2 0.1 pad_add_fusion.1
  21.4 0.1 pad_add_fusion
  21.5 0.1 pad_maximum_fusion.wg
  21.5 1.1 copy-done.6
  22.6 0.5 copy-done.7
  23.1 1.9 fusion.2.wbi
  25.0 1.3 pad.36.wo
  26.3 0.1 pad_select_fusion.par
  26.4 81.5 %gather_project.1 = (bf16[8,256,2048]{2,1,0:T(8,128)(2,1)}, f32[2048,768]{1,0:T(8,128)}) custom-call(bf16[256,2048]{1,0:T(8,128)(2,1)} %stream.5, f32[1,2048]{1,0:T(1,128)} %bitcast.38, bf16[2048,768]{1,0:T(8,128)(2,1)} %fusion.2.wbi), custom_call_target="tpu_custom_call" | custom-call | tf_op jit(solution)/shard_map/gather_project/pallas_call | solution.py:564
  108.0 0.3 broadcast_in_dim.42.pos
  108.3 17.4 %recurrence_forward.1 = (f32[2048,384]{1,0:T(8,128)S(1)}, f32[2048,384]{1,0:T(8,128)S(1)}, f32[2048,384]{1,0:T(8,128)S(1)}, f32[2048,384]{1,0:T(8,128)}, bf16[2048,384]{1,0:T(8,128)(2,1)S(1)}) custom-call(f32[2048,768]{1,0:T(8,128)} %get-tuple-element.39.pre.pre_halo, s32[2048,128]{1,0:T(8,128)S(1)} %broadcast_in_dim.42.pos, ...), custom_call_target="tpu_custom_call" | custom-call | tf_op jit(solution)/shard_map/recurrence_forward/pallas_call | solution.py:152
  125.7 1.6 copy-done
  127.3 1.6 copy-done.2
  129.0 1.6 copy-done.3
  130.6 1.1 copy-done.5
  131.7 103.3 %mixer_out.1 = (bf16[8,256,2048]{2,1,0:T(8,128)(2,1)}, f32[256,2048]{1,0:T(8,128)}, bf16[256,2048]{1,0:T(8,128)(2,1)}) custom-call(bf16[2048,384]{1,0:T(8,128)(2,1)} %copy-done.5, bf16[384,2048]{1,0:T(8,128)(2,1)} %pad.36.wo, bf16[256,2048]{1,0:T(8,128)(2,1)} %stream.5, f32[1,2048]{1,0:T(1,128)} %bitcast.36, bf16[256,2048]{1,0:T(8,128)(2,1)} %cot.3), custom_call_target="tpu_custom_call" | custom-call | tf_op jit(solution)/shard_map/mixer_out/pallas_call | solution.py:641
  235.1 167.4 %feed_forward.1 = (bf16[8,256,2048]{2,1,0:T(8,128)(2,1)}, bf16[4,3,512,768]{3,2,1,0:T(8,128)(2,1)}, f32[256,2048]{1,0:T(8,128)}, bf16[256,2048]{1,0:T(8,128)(2,1)}, f32[1,2048]{1,0:T(1,128)}) custom-call(bf16[256,2048]{1,0:T(8,128)(2,1)} %get-tuple-element.41.low, bf16[8,256,2048]{2,1,0:T(8,128)(2,1)} %get-tuple-element.42.cot_rows, bf16[256,2048]{1,0:T(8,128)(2,1)} %cot.3, ...), custom_call_target="tpu_custom_call" | custom-call | tf_op jit(solution)/shard_map/feed_forward/pallas_call | solution.py:791
  402.5 105.5 %gather_resid.1 = (bf16[8,256,2048]{2,1,0:T(8,128)(2,1)}, bf16[256,2048]{1,0:T(8,128)(2,1)}) custom-call(bf16[256,2048]{1,0:T(8,128)(2,1)} %get-tuple-element.44.low, bf16[8,256,2048]{2,1,0:T(8,128)(2,1)} %get-tuple-element.45.out_part, f32[256,2048]{1,0:T(8,128)} %get-tuple-element.43.hidden), custom_call_target="tpu_custom_call" | custom-call | tf_op jit(solution)/shard_map/gather_resid/pallas_call | solution.py:849
  508.0 0.0 copy-start.9
  508.0 7.5 fusion.19
  515.5 4.5 fusion.13.gg
  520.1 1.2 slice.126
  521.4 24.9 %recurrence_backward.1 = (bf16[2048,768]{1,0:T(8,128)(2,1)S(1)}, f32[384,768]{1,0:T(8,128)S(1)}, f32[8,384]{1,0:T(8,128)S(1)}) custom-call(f32[2048,384]{1,0:T(8,128)S(1)} %fusion.13.gg, f32[2048,768]{1,0:T(8,128)} %get-tuple-element.39.pre.pre_halo, f32[2048,768]{1,0:T(8,128)} %get-tuple-element.39.pre.pre_halo, s32[2048,128]{1,0:T(8,128)S(1)} %broadcast_in_dim.42.pos, ...), custom_call_target="tpu_custom_call" | custom-call | tf_op jit(solution)/shard_map/recurrence_backward/pallas_call | solution.py:282
  546.3 7.4 convolution_convert_fusion
  553.7 1.9 fusion.15
  555.6 0.1 convert.31
  555.7 0.1 slice_bitcast_fusion.4
  555.9 0.7 pad_maximum_fusion.2
  556.6 0.7 pad_maximum_fusion.1
  557.3 0.0 all-reduce.13.cloned.1.call-update
  557.3 0.0 reduce-scatter.4.cloned.1.call-start
  557.3 0.7 reduce-scatter.4.cloned.1.call-update
  558.0 10.0 %psum.59 = bf16[8,342]{1,0:T(8,128)(2,1)S(1)} all-reduce(bf16[8,342]{1,0:T(8,128)(2,1)S(1)} %slice.127), channel_id=1, replica_groups=mesh['dp'=4,'head'=8] {'dp'}, use_global_device_ids=true, to_apply=%region_5.6 | all-reduce | flops 2736 | bytes 10944 | tf_op jit(solution)/shard_map/psum | solution.py:991
  568.1 0.6 slice.100
  568.7 76.8 %stream_back.1 = (bf16[256,2048]{1,0:T(8,128)(2,1)}, f32[1,2048]{1,0:T(1,128)}) custom-call(bf16[2048,768]{1,0:T(8,128)(2,1)} %copy-done.4, bf16[2048,768]{1,0:T(8,128)(2,1)} %fusion.2.wbi, bf16[256,2048]{1,0:T(8,128)(2,1)} %stream.5, f32[1,2048]{1,0:T(1,128)} %bitcast.39, f32[256,2048]{1,0:T(8,128)} %get-tuple-element.53.resid), custom_call_target="tpu_custom_call" | custom-call | tf_op jit(solution)/shard_map/stream_back/pallas_call | solution.py:902
  645.5 0.6 slice_reduce_fusion
  646.1 0.7 reshape_squeeze.7
  646.7 0.7 reshape_squeeze.6
  647.4 54.5 %all-reduce.9 = (f32[2048]{0:T(1024)}, f32[2048]{0:T(1024)}) all-reduce(f32[2048]{0:T(1024)} %bitcast.41, f32[2048]{0:T(1024)S(1)} %bitcast.40), channel_id=1, replica_groups=mesh['dp'=4,'head'=8] {'dp','head'}, use_global_device_ids=true, to_apply=%region_2.3 | all-reduce | flops 4096 | bytes 32768 | tf_op jit(solution)/shard_map/psum | solution.py:1008
  701.9 0.6 fusion.7
  702.5 1.9 copy.57
  704.4 1.8 copy.58
  706.2 3.3 convert_element_type.90
  709.5 1.9 convert_element_type.91
  711.4 1.9 convert_element_type.95
  713.3 66.1 %reduce-scatter.4.cloned.1.call-done = bf16[1,3,512,768]{3,2,1,0:T(8,128)(2,1)} async-done(((bf16[4,3,512,768]{3,2,1,0:T(8,128)(2,1)}), bf16[1,3,512,768]{3,2,1,0:T(8,128)(2,1)}) %reduce-scatter.4.cloned.1.call-update) | async-done | bytes 2359312
  779.4 2.1 convert_element_type.96
  781.5 2.3 slice_bitcast_fusion
  783.8 1.0 copy.74
  784.8 1.0 copy.75
  (46 shorter events, 0.2 us)
Async XLA Ops:
  7.2 12.5 %copy-start.10 = (bf16[2048,342]{0,1:T(8,128)(2,1)S(1)}, bf16[2048,342]{0,1:T(8,128)(2,1)}, u32[]{:S(2)}) copy-start(bf16[2048,342]{0,1:T(8,128)(2,1)} %param.22) | copy-start | bytes 4202500
  7.2 695.3 %all-reduce.13.cloned.1.call-start = ((), (), s32[]{:S(2)}) async-start(), calls=%async_computation.2 | async-start | bytes 9175040 | tf_op jit(solution)/shard_map/psum | solution.py:991
  21.2 1.4 copy-start.6
  21.2 1.9 copy-start.7
  23.1 1.9 copy-start.8
  23.1 3.2 copy-start.17
  125.7 1.6 copy-start
  127.3 1.6 copy-start.2
  129.0 1.6 copy-start.3
  130.6 1.1 copy-start.5
  508.0 7.5 copy-start.9
  508.0 7.5 copy-start.18
  515.5 5.8 copy-start.1
  520.1 26.2 %slice-start = ((s8[8388608]{0:T(1024)(128)(4,1)}), s8[4194304]{0:T(1024)(128)(4,1)S(1)}, s32[]{:S(2)}) async-start(s8[8388608]{0:T(1024)(128)(4,1)} %bitcast.42), calls=%async_computation.3 | async-start | bytes 8388608
  521.4 24.9 %slice-start.1 = ((s8[8388608]{0:T(1024)(128)(4,1)}), s8[4194304]{0:T(1024)(128)(4,1)S(1)}, s32[]{:S(2)}) async-start(s8[8388608]{0:T(1024)(128)(4,1)} %bitcast.42), calls=%async_computation.4 | async-start | bytes 8388608
  546.3 7.5 copy-start.4
  557.3 222.1 %reduce-scatter.4.cloned.1.call-start = ((), (), s32[]{:S(2)}) async-start(), calls=%async_computation.1 | async-start | bytes 11796480
  568.7 78.7 %copy-start.15 = (f32[1,2048]{1,0:T(1,128)S(1)}, f32[1,2048]{1,0:T(1,128)}, u32[]{:S(2)}) copy-start(f32[1,2048]{1,0:T(1,128)} %get-tuple-element.59) | copy-start | bytes 24580
  568.7 133.2 %copy-start.16 = (bf16[342]{0:T(512)(128)(2,1)S(1)}, bf16[342]{0:T(512)(128)(2,1)}, u32[]{:S(2)}) copy-start(bf16[342]{0:T(512)(128)(2,1)} %param.29) | copy-start | bytes 2056
  702.5 7.0 copy-start.12
  709.5 1.9 copy-start.11
  781.5 2.3 copy-start.13
  781.5 3.3 copy-start.14
Sparse Core Ops, SparseCore 0:
  557.4 123.2 all-reduce.12
  683.8 95.6 reduce-scatter.3

commit v3 on v2

--- a/solution.py
+++ b/solution.py
@@ -15,7 +15,11 @@
 LANES = 128
 HALO = 8
 PARTS = 2
+LAG = 1
 VMEM_BYTES = 62 * 2**20
+IN_VMEM = pl.BlockSpec(memory_space=pltpu.VMEM)
+IN_SMEM = pl.BlockSpec(memory_space=pltpu.SMEM)
+IN_ANY = pl.BlockSpec(memory_space=pl.ANY)
 
 EPSILON = 1e-06
 DECAY_SCALE = 8.0
@@ -24,6 +28,7 @@
 
 BIAS, TAP, RATE_B, ENTRY_B, DECAY = 0, 1, 5, 6, 7
 PARAMS = 8
+SAVED = 4
 G_BIAS, G_TAP, G_RATE, G_ENTRY, G_DECAY = 0, 1, 5, 6, 7
 
 
@@ -78,8 +83,21 @@
     )
 
 
-def rec_fwd_kernel(pre, pos, wg, par, u_out, r_out, e_out, h_out, gated, xbuf, z, carry):
-    width = u_out.shape[1]
+def doc_places(lengths, first, rows):
+    spots = first + lax.broadcasted_iota(jnp.int32, (rows, LANES), 0)
+    begin = jnp.zeros((rows, LANES), jnp.int32)
+    start = jnp.int32(0)
+    for k in range(lengths.shape[1] - 1):
+        start = start + lengths[0, k]
+        begin = jnp.where(spots >= start, start, begin)
+    return spots - begin
+
+
+def rec_fwd_kernel(lengths, pre, wg, par, saved, gated, xbuf, z, carry):
+    width = gated.shape[1]
+    u_out, r_out, e_out, h_out = (
+        saved.at[:, i * width : (i + 1) * width] for i in range(SAVED)
+    )
     tiles = width // LANES
 
     @pl.when(pl.program_id(0) == 0)
@@ -93,9 +111,11 @@
 
     xbuf[HALO : HALO + CHUNK, :] = pre[:, width:]
 
+    first = pl.program_id(0) * CHUNK
+
     def conv_step(i, _):
         row = pl.multiple_of(i * BLOCK, BLOCK)
-        place = pos[pl.ds(row, BLOCK), :]
+        place = doc_places(lengths, first + row, BLOCK)
         for t in range(tiles):
             cols = pl.ds(t * LANES, LANES)
             xs = xbuf[pl.ds(row, BLOCK + HALO), cols]
@@ -112,7 +132,7 @@
     def scan_step(i, _):
         row = pl.multiple_of(i * BLOCK, BLOCK)
         rows = pl.ds(row, BLOCK)
-        fresh = pos[rows, :] == 0
+        fresh = doc_places(lengths, first + row, BLOCK) == 0
         inner = lax.broadcasted_iota(jnp.int32, (BLOCK, LANES), 0) % 8
         for t in range(tiles):
             cols = pl.ds(t * LANES, LANES)
@@ -144,17 +164,19 @@
     lax.fori_loop(0, CHUNK // BLOCK, scan_step, 0)
 
 
-def rec_fwd(pre, pos, wg, par):
+def rec_fwd(lengths, pre, wg, par):
     length, width = pre.shape[0], pre.shape[1] // 2
     rows = lambda cols: pl.BlockSpec((CHUNK, cols), lambda i: (i, 0))
     whole = lambda a: pl.BlockSpec(a.shape, lambda i: (0,) * a.ndim)
-    wide = jax.ShapeDtypeStruct((length, width), jnp.float32)
     return pl.pallas_call(
         rec_fwd_kernel,
         grid=(length // CHUNK,),
-        out_shape=(wide, wide, wide, wide, jax.ShapeDtypeStruct((length, width), jnp.bfloat16)),
-        in_specs=[rows(2 * width), rows(LANES), whole(wg), whole(par)],
-        out_specs=[rows(width)] * 5,
+        out_shape=(
+            jax.ShapeDtypeStruct((length, SAVED * width), jnp.float32),
+            jax.ShapeDtypeStruct((length, width), jnp.bfloat16),
+        ),
+        in_specs=[IN_SMEM, rows(2 * width), whole(wg), whole(par)],
+        out_specs=[rows(SAVED * width), rows(width)],
         scratch_shapes=[
             pltpu.VMEM((CHUNK + HALO, width), jnp.float32),
             pltpu.VMEM((CHUNK, 2 * width), jnp.float32),
@@ -162,146 +184,8 @@
         ],
         compiler_params=pltpu.CompilerParams(vmem_limit_bytes=40 * 2**20),
         name="recurrence_forward",
-    )(pre, pos, wg, par)
-
-
-def rec_bwd_kernel(
-    gg, pre, pre_halo, pos, u_in, r_in, e_in, h_in, h_halo, wg, par,
-    dpre, dgate, dpar, dz, du, pbuf, carry,
-):
-    width = u_in.shape[1]
-    tiles = width // LANES
-    step = pl.program_id(0)
-
-    @pl.when(step == 0)
-    def _():
-        du[CHUNK:, :] = jnp.zeros((HALO, width), jnp.float32)
-        pbuf[CHUNK:, :] = jnp.zeros((HALO, LANES), jnp.int32)
-        carry[...] = jnp.zeros_like(carry)
-        dgate[...] = jnp.zeros_like(dgate)
-        dpar[...] = jnp.zeros_like(dpar)
-
-    @pl.when(step > 0)
-    def _():
-        du[CHUNK:, :] = du[0:HALO, :]
-        pbuf[CHUNK:, :] = pbuf[0:HALO, :]
-
-    pbuf[0:CHUNK, :] = pos[...]
-
-    def total(v):
-        return jnp.sum(v, axis=0, keepdims=True)
-
-    def scan_step(j, _):
-        i = CHUNK // BLOCK - 1 - j
-        row = pl.multiple_of(i * BLOCK, BLOCK)
-        rows = pl.ds(row, BLOCK)
-        fresh = pos[rows, :] == 0
-        place = lax.broadcasted_iota(jnp.int32, (BLOCK, LANES), 0)
-        inner = place % 8
-        before = pl.multiple_of(jnp.maximum(row - 8, 0), 8)
-        for t in range(tiles):
-            cols = pl.ds(t * LANES, LANES)
-            other = pl.ds(width + t * LANES, LANES)
-            r, e, u, h = r_in[rows, cols], e_in[rows, cols], u_in[rows, cols], h_in[rows, cols]
-            grad = gg[rows, cols]
-            act, slope = gelu_pair(pre[rows, cols])
-            dpre[rows, cols] = (grad * h * slope).astype(jnp.bfloat16)
-            dh = grad * act
-            decay = par[DECAY : DECAY + 1, cols]
-            c, m, ratio = decay_terms(r, decay, fresh)
-            b, a = c * dh, c
-            for d in (1, 2, 4):
-                near = inner < 8 - d
-                b = b + a * jnp.where(near, pltpu.roll(b, BLOCK - d, 0), 0.0)
-                a = a * jnp.where(near, pltpu.roll(a, BLOCK - d, 0), 1.0)
-            later = carry[0:1, cols]
-            pieces = []
-            first = later
-            for g in reversed(range(BLOCK // 8)):
-                part = slice(g * 8, g * 8 + 8)
-                state = b[part] + a[part] * first
-                first = state[0:1]
-                pieces.append(state)
-            carry[0:1, cols] = first
-            mu = jnp.concatenate(pieces[::-1], axis=0)
-            adj = dh + jnp.where(place == BLOCK - 1, later, pltpu.roll(mu, BLOCK - 1, 0))
-            edge = jnp.where(i == 0, h_halo[7:8, cols], h_in[pl.ds(before, 8), cols][7:8])
-            prior = jnp.where(place == 0, edge, pltpu.roll(h, 1, 0))
-            eu = e * u
-            dlog = adj * (prior * c - eu * ratio)
-            dpar[G_DECAY : G_DECAY + 1, cols] += total(dlog * r)
-            dzr = decay * dlog * (r * (1.0 - r))
-            dze = adj * m * eu * (1.0 - e)
-            dpar[G_RATE : G_RATE + 1, cols] += total(dzr)
-            dpar[G_ENTRY : G_ENTRY + 1, cols] += total(dze)
-            dz[rows, cols] = dzr.astype(jnp.bfloat16)
-            dz[rows, other] = dze.astype(jnp.bfloat16)
-            du[rows, cols] = adj * m * e
-        return 0
-
-    lax.fori_loop(0, CHUNK // BLOCK, scan_step, 0)
-    du[0:CHUNK, :] += contract_cols(dz[...], wg[...])
-    dgate[...] += contract_rows(u_in[...].astype(jnp.bfloat16), dz[...])
-
-    def conv_step(i, _):
-        row = pl.multiple_of(i * BLOCK, BLOCK)
-        rows = pl.ds(row, BLOCK)
-        before = pl.multiple_of(jnp.maximum(row - 8, 0), 8)
-        place = pbuf[pl.ds(row, BLOCK + HALO), :]
-        for t in range(tiles):
-            cols = pl.ds(t * LANES, LANES)
-            other = pl.ds(width + t * LANES, LANES)
-            ds = du[pl.ds(row, BLOCK + HALO), cols]
-            near = ds[0:BLOCK]
-            x = pre[rows, other]
-            head = jnp.where(i == 0, pre_halo[:, other], pre[pl.ds(before, 8), other])
-            xs = jnp.concatenate([head, x], axis=0)
-            dx = par[TAP : TAP + 1, cols] * near
-            dpar[G_BIAS : G_BIAS + 1, cols] += total(near)
-            dpar[G_TAP : G_TAP + 1, cols] += total(near * x)
-            for k in range(1, CONVW):
-                inside = jnp.where(place >= k, ds, 0.0)
-                dx = dx + par[TAP + k : TAP + k + 1, cols] * inside[k : k + BLOCK]
-                dpar[G_TAP + k : G_TAP + k + 1, cols] += total(
-                    inside[0:BLOCK] * xs[HALO - k : HALO - k + BLOCK]
-                )
-            dpre[rows, other] = dx.astype(jnp.bfloat16)
-        return 0
-
-    lax.fori_loop(0, CHUNK // BLOCK, conv_step, 0)
-
-
-def rec_bwd(gg, pre, pos, u, r, e, h, wg, par):
-    length, width = u.shape
-    count = length // CHUNK
-    rows = lambda cols: pl.BlockSpec((CHUNK, cols), lambda i: (count - 1 - i, 0))
-    halo = lambda cols: pl.BlockSpec(
-        (HALO, cols), lambda i: (jnp.maximum((count - 1 - i) * (CHUNK // HALO) - 1, 0), 0)
-    )
-    whole = lambda shape: pl.BlockSpec(shape, lambda i: (0,) * len(shape))
-    return pl.pallas_call(
-        rec_bwd_kernel,
-        grid=(count,),
-        out_shape=(
-            jax.ShapeDtypeStruct((length, 2 * width), jnp.bfloat16),
-            jax.ShapeDtypeStruct((width, 2 * width), jnp.float32),
-            jax.ShapeDtypeStruct((PARAMS, width), jnp.float32),
-        ),
-        in_specs=[
-            rows(width), rows(2 * width), halo(2 * width), rows(LANES),
-            rows(width), rows(width), rows(width), rows(width), halo(width),
-            whole(wg.shape), whole(par.shape),
-        ],
-        out_specs=[rows(2 * width), whole((width, 2 * width)), whole((PARAMS, width))],
-        scratch_shapes=[
-            pltpu.VMEM((CHUNK, 2 * width), jnp.bfloat16),
-            pltpu.VMEM((CHUNK + HALO, width), jnp.float32),
-            pltpu.VMEM((CHUNK + HALO, LANES), jnp.int32),
-            pltpu.VMEM((8, width), jnp.float32),
-        ],
-        compiler_params=pltpu.CompilerParams(vmem_limit_bytes=40 * 2**20),
-        name="recurrence_backward",
-    )(gg, pre, pre, pos, u, r, e, h, h, wg, par)
+    )(lengths, pre, wg, par)
+
 
 def each(count, body):
     def step(i, _):
@@ -315,6 +199,49 @@
     return lax.axis_index("head"), lax.axis_size("head")
 
 
+def peers(axis):
+    n = lax.axis_size(axis)
+    return [lax.rem(lax.axis_index(axis) + k, n) for k in range(1, n)]
+
+
+def far_peer(axis):
+    return lax.axis_size(axis) - 1 - lax.axis_index(axis)
+
+
+def near_peers(axis):
+    n, me = lax.axis_size(axis), lax.axis_index(axis)
+    far = far_peer(axis)
+    for k in range(n - 2):
+        peer = k + jnp.where(k >= jnp.minimum(me, far), 1, 0)
+        peer = peer + jnp.where(k + 1 >= jnp.maximum(me, far), 1, 0)
+        ahead = jnp.where(peer < me, 1, 0) + jnp.where(n - 1 - peer < me, 1, 0)
+        yield k, peer, me - ahead
+
+
+def peer_barrier(axes):
+    barrier = pltpu.get_barrier_semaphore()
+    count = 0
+    for axis in axes:
+        for peer in peers(axis):
+            pl.semaphore_signal(
+                barrier, inc=1, device_id={axis: peer}, device_id_type=pl.DeviceIdType.MESH
+            )
+            count += 1
+    pl.semaphore_wait(barrier, count)
+
+
+def wait_neighbours(sem, j, n):
+    inside = (j > 0) & (j < n - 1)
+
+    @pl.when(inside)
+    def _():
+        pl.semaphore_wait(sem, 2)
+
+    @pl.when(jnp.logical_not(inside))
+    def _():
+        pl.semaphore_wait(sem, 1)
+
+
 def line_barrier(j, n):
     barrier = pltpu.get_barrier_semaphore()
     for side in (-1, 1):
@@ -325,15 +252,7 @@
                 barrier, inc=1, device_id={"head": j + side}, device_id_type=pl.DeviceIdType.MESH
             )
 
-    inside = (j > 0) & (j < n - 1)
-
-    @pl.when(inside)
-    def _():
-        pl.semaphore_wait(barrier, 2)
-
-    @pl.when(jnp.logical_not(inside))
-    def _():
-        pl.semaphore_wait(barrier, 1)
+    wait_neighbours(barrier, j, n)
 
 
 class Gather:
@@ -397,6 +316,13 @@
     def __init__(self, j, n, own, held, send, recv):
         self.j, self.n, self.own, self.held, self.send, self.recv = j, n, own, held, send, recv
         self.span = own.shape[1] // PARTS
+        self.compact = own.shape[0] != n
+
+    def place(self, block, side):
+        return block if not self.compact else (1 - side) // 2
+
+    def last(self):
+        return self.j if not self.compact else 2
 
     def rows(self, s):
         return pl.ds(s * self.span, self.span)
@@ -433,23 +359,29 @@
 
                 @pl.when(live & jnp.logical_not(behind))
                 def _():
-                    self.copy(self.own, block, s, side).start()
+                    if self.compact:
+                        self.held[block, self.rows(s), :] = self.own[
+                            self.place(block, side), self.rows(s), :
+                        ]
+                        self.copy(self.held, block, s, side).start()
+                    else:
+                        self.copy(self.own, block, s, side).start()
 
                 @pl.when(live & behind)
                 def _():
                     self.arrival(block, s).wait()
-                    self.add(block, s)
+                    self.add(block, s, side)
                     self.copy(self.held, block, s, side).start()
 
-    def add(self, block, s):
+    def add(self, block, s, side):
         def add_rows(i):
-            rows = pl.ds(pl.multiple_of(s * self.span + i * 16, 16), 16)
-            total = self.own[block, rows, :].astype(jnp.float32) + self.held[
+            rows = pl.ds(pl.multiple_of(s * self.span + i * STRIP, STRIP), STRIP)
+            total = self.own[self.place(block, side), rows, :].astype(jnp.float32) + self.held[
                 block, rows, :
             ].astype(jnp.float32)
             self.held[block, rows, :] = total.astype(jnp.bfloat16)
 
-        each(self.span // 16, add_rows)
+        each(self.span // STRIP, add_rows)
 
     def arrive(self):
         for s in range(PARTS):
@@ -463,7 +395,7 @@
                 self.arrival(self.n, s).wait()
 
     def result(self, rows):
-        total = self.own[self.j, rows, :].astype(jnp.float32)
+        total = self.own[self.last(), rows, :].astype(jnp.float32)
         left = self.held[self.j, rows, :].astype(jnp.float32)
         right = self.held[self.n, rows, :].astype(jnp.float32)
         total = total + jnp.where(self.j > 0, left, 0.0)
@@ -476,9 +408,84 @@
 
                     @pl.when(live)
                     def _():
-                        self.copy(self.own, block, s, side).wait_send()
+                        self.copy(self.held, block, s, side).wait_send()
 
         each(self.n - 1, drain)
+
+
+class Share:
+    def __init__(self, axis, slots, send, recv):
+        self.axis, self.slots, self.send, self.recv = axis, slots, send, recv
+        self.me = lax.axis_index(axis)
+
+    def copy(self, slot, peer, source=None):
+        return pltpu.make_async_remote_copy(
+            src_ref=self.slots.at[slot] if source is None else source,
+            dst_ref=self.slots.at[slot],
+            send_sem=self.send.at[peer],
+            recv_sem=self.recv.at[slot],
+            device_id={self.axis: peer},
+            device_id_type=pl.DeviceIdType.MESH,
+        )
+
+    def start(self, sources=None):
+        for peer in peers(self.axis):
+            source = None if sources is None else sources.at[peer]
+            self.copy(self.me, peer, source).start()
+
+    def arrive(self):
+        for peer in peers(self.axis):
+            self.copy(peer, peer).wait_recv()
+
+    def finish(self):
+        for peer in peers(self.axis):
+            self.copy(self.me, peer).wait_send()
+
+
+def share_sems(axis):
+    n = lax.axis_size(axis)
+    return [pltpu.SemaphoreType.DMA((n,)), pltpu.SemaphoreType.DMA((n,))]
+
+
+class Sum:
+    def __init__(self, terms, slots, total, sems):
+        self.terms, self.slots, self.total = terms, slots, total
+        self.parts = Share("dp", slots, sems[0], sems[1])
+        self.whole = Share("dp", total, sems[2], sems[3])
+        self.me, self.sem = self.parts.me, sems[4]
+
+    def start(self):
+        self.parts.start(self.terms)
+
+    def keep(self):
+        return pltpu.make_async_copy(self.slots.at[self.me], self.total.at[self.me], self.sem)
+
+    def spread(self):
+        self.parts.arrive()
+        rows = self.slots.shape[1]
+
+        def add(part):
+            value = jnp.zeros((STRIP, self.slots.shape[2]), jnp.float32)
+            for i in range(self.slots.shape[0]):
+                mine = self.terms[i, part, :].astype(jnp.float32)
+                other = self.slots[i, part, :].astype(jnp.float32)
+                value = value + jnp.where(self.me == i, mine, other)
+            self.slots[self.me, part, :] = value.astype(jnp.bfloat16)
+
+        strips(rows, add)
+        for peer in peers("dp"):
+            self.whole.copy(self.me, peer, self.slots.at[self.me]).start()
+        self.keep().start()
+
+    def finish(self):
+        self.whole.arrive()
+        self.keep().wait()
+        self.parts.finish()
+        self.whole.finish()
+
+
+def sum_sems():
+    return [*share_sems("dp"), *share_sems("dp"), pltpu.SemaphoreType.DMA]
 
 
 def gather_sems(n):
@@ -503,8 +510,6 @@
     )
 
 
-IN_VMEM = pl.BlockSpec(memory_space=pltpu.VMEM)
-IN_ANY = pl.BlockSpec(memory_space=pl.ANY)
 STRIP = 16
 
 
@@ -529,7 +534,7 @@
 
     def project(block, source):
         part = pl.ds(pl.multiple_of(block * local, local), local)
-        pre[part, :] = jnp.dot(source, wbi[...], preferred_element_type=jnp.float32)
+        pre[part, :] = contract_cols(source, wbi[...])
 
     def keep(source, block):
         return pltpu.make_async_copy(source, rows_out.at[block], keep_sem.at[block])
@@ -565,7 +570,7 @@
         project_kernel, 0, "gather_project",
         (
             jax.ShapeDtypeStruct((n, local, depth), jnp.bfloat16),
-            jax.ShapeDtypeStruct((n * local, wbi.shape[1]), jnp.float32),
+            jax.ShapeDtypeStruct((n * local, wbi.shape[0]), jnp.float32),
         ),
         [IN_VMEM] * 3,
         [IN_ANY, IN_VMEM],
@@ -645,7 +650,7 @@
             jax.ShapeDtypeStruct((local, depth), jnp.float32),
             jax.ShapeDtypeStruct((local, depth), jnp.bfloat16),
         ),
-        [IN_VMEM] * 4 + [IN_ANY],
+        [IN_VMEM] * 5,
         [IN_ANY, IN_VMEM, IN_VMEM],
         [
             pltpu.VMEM((n, local, depth), jnp.bfloat16),
@@ -659,12 +664,12 @@
 
 def ffn_kernel(
     low, cot_rows, cot, hidden, gain, wg, wu, wd,
-    out_part, terms, resid, resid_low, gain_grad,
+    out_part, terms, far_terms, resid, resid_low, gain_grad,
     rows, cot_unit, kept, own, held, stage, wstage, cot_cols,
-    gsend, grecv, send, recv, cot_sem, out_sem, col_sem, term_sem,
+    gsend, grecv, send, recv, cot_sem, out_sem, col_sem, term_sem, fsend, frecv,
 ):
     j, n = line_place()
-    line_barrier(j, n)
+    peer_barrier(("head", "dp"))
     f32, bf16 = jnp.float32, jnp.bfloat16
     local, depth = low.shape
     units = wg.shape[1]
@@ -731,22 +736,41 @@
     width = depth // n
     per = depth // terms.shape[0] // width
 
+    far = far_peer("dp")
+
+    def columns(b):
+        return pl.ds(pl.multiple_of(lax.rem(b + far * per, n) * width, width), width)
+
     def take(b):
-        cols = pl.ds(pl.multiple_of(b * width, width), width)
-        return pltpu.make_async_copy(cot_rows.at[:, :, cols], cot_cols, col_sem)
+        return pltpu.make_async_copy(cot_rows.at[:, :, columns(b)], cot_cols, col_sem)
 
     def give(b):
+        owner = lax.rem(b // per + far, n // per)
         spot = pl.ds(pl.multiple_of(lax.rem(b, per) * width, width), width)
-        return pltpu.make_async_copy(wstage, terms.at[b // per, :, spot, :], term_sem)
+        return pltpu.make_async_copy(wstage, terms.at[owner, :, spot, :], term_sem)
+
+    def send_far():
+        return pltpu.make_async_remote_copy(
+            src_ref=terms.at[far],
+            dst_ref=far_terms,
+            send_sem=fsend,
+            recv_sem=frecv,
+            device_id={"dp": far},
+            device_id_type=pl.DeviceIdType.MESH,
+        )
 
     def weights(b):
-        cols = pl.ds(pl.multiple_of(b * width, width), width)
+        cols = columns(b)
         xs = rows[:, :, cols].reshape(n * local, width)
         take(b).wait()
 
         @pl.when(b > 0)
         def _():
             give(b).wait()
+
+        @pl.when(b == per)
+        def _():
+            send_far().start()
 
         wstage[0] = contract_rows(xs, kept[0]).astype(bf16)
         wstage[1] = contract_rows(xs, kept[1]).astype(bf16)
@@ -781,6 +805,7 @@
     give(0).wait()
     gather.finish()
     scatter.finish()
+    send_far().wait()
 
 
 def feed_forward(low, cot_rows, cot, hidden, gain, wg, wu, wd):
@@ -793,12 +818,13 @@
         (
             jax.ShapeDtypeStruct((n, local, depth), bf16),
             jax.ShapeDtypeStruct((group, 3, depth // group, units), bf16),
+            jax.ShapeDtypeStruct((3, depth // group, units), bf16),
             jax.ShapeDtypeStruct((local, depth), jnp.float32),
             jax.ShapeDtypeStruct((local, depth), bf16),
             jax.ShapeDtypeStruct((1, depth), jnp.float32),
         ),
         [IN_VMEM, IN_ANY] + [IN_VMEM] * 6,
-        [IN_ANY, IN_ANY, IN_VMEM, IN_VMEM, IN_VMEM],
+        [IN_ANY, IN_ANY, IN_ANY, IN_VMEM, IN_VMEM, IN_VMEM],
         [
             pltpu.VMEM((n, local, depth), bf16),
             pltpu.VMEM((local, depth), bf16),
@@ -810,120 +836,445 @@
             pltpu.VMEM((n, local, depth // n), bf16),
             *gather_sems(n),
             *scatter_sems(n),
-            *[pltpu.SemaphoreType.DMA] * 4,
+            *[pltpu.SemaphoreType.DMA] * 6,
         ],
     )(low, cot_rows, cot, hidden, gain, wg, wu, wd)
 
 
-def resid_kernel(
-    low, out_part, hidden, grad_rows, layer_out, held, send, recv, gsend, grecv, sem
+def back_kernel(
+    lengths, low, out_part, hidden, terms, gated, wo, wbi, wg, par, pre, saved,
+    normed_rows, stream, gain, resid, preffn_grad,
+    layer_out, sums, stream_grad, ob_total, i_total, g_total, par_grad, gains,
+    rows, own, held, dh, dpre, acc, dgate, dz, du, carry, dpar, wide,
+    unit_bp, unit_h, unit_gated, unit_normed,
+    obterms, obslots, iterms, islots, gterms, gslots, pslots, dslots, hslots,
+    gsend, grecv, send4, recv4, send8, recv8, tsend, trecv, unit_sem, own_sem, chunk_sem,
+    row_sem, wide_sem, free, psend, precv, dsend, drecv, hsend, hrecv, *sems,
 ):
     j, n = line_place()
-    line_barrier(j, n)
-    gather = Gather(j, n, grad_rows, gsend, grecv)
-    scatter = Scatter(j, n, out_part, held, send, recv)
+    f32, bf16 = jnp.float32, jnp.bfloat16
+    local, depth = stream.shape
+    width = dh.shape[1]
+    tiles = width // LANES
+    peer_barrier(("head", "dp"))
+
+    def near():
+        for k, peer, slot in near_peers("dp"):
+            yield pltpu.make_async_remote_copy(
+                src_ref=terms.at[peer],
+                dst_ref=sums.at[slot],
+                send_sem=tsend.at[k],
+                recv_sem=trecv.at[slot],
+                device_id={"dp": peer},
+                device_id_type=pl.DeviceIdType.MESH,
+            )
+
+    gather = Gather(j, n, rows, gsend, grecv)
     gather.start(low)
-    mine = pltpu.make_async_copy(low, grad_rows.at[j], sem)
-    mine.start()
-
-    def step(t):
-        pl.when(t > 0)(lambda: gather.step(t))
-        pl.when(t < n - 1)(lambda: scatter.step(t))
-
-    each(n, step)
-    scatter.arrive()
-
-    def settle(part):
-        layer_out[part, :] = (hidden[part, :] + scatter.result(part)).astype(jnp.bfloat16)
-
-    strips(low.shape[0], settle)
+    for copy in near():
+        copy.start()
+    rows[j] = low[...]
+    outs = Scatter(j, n, own, held, send4, recv4)
+    acc[...] = jnp.zeros_like(acc)
+
+    def fetch_out(block, slot):
+        return pltpu.make_async_copy(out_part.at[block], own.at[slot], own_sem.at[slot])
+
+    def outs_ahead(t):
+        for start in (True, False):
+            for side, block, live in outs.flows(t):
+                copy = fetch_out(block, outs.place(block, side))
+                pl.when(live)(copy.start if start else copy.wait)
+
+    def outs_step(t):
+        @pl.when((t >= 0) & (t < n - 1))
+        def _():
+            outs.step(t)
+            outs_ahead(t + 1)
+
+    outs_ahead(0)
+    fetch_out(j, 2).start()
+    fetch_out(j, 2).wait()
+
+    def unit_copies(block):
+        span = pl.ds(pl.multiple_of(block * local, local), local)
+        return (
+            pltpu.make_async_copy(pre.at[span, 0:width], unit_bp, unit_sem.at[0]),
+            pltpu.make_async_copy(
+                saved.at[span, 3 * width : 4 * width], unit_h, unit_sem.at[1]
+            ),
+            pltpu.make_async_copy(gated.at[span], unit_gated, unit_sem.at[2]),
+            pltpu.make_async_copy(normed_rows.at[block], unit_normed, unit_sem.at[3]),
+        )
+
+    def unit(block):
+        span = pl.ds(pl.multiple_of(block * local, local), local)
+        dh[span, :] = contract_cols(rows[block], wo[...])
+
+        def act(i):
+            part = pl.ds(pl.multiple_of(i * BLOCK, BLOCK), BLOCK)
+            spot = pl.ds(pl.multiple_of(block * local + i * BLOCK, BLOCK), BLOCK)
+            for t in range(tiles):
+                cols = pl.ds(t * LANES, LANES)
+                grad = dh[spot, cols]
+                value, slope = gelu_pair(unit_bp[part, cols])
+                dpre[spot, cols] = (grad * unit_h[part, cols] * slope).astype(bf16)
+                dh[spot, cols] = grad * value
+
+        each(local // BLOCK, act)
+        acc[0:width, :] += contract_rows(unit_gated[...], rows[block])
+        acc[width : 2 * width, :] += contract_rows(dpre[span, 0:width], unit_normed[...])
+
+    def visit(v):
+        t = (v + 1) // 2
+        block = jnp.where(v % 2 == 1, j - t, j + t)
+        live = (block >= 0) & (block < n)
+
+        @pl.when(live)
+        def _():
+            for copy in unit_copies(block):
+                copy.start()
+
+        @pl.when(v % 2 == 1)
+        def _():
+            gather.step(t)
+            outs_step(t - 1 - LAG)
+
+        @pl.when(live)
+        def _():
+            for copy in unit_copies(block):
+                copy.wait()
+            unit(block)
+
+    each(2 * n - 1, visit)
     gather.finish()
-    scatter.finish()
-    mine.wait()
-
-
-def gather_resid(low, out_part, hidden):
-    n = lax.axis_size("head")
-    local, depth = low.shape
-    bf16 = jnp.bfloat16
-    return line_call(
-        resid_kernel, 3, "gather_resid",
-        (jax.ShapeDtypeStruct((n, local, depth), bf16), jax.ShapeDtypeStruct((local, depth), bf16)),
-        [IN_VMEM] * 3,
-        [IN_ANY, IN_VMEM],
-        [
-            pltpu.VMEM((n + 1, local, depth), bf16),
-            *scatter_sems(n),
-            *gather_sems(n),
-            pltpu.SemaphoreType.DMA,
-        ],
-    )(low, out_part, hidden)
-
-
-def stream_kernel(dpre, wbi, stream, gain, resid, stream_grad, gain_grad, own, held, send, recv):
-    j, n = line_place()
-    line_barrier(j, n)
-    local = stream.shape[0]
-    scatter = Scatter(j, n, own, held, send, recv)
-
-    def compute(block):
-        part = pl.ds(pl.multiple_of(block * local, local), local)
-        own[block] = contract_cols(dpre[part, :], wbi[...]).astype(jnp.bfloat16)
+
+    def pack(target, source, count):
+        span = target.shape[1]
+
+        def strip(i):
+            row = pl.multiple_of(i * STRIP, STRIP)
+            target[row // span, pl.ds(pl.multiple_of(lax.rem(row, span), STRIP), STRIP), :] = source[
+                pl.ds(row, STRIP), :
+            ].astype(bf16)
+
+        each(count // STRIP, strip)
+
+    obsum = Sum(obterms, obslots, ob_total, sems[0:5])
+    isum = Sum(iterms, islots, i_total, sems[5:10])
+    gsum = Sum(gterms, gslots, g_total, sems[10:15])
+    pack(obterms, acc, 2 * width)
+    obsum.start()
+    load = pltpu.make_async_copy(normed_rows, rows, row_sem)
+    load.start()
+    load_hidden = pltpu.make_async_copy(hidden, wide, wide_sem.at[0])
+    load_hidden.start()
+
+    count = n * local // CHUNK
+
+    def chunk_copies(i):
+        base = lax.rem(i, 2) * (CHUNK + HALO)
+        start = pl.multiple_of(i * CHUNK, CHUNK)
+        ahead = pl.multiple_of(jnp.maximum(start - HALO, 0), HALO)
+        halo, main = pl.ds(pl.multiple_of(base, HALO), HALO), pl.ds(
+            pl.multiple_of(base + HALO, HALO), CHUNK
+        )
+        kept, x = slice(0, SAVED * width), slice(SAVED * width, (SAVED + 1) * width)
+        pairs = (
+            (saved.at[pl.ds(ahead, HALO)], acc.at[halo, kept]),
+            (saved.at[pl.ds(start, CHUNK)], acc.at[main, kept]),
+            (pre.at[pl.ds(ahead, HALO), width : 2 * width], acc.at[halo, x]),
+            (pre.at[pl.ds(start, CHUNK), width : 2 * width], acc.at[main, x]),
+        )
+        return [
+            pltpu.make_async_copy(a, b, chunk_sem.at[lax.rem(i, 2), k])
+            for k, (a, b) in enumerate(pairs)
+        ]
+
+    def total(v):
+        return jnp.sum(v, axis=0, keepdims=True)
+
+    for copy in chunk_copies(count - 1):
+        copy.start()
+    du[...] = jnp.zeros_like(du)
+    carry[...] = jnp.zeros_like(carry)
+    dgate[...] = jnp.zeros_like(dgate)
+    dpar[...] = jnp.zeros_like(dpar)
+
+    def chunk(k):
+        i = count - 1 - k
+
+        @pl.when(i > 0)
+        def _():
+            for copy in chunk_copies(i - 1):
+                copy.start()
+
+        for copy in chunk_copies(i):
+            copy.wait()
+        base = lax.rem(i, 2) * (CHUNK + HALO)
+        first = i * CHUNK
+        du[CHUNK:, :] = du[0:HALO, :]
+
+        def scan_step(b):
+            row = pl.multiple_of(CHUNK - BLOCK - b * BLOCK, BLOCK)
+            part = pl.ds(row, BLOCK)
+            spot = pl.ds(pl.multiple_of(first + row, BLOCK), BLOCK)
+            here = pl.ds(pl.multiple_of(base + HALO + row, HALO), BLOCK)
+            halo = pl.ds(pl.multiple_of(base + row, HALO), BLOCK + HALO)
+            fresh = doc_places(lengths, first + row, BLOCK) == 0
+            place = lax.broadcasted_iota(jnp.int32, (BLOCK, LANES), 0)
+            inner = place % 8
+            for t in range(tiles):
+                cols = pl.ds(t * LANES, LANES)
+                u, r, e = (acc[here, pl.ds(m * width + t * LANES, LANES)] for m in range(3))
+                prior = acc[halo, pl.ds(3 * width + t * LANES, LANES)][HALO - 1 : HALO - 1 + BLOCK]
+                near_h = dh[spot, cols]
+                decay = par[DECAY : DECAY + 1, cols]
+                c, m, ratio = decay_terms(r, decay, fresh)
+                b_, a_ = c * near_h, c
+                for d in (1, 2, 4):
+                    near_row = inner < 8 - d
+                    b_ = b_ + a_ * jnp.where(near_row, pltpu.roll(b_, BLOCK - d, 0), 0.0)
+                    a_ = a_ * jnp.where(near_row, pltpu.roll(a_, BLOCK - d, 0), 1.0)
+                later = carry[0:1, cols]
+                pieces = []
+                front = later
+                for g in reversed(range(BLOCK // 8)):
+                    eight = slice(g * 8, g * 8 + 8)
+                    state = b_[eight] + a_[eight] * front
+                    front = state[0:1]
+                    pieces.append(state)
+                carry[0:1, cols] = front
+                mu = jnp.concatenate(pieces[::-1], axis=0)
+                adj = near_h + jnp.where(
+                    place == BLOCK - 1, later, pltpu.roll(mu, BLOCK - 1, 0)
+                )
+                eu = e * u
+                dlog = adj * (prior * c - eu * ratio)
+                dpar[G_DECAY : G_DECAY + 1, cols] += total(dlog * r)
+                dzr = decay * dlog * (r * (1.0 - r))
+                dze = adj * m * eu * (1.0 - e)
+                dpar[G_RATE : G_RATE + 1, cols] += total(dzr)
+                dpar[G_ENTRY : G_ENTRY + 1, cols] += total(dze)
+                dz[part, cols] = dzr.astype(bf16)
+                dz[part, pl.ds(width + t * LANES, LANES)] = dze.astype(bf16)
+                du[part, cols] = adj * m * e
+
+        each(CHUNK // BLOCK, scan_step)
+        u_chunk = acc[pl.ds(pl.multiple_of(base + HALO, HALO), CHUNK), 0:width]
+        du[0:CHUNK, :] += contract_cols(dz[...], wg[...])
+        dgate[...] += contract_rows(u_chunk.astype(bf16), dz[...])
+
+        def conv_step(b):
+            row = pl.multiple_of(b * BLOCK, BLOCK)
+            spot = pl.ds(pl.multiple_of(first + row, BLOCK), BLOCK)
+            halo = pl.ds(pl.multiple_of(base + row, HALO), BLOCK + HALO)
+            place = doc_places(lengths, first + row, BLOCK + HALO)
+            for t in range(tiles):
+                cols = pl.ds(t * LANES, LANES)
+                ds = du[pl.ds(row, BLOCK + HALO), cols]
+                xs = acc[halo, pl.ds(SAVED * width + t * LANES, LANES)]
+                mine = ds[0:BLOCK]
+                dx = par[TAP : TAP + 1, cols] * mine
+                dpar[G_BIAS : G_BIAS + 1, cols] += total(mine)
+                dpar[G_TAP : G_TAP + 1, cols] += total(mine * xs[HALO:])
+                for k in range(1, CONVW):
+                    inside = jnp.where(place >= k, ds, 0.0)
+                    dx = dx + par[TAP + k : TAP + k + 1, cols] * inside[k : k + BLOCK]
+                    dpar[G_TAP + k : G_TAP + k + 1, cols] += total(
+                        inside[0:BLOCK] * xs[HALO - k : HALO - k + BLOCK]
+                    )
+                dpre[spot, pl.ds(width + t * LANES, LANES)] = dx.astype(bf16)
+
+        each(CHUNK // BLOCK, conv_step)
+        if LAG:
+            late = n - 1 - LAG
+
+            @pl.when((k % 2 == 1) & (k // 2 < LAG))
+            def _():
+                outs_step(late + k // 2)
+
+    each(count, chunk)
+
+    pack(gterms, dgate, width)
+    gsum.start()
+    pshare = Share("dp", pslots, psend, precv)
+    pslots[pshare.me] = dpar[...]
+    pshare.start()
+    outs.arrive()
+    load_hidden.wait()
+
+    def settle_out(part):
+        layer_out[part, :] = (wide[part, :] + outs.result(part)).astype(bf16)
+
+    strips(local, settle_out)
+    outs.finish()
+    load_resid = pltpu.make_async_copy(resid, wide, wide_sem.at[1])
+    load_resid.start()
+    for side in (-1, 1):
+
+        @pl.when((j + side >= 0) & (j + side < n))
+        def _():
+            pl.semaphore_signal(
+                free, inc=1, device_id={"head": j + side}, device_id_type=pl.DeviceIdType.MESH
+            )
+
+    scatter = Scatter(j, n, own, held, send8, recv8)
+
+    def compute(block, slot):
+        span = pl.ds(pl.multiple_of(block * local, local), local)
+        own[slot] = jnp.dot(dpre[span, :], wbi[...], preferred_element_type=f32).astype(bf16)
 
     def ahead(t):
-        for _, block, live in scatter.flows(t):
-            pl.when(live)(lambda: compute(block))
+        for side, block, live in scatter.flows(t):
+            pl.when(live)(functools.partial(compute, block, scatter.place(block, side)))
 
     ahead(0)
+    wait_neighbours(free, j, n)
+    scatter.step(0)
+    ahead(1)
+    load.wait()
+    for c in range(0, width, LANES):
+        acc[c : c + LANES, :] = contract_rows(
+            dpre[:, width + c : width + c + LANES], rows[...].reshape(n * local, depth)
+        )
+    pack(iterms, acc, width)
+    isum.start()
+    compute(j, 2)
+    obsum.spread()
 
     def step(t):
         scatter.step(t)
         ahead(t + 1)
-        pl.when(t == 0)(lambda: compute(j))
-
-    each(n - 1, step)
+
+        @pl.when(t == n // 2)
+        def _():
+            gsum.spread()
+            isum.spread()
+
+    lax.fori_loop(1, n - 1, lambda t, _: (step(t), 0)[1], 0)
     scatter.arrive()
-    gain_grad[...] = jnp.zeros_like(gain_grad)
+    load_resid.wait()
+    gains[...] = jnp.zeros_like(gains)
 
     def settle(part):
-        rinv, u = rms_parts(stream[part, :].astype(jnp.float32))
+        rinv, u = rms_parts(stream[part, :].astype(f32))
         grad = scatter.result(part)
-        gain_grad[...] += jnp.sum(grad * u, axis=0, keepdims=True)
-        total = resid[part, :] + norm_back(u, rinv, gain[...], grad)
-        stream_grad[part, :] = total.astype(jnp.bfloat16)
+        gains[0:1, :] += jnp.sum(grad * u, axis=0, keepdims=True)
+        value = wide[part, :] + norm_back(u, rinv, gain[...], grad)
+        stream_grad[part, :] = value.astype(bf16)
 
     strips(local, settle)
+
+    gains[1:2, :] = preffn_grad[...]
+    for axis, slots, ssem, rsem in (("dp", dslots, dsend, drecv), ("head", hslots, hsend, hrecv)):
+        share = Share(axis, slots, ssem, rsem)
+        slots[share.me] = gains[...]
+        share.start()
+        share.arrive()
+        value = slots[0]
+        for i in range(1, slots.shape[0]):
+            value = value + slots[i]
+        gains[...] = value
+        share.finish()
+
+    pshare.arrive()
+    value = pslots[0]
+    for i in range(1, pslots.shape[0]):
+        value = value + pslots[i]
+    par_grad[...] = value
+    pshare.finish()
+    for one in (gsum, obsum, isum):
+        one.finish()
     scatter.finish()
-
-
-def stream_back(dpre, wbi, stream, gain, resid):
-    n = lax.axis_size("head")
+    for copy in near():
+        copy.wait_send()
+    for k in range(sums.shape[0]):
+        pltpu.make_async_copy(sums.at[k], sums.at[k], trecv.at[k]).wait()
+
+
+def mixer_back(
+    lengths, low, out_part, hidden, terms, gated, wo, wbi, wg, par, pre, saved,
+    normed_rows, stream, gain, resid, preffn_grad,
+):
+    n, group = lax.axis_size("head"), lax.axis_size("dp")
     local, depth = stream.shape
+    width, tokens = wo.shape[0], pre.shape[0]
+    f32, bf16 = jnp.float32, jnp.bfloat16
+    ob = (group, 2 * width // group, depth)
+    one = (group, width // group, depth)
+    gate = (group, width // group, 2 * width)
+    dma = pltpu.SemaphoreType.DMA
+    shape = jax.ShapeDtypeStruct
     return line_call(
-        stream_kernel, 4, "stream_back",
+        back_kernel, 3, "mixer_back",
         (
-            jax.ShapeDtypeStruct((local, depth), jnp.bfloat16),
-            jax.ShapeDtypeStruct((1, depth), jnp.float32),
+            shape((local, depth), bf16),
+            shape((group - 2, *terms.shape[1:]), bf16),
+            shape((local, depth), bf16),
+            shape(ob, bf16),
+            shape(one, bf16),
+            shape(gate, bf16),
+            shape((PARAMS, width), f32),
+            shape((8, depth), f32),
         ),
-        [IN_VMEM] * 5,
-        [IN_VMEM, IN_VMEM],
         [
-            pltpu.VMEM((n, local, depth), jnp.bfloat16),
-            pltpu.VMEM((n + 1, local, depth), jnp.bfloat16),
+            IN_SMEM, IN_VMEM, IN_ANY, IN_ANY, IN_ANY, IN_ANY, *[IN_VMEM] * 4, IN_ANY, IN_ANY,
+            IN_ANY, IN_VMEM, IN_VMEM, IN_ANY, IN_VMEM,
+        ],
+        [IN_VMEM, IN_ANY, IN_VMEM, IN_ANY, IN_ANY, IN_ANY, IN_VMEM, IN_VMEM],
+        [
+            pltpu.VMEM((n, local, depth), bf16),
+            pltpu.VMEM((3, local, depth), bf16),
+            pltpu.VMEM((n + 1, local, depth), bf16),
+            pltpu.VMEM((tokens, width), f32),
+            pltpu.VMEM((tokens, 2 * width), bf16),
+            pltpu.VMEM((max(2 * width, 2 * (CHUNK + HALO)), depth), f32),
+            pltpu.VMEM((width, 2 * width), f32),
+            pltpu.VMEM((CHUNK, 2 * width), bf16),
+            pltpu.VMEM((CHUNK + HALO, width), f32),
+            pltpu.VMEM((8, width), f32),
+            pltpu.VMEM((PARAMS, width), f32),
+            pltpu.VMEM((local, depth), f32),
+            pltpu.VMEM((local, width), f32),
+            pltpu.VMEM((local, width), f32),
+            pltpu.VMEM((local, width), bf16),
+            pltpu.VMEM((local, depth), bf16),
+            pltpu.VMEM(ob, bf16),
+            pltpu.VMEM(ob, bf16),
+            pltpu.VMEM(one, bf16),
+            pltpu.VMEM(one, bf16),
+            pltpu.VMEM(gate, bf16),
+            pltpu.VMEM(gate, bf16),
+            pltpu.VMEM((group, PARAMS, width), f32),
+            pltpu.VMEM((group, 8, depth), f32),
+            pltpu.VMEM((n, 8, depth), f32),
+            *gather_sems(n),
             *scatter_sems(n),
+            *scatter_sems(n),
+            dma((group,)),
+            dma((group,)),
+            dma((4,)),
+            dma((3,)),
+            dma((2, 4)),
+            dma,
+            dma((2,)),
+            pltpu.SemaphoreType.REGULAR,
+            *share_sems("dp"),
+            *share_sems("dp"),
+            *share_sems("head"),
+            *sum_sems(),
+            *sum_sems(),
+            *sum_sems(),
         ],
-    )(dpre, wbi, stream, gain, resid)
-
-
-def places(lengths):
-    starts = jnp.cumsum(lengths, axis=1) - lengths
-    spots = jnp.arange(SEQ, dtype=jnp.int32)
-    earlier = jnp.where(starts[:, :, None] <= spots[None, None, :], starts[:, :, None], 0)
-    return (spots[None, :] - jnp.max(earlier, axis=1))[0]
+    )(
+        lengths, low, out_part, hidden, terms, gated, wo, wbi, wg, par, pre, saved,
+        normed_rows, stream, gain, resid, preffn_grad,
+    )
 
 
 def widen(values, width):
-    return jnp.pad(values, ((0, 0), (0, width - values.shape[1])))
+    return jnp.pad(values, ((0, width - values.shape[0]), (0, 0)))
 
 
 def block_diagonal(weights, width):
@@ -950,7 +1301,6 @@
     chans = branch_weight.shape[1]
     width = -(-chans // LANES) * LANES
 
-    pos = jnp.broadcast_to(places(doc_lengths)[:, None], (SEQ, LANES))
     slope = -DECAY_SCALE * jax.nn.softplus(decay_param.astype(f32))
     par = jnp.concatenate(
         [
@@ -966,62 +1316,45 @@
     wg = jnp.concatenate(
         [block_diagonal(rate_weight, width), block_diagonal(entry_weight, width)], axis=1
     )
-    wbi = jnp.concatenate([widen(branch_weight, width), widen(input_weight, width)], axis=1)
-    wo = jnp.pad(output_weight, ((0, width - chans), (0, 0)))
+    wbi = jnp.concatenate([widen(branch_weight.T, width), widen(input_weight.T, width)])
+    wo = widen(output_weight, width)
 
     premix = premix_gain.astype(f32)[None]
     preffn = preffn_gain.astype(f32)[None]
     normed_rows, pre = project(stream, premix, wbi)
-    u, r, e, h, gated = rec_fwd(pre, pos, wg, par)
+    saved, gated = rec_fwd(doc_lengths, pre, wg, par)
     cot_rows, hidden_in, ffn_low = mixer_out(gated, wo, stream, preffn, cotangent)
 
-    out_part, terms, resid_grad, resid_low, preffn_grad = feed_forward(
+    out_part, terms, far_terms, resid_grad, resid_low, preffn_grad = feed_forward(
         ffn_low, cot_rows, cotangent, hidden_in, preffn, ffn_gate, ffn_upward, ffn_down
     )
-    ffn_sums = lax.psum_scatter(terms, "dp", scatter_dimension=0, tiled=False).astype(f32)
-
-    grad_rows, layer_out = gather_resid(resid_low, out_part, hidden_in)
-    grad_rows = grad_rows.reshape(SEQ, -1)
-    gated_grad = contract_cols(grad_rows, wo)
-    output_grad = contract_rows(gated, grad_rows)[:chans]
-    dpre, dgate, dpar = rec_bwd(gated_grad, pre, pos, u, r, e, h, wg, par)
-    dwbi = contract_rows(normed_rows.reshape(SEQ, -1), dpre)
-    stream_grad, premix_grad = stream_back(dpre, wbi, stream, premix, resid_grad)
-
-    sums = lax.psum(
-        tuple(
-            v.astype(bf16)
-            for v in (
-                dwbi[:, :chans],
-                dwbi[:, width : width + chans],
-                output_grad,
-                diagonal_blocks(dgate[:, :width], heads, size),
-                diagonal_blocks(dgate[:, width:], heads, size),
-                dpar[:, :chans],
-            )
-        ),
-        "dp",
+
+    layer_out, sums, stream_grad, ob_grad, input_grad, gate_grad, dpar, gains = mixer_back(
+        doc_lengths, resid_low, out_part, hidden_in, terms, gated, wo, wbi, wg, par, pre, saved,
+        normed_rows, stream, premix, resid_grad, preffn_grad,
     )
-    branch_grad, input_grad, output_grad, rate_grad, entry_grad, dpar = (
-        v.astype(f32) for v in sums
-    )
-    premix_grad, preffn_grad = lax.psum((premix_grad[0], preffn_grad[0]), ("dp", "head"))
+    mine = lax.dynamic_index_in_dim(terms, lax.axis_index("dp"), keepdims=False)
+    ffn_sums = mine.astype(f32) + far_terms.astype(f32) + jnp.sum(sums.astype(f32), axis=0)
+    ob_grad = ob_grad.reshape(2 * width, -1).astype(f32)
+    input_grad = input_grad.reshape(width, -1).astype(f32)
+    gate_grad = gate_grad.reshape(width, -1).astype(f32)
+    dpar = dpar[:, :chans]
     decay_grad = dpar[G_DECAY] * (-DECAY_SCALE * jax.nn.sigmoid(decay_param.astype(f32)))
     return (
         layer_out,
         stream_grad,
-        premix_grad,
-        branch_grad,
-        input_grad,
+        gains[0],
+        ob_grad[width : width + chans].T,
+        input_grad[:chans].T,
         dpar[G_TAP : G_TAP + CONVW],
         dpar[G_BIAS],
-        rate_grad,
+        diagonal_blocks(gate_grad[:, :width], heads, size),
         dpar[G_RATE].reshape(heads, size),
-        entry_grad,
+        diagonal_blocks(gate_grad[:, width:], heads, size),
         dpar[G_ENTRY].reshape(heads, size),
         decay_grad,
-        output_grad,
-        preffn_grad,
+        ob_grad[:chans],
+        gains[1],
         ffn_sums[0],
         ffn_sums[1],
         ffn_sums[2],

time: 794 us -> 643 us (0.81)
  waiting for transfers between devices: 66.8 us -> 0 us
  blocking collectives: 64.6 us -> 0 us
  Pallas kernels: 577 us -> 602 us
  matrix products: 19.4 us -> 0 us
  between operations: 14.4 us -> 0.94 us
  local copies, waits for them, and re-layouts: 32 us -> 21.7 us
    unnamed x3 -> x0, waiting for transfers between devices: 66.8 us -> none
    psum x2 -> x0, blocking collectives: 64.6 us -> none  [the longest x1 54.5 us: shards(): lax.psum((premix_grad[0], preffn_grad[0]), ('dp', 'head'))]
    pallas_call x4 -> x2, Pallas kernels: 225 us -> 246 us  [the longest x1 227 us: mixer_back(): line_call(back_kernel, 3, 'mixer_back', (shape((local, depth), bf16), sha...]
    dot_general x3 -> x0, matrix products: 19.4 us -> none  [the longest x2 14.9 us: contract_rows(): lax.dot_general(leading, trailing, (((0,), (0,)), ((), ())), preferred_el...]
    unnamed x48, local copies, waits for them, and re-layouts: 17.4 us -> 7.96 us
    convert_element_type x5 -> x2, other arithmetic: 9.14 us -> 1.15 us  [the longest x1 1.03 us: shards(): ob_grad = ob_grad.reshape(2 * width, -1).astype(f32)]
  transfers between devices with their start and end apart: 2 -> 0, of which waited for: 1 -> 0; matrix products, arithmetic and copies ran while one was open for 2% -> 0% of each run, Pallas kernels for 10% -> 0%
where the time goes in v3:
time: 643 us; the launch traced here: 642 us
  Pallas kernels  602 us (94%)
  local copies, waits for them, and re-layouts  21.7 us (3%)
  other arithmetic  16.7 us (3%)
    pallas_call x1, Pallas kernels, mixer_back(): line_call(back_kernel, 3, 'mixer_back', (shape((local, depth), bf16), sha...  227 us
    pallas_call x1, Pallas kernels, feed_forward(): line_call(ffn_kernel, 2, 'feed_forward', (jax.ShapeDtypeStruct((n, local,...  172 us
    pallas_call x1, Pallas kernels, mixer_out(): line_call(mixer_out_kernel, 1, 'mixer_out', (jax.ShapeDtypeStruct((n, loc...  103 us
    pallas_call x1, Pallas kernels, project(): line_call(project_kernel, 0, 'gather_project', (jax.ShapeDtypeStruct((n,...  81.5 us
    pallas_call x1, Pallas kernels, rec_fwd(): pl.pallas_call(rec_fwd_kernel, grid=(length // CHUNK,), out_shape=(jax.Sh...  18.5 us

profile of v3, /device:TPU:0, one launch (start us, length us, event | category | flops | bytes accessed | tf_op | source)
XLA Modules:
  0.0 641.8 jit_solution(127963904004593055)
XLA Ops:
  0.7 0.0 copy-start.9
  0.7 0.0 copy-start.8
  0.7 1.5 fusion.16
  2.2 0.1 pad_add_fusion
  2.3 1.3 fusion.15
  3.6 0.1 pad_add_fusion.1
  3.7 0.1 pad_maximum_fusion.wg
  3.8 0.0 copy-start.2
  3.8 0.0 copy-start.15
  3.8 0.0 copy-done.9
  3.8 0.0 copy-done.8
  3.8 1.9 fusion.3.wbi
  5.8 0.0 copy-done.15
  5.8 0.0 copy-start.21
  5.8 0.0 copy-start.18
  5.8 0.0 copy-start.4
  5.8 0.6 broadcast_in_dim.26
  6.4 81.5 %gather_project.1 = (bf16[8,256,2048]{2,1,0:T(8,128)(2,1)}, f32[2048,768]{1,0:T(8,128)}) custom-call(bf16[256,2048]{1,0:T(8,128)(2,1)} %stream.5, f32[1,2048]{1,0:T(1,128)} %bitcast.47, bf16[768,2048]{1,0:T(8,128)(2,1)} %fusion.3.wbi), custom_call_target="tpu_custom_call" | custom-call | tf_op jit(solution)/shard_map/gather_project/pallas_call | solution.py:569
  88.0 0.0 copy-done.17
  88.0 0.0 copy-done.19
  88.0 0.0 copy-done.20
  88.1 0.1 reshape.89
  88.1 0.0 copy-done.21
  88.1 0.1 reshape.90
  88.2 0.0 copy-done.18
  88.3 0.1 pad_select_fusion.par
  88.4 0.0 copy-done.2
  88.4 0.0 copy-done.4
  88.4 2.8 copy-done
  91.2 18.5 %recurrence_forward.1 = (f32[2048,1536]{1,0:T(8,128)}, bf16[2048,384]{1,0:T(8,128)(2,1)S(1)}) custom-call(s32[1,8]{1,0:T(1,128)S(1)} %copy-done.4, f32[2048,768]{1,0:T(8,128)S(1)} %copy-done, bf16[384,768]{1,0:T(8,128)(2,1)S(1)} %pad_maximum_fusion.wg, f32[8,384]{1,0:T(8,128)S(1)} %pad_select_fusion.par), custom_call_target="tpu_custom_call" | custom-call | tf_op jit(solution)/shard_map/recurrence_forward/pallas_call | solution.py:171
  109.7 0.0 copy-done.3
  109.7 1.1 copy-done.1
  110.8 0.0 copy-done.7
  110.8 1.3 pad.35.wo
  112.1 0.0 copy-done.16
  112.1 0.6 broadcast_in_dim.27
  112.7 103.4 %mixer_out.1 = (bf16[8,256,2048]{2,1,0:T(8,128)(2,1)}, f32[256,2048]{1,0:T(8,128)}, bf16[256,2048]{1,0:T(8,128)(2,1)}) custom-call(bf16[2048,384]{1,0:T(8,128)(2,1)} %copy-done.1, bf16[384,2048]{1,0:T(8,128)(2,1)} %pad.35.wo, bf16[256,2048]{1,0:T(8,128)(2,1)} %stream.5, f32[1,2048]{1,0:T(1,128)} %bitcast.45, bf16[256,2048]{1,0:T(8,128)(2,1)} %cot.3), custom_call_target="tpu_custom_call" | custom-call | tf_op jit(solution)/shard_map/mixer_out/pallas_call | solution.py:646
  216.2 171.9 %feed_forward.1 = (bf16[8,256,2048]{2,1,0:T(8,128)(2,1)}, bf16[4,3,512,768]{3,2,1,0:T(8,128)(2,1)}, bf16[3,512,768]{2,1,0:T(8,128)(2,1)}, f32[256,2048]{1,0:T(8,...) custom-call(bf16[256,2048]{1,0:T(8,128)(2,1)} %get-tuple-element.40.low, ...), custom_call_target="tpu_custom_call" | custom-call | tf_op jit(solution)/shard_map/feed_forward/pallas_call | solution.py:816
  388.1 227.1 %mixer_back.1 = (bf16[256,2048]{1,0:T(8,128)(2,1)}, bf16[2,3,512,768]{3,2,1,0:T(8,128)(2,1)}, bf16[256,2048]{1,0:T(8,128)(2,1)}, bf16[4,192,2048]{2,1,0:T(8,128)...) custom-call(s32[1,8]{1,0:T(1,128)} %lengths.3, ...), custom_call_target="tpu_custom_call" | custom-call | tf_op jit(solution)/shard_map/mixer_back/pallas_call | solution.py:1209
  615.2 0.0 copy-start.6
  615.2 5.8 convert_reduce_fusion
  621.0 0.0 copy-done.6
  621.0 3.7 fusion.2
  624.7 0.0 copy-start.13
  624.8 2.3 slice_bitcast_fusion.1
  627.0 0.0 copy-done.13
  627.0 0.1 bitcast_convert_fusion.1
  627.2 0.2 slice_bitcast_fusion.5
  627.4 1.0 copy.46
  628.4 1.0 copy.45
  629.4 0.0 copy-done.5
  629.4 1.0 bitcast_convert_fusion
  630.4 0.0 copy-start.10
  630.4 2.9 fusion.14
  633.3 0.0 copy-done.10
  633.3 1.9 convert_bitcast_fusion
  635.2 1.5 fusion.17
  636.7 0.6 slice_reduce_fusion
  637.4 0.6 fusion.8
  637.9 0.7 reshape_squeeze.6
  638.6 0.7 reshape_squeeze.7
  639.3 0.6 slice.83
  639.9 1.0 copy.57
  640.8 1.0 copy.58
  (25 shorter events, 0.2 us)
Async XLA Ops:
  0.7 3.2 copy-start.9
  0.7 3.2 copy-start.8
  3.8 84.6 %copy-start.2 = (bf16[384,768]{1,0:T(8,128)(2,1)}, bf16[384,768]{1,0:T(8,128)(2,1)S(1)}, u32[]{:S(2)}) copy-start(bf16[384,768]{1,0:T(8,128)(2,1)S(1)} %pad_maximum_fusion.wg) | copy-start | bytes 1769476
  3.8 2.0 copy-start.15
  5.8 82.2 %copy-start.17 = (bf16[342]{0:T(512)(128)(2,1)S(1)}, bf16[342]{0:T(512)(128)(2,1)}, u32[]{:S(2)}) copy-start(bf16[342]{0:T(512)(128)(2,1)} %param.29) | copy-start | bytes 2056
  5.8 82.2 %copy-start.19 = (bf16[342]{0:T(512)(128)(2,1)S(1)}, bf16[342]{0:T(512)(128)(2,1)}, u32[]{:S(2)}) copy-start(bf16[342]{0:T(512)(128)(2,1)} %param.24) | copy-start | bytes 2056
  5.8 82.3 %copy-start.20 = (bf16[2,171]{1,0:T(2,128)(2,1)S(1)}, bf16[2,171]{1,0:T(2,128)(2,1)}, u32[]{:S(2)}) copy-start(bf16[2,171]{1,0:T(2,128)(2,1)} %param.26) | copy-start | bytes 2056
  5.8 82.3 %copy-start.21 = (bf16[2,171]{1,0:T(2,128)(2,1)S(1)}, bf16[2,171]{1,0:T(2,128)(2,1)}, u32[]{:S(2)}) copy-start(bf16[2,171]{1,0:T(2,128)(2,1)} %param.28) | copy-start | bytes 2056
  5.8 82.4 %copy-start.18 = (bf16[4,342]{1,0:T(4,128)(2,1)S(1)}, bf16[4,342]{1,0:T(4,128)(2,1)}, u32[]{:S(2)}) copy-start(bf16[4,342]{1,0:T(4,128)(2,1)} %param.23) | copy-start | bytes 8212
  5.8 82.5 %copy-start.4 = (s32[1,8]{1,0:T(1,128)S(1)}, s32[1,8]{1,0:T(1,128)}, u32[]{:S(2)}) copy-start(s32[1,8]{1,0:T(1,128)} %lengths.3) | copy-start | bytes 100
  88.4 2.8 copy-start
  91.1 18.5 %copy-start.3 = (f32[8,384]{1,0:T(8,128)}, f32[8,384]{1,0:T(8,128)S(1)}, u32[]{:S(2)}) copy-start(f32[8,384]{1,0:T(8,128)S(1)} %pad_select_fusion.par) | copy-start | bytes 36868
  91.2 19.7 %copy-start.7 = (bf16[342,2048]{1,0:T(8,128)(2,1)S(1)}, bf16[342,2048]{1,0:T(8,128)(2,1)}, u32[]{:S(2)}) copy-start(bf16[342,2048]{1,0:T(8,128)(2,1)} %param.30) | copy-start | bytes 4202500
  91.2 21.0 %copy-start.16 = (bf16[2048]{0:T(1024)(128)(2,1)S(1)}, bf16[2048]{0:T(1024)(128)(2,1)}, u32[]{:S(2)}) copy-start(bf16[2048]{0:T(1024)(128)(2,1)} %param.31) | copy-start | bytes 12292
  109.7 1.1 copy-start.1
  615.2 5.8 copy-start.6
  624.7 2.3 copy-start.13
  627.0 2.4 copy-start.5
  630.4 2.9 copy-start.10
  633.3 3.4 copy-start.14
  633.3 6.6 %copy-start.12 = (bf16[256,2048]{1,0:T(8,128)(2,1)S(1)}, bf16[256,2048]{1,0:T(8,128)(2,1)}, u32[]{:S(2)}) copy-start(bf16[256,2048]{1,0:T(8,128)(2,1)} %get-tuple-element.133) | copy-start | bytes 3145732
  633.3 7.5 %copy-start.11 = (bf16[256,2048]{1,0:T(8,128)(2,1)S(1)}, bf16[256,2048]{1,0:T(8,128)(2,1)}, u32[]{:S(2)}) copy-start(bf16[256,2048]{1,0:T(8,128)(2,1)} %get-tuple-element.134) | copy-start | bytes 3145732

commit v4 on v3

--- a/solution.py
+++ b/solution.py
@@ -16,6 +16,7 @@
 HALO = 8
 PARTS = 2
 LAG = 1
+FAR_TERMS = 2
 VMEM_BYTES = 62 * 2**20
 IN_VMEM = pl.BlockSpec(memory_space=pltpu.VMEM)
 IN_SMEM = pl.BlockSpec(memory_space=pltpu.SMEM)
@@ -93,100 +94,6 @@
     return spots - begin
 
 
-def rec_fwd_kernel(lengths, pre, wg, par, saved, gated, xbuf, z, carry):
-    width = gated.shape[1]
-    u_out, r_out, e_out, h_out = (
-        saved.at[:, i * width : (i + 1) * width] for i in range(SAVED)
-    )
-    tiles = width // LANES
-
-    @pl.when(pl.program_id(0) == 0)
-    def _():
-        xbuf[0:HALO, :] = jnp.zeros((HALO, width), jnp.float32)
-        carry[...] = jnp.zeros_like(carry)
-
-    @pl.when(pl.program_id(0) > 0)
-    def _():
-        xbuf[0:HALO, :] = xbuf[CHUNK : CHUNK + HALO, :]
-
-    xbuf[HALO : HALO + CHUNK, :] = pre[:, width:]
-
-    first = pl.program_id(0) * CHUNK
-
-    def conv_step(i, _):
-        row = pl.multiple_of(i * BLOCK, BLOCK)
-        place = doc_places(lengths, first + row, BLOCK)
-        for t in range(tiles):
-            cols = pl.ds(t * LANES, LANES)
-            xs = xbuf[pl.ds(row, BLOCK + HALO), cols]
-            total = par[BIAS : BIAS + 1, cols] + par[TAP : TAP + 1, cols] * xs[HALO:]
-            for k in range(1, CONVW):
-                term = par[TAP + k : TAP + k + 1, cols] * xs[HALO - k : HALO - k + BLOCK]
-                total = total + jnp.where(place >= k, term, 0.0)
-            u_out[pl.ds(row, BLOCK), cols] = total
-        return 0
-
-    lax.fori_loop(0, CHUNK // BLOCK, conv_step, 0)
-    z[...] = jnp.dot(u_out[...].astype(jnp.bfloat16), wg[...], preferred_element_type=jnp.float32)
-
-    def scan_step(i, _):
-        row = pl.multiple_of(i * BLOCK, BLOCK)
-        rows = pl.ds(row, BLOCK)
-        fresh = doc_places(lengths, first + row, BLOCK) == 0
-        inner = lax.broadcasted_iota(jnp.int32, (BLOCK, LANES), 0) % 8
-        for t in range(tiles):
-            cols = pl.ds(t * LANES, LANES)
-            other = pl.ds(width + t * LANES, LANES)
-            r = jax.nn.sigmoid(z[rows, cols] + par[RATE_B : RATE_B + 1, cols])
-            e = jax.nn.sigmoid(z[rows, other] + par[ENTRY_B : ENTRY_B + 1, cols])
-            u = u_out[rows, cols]
-            c, m, _ = decay_terms(r, par[DECAY : DECAY + 1, cols], fresh)
-            r_out[rows, cols] = r
-            e_out[rows, cols] = e
-            b = m * e * u
-            for d in (1, 2, 4):
-                near = inner >= d
-                b = b + c * jnp.where(near, pltpu.roll(b, d, 0), 0.0)
-                c = c * jnp.where(near, pltpu.roll(c, d, 0), 1.0)
-            last = carry[0:1, cols]
-            pieces = []
-            for g in range(BLOCK // 8):
-                part = slice(g * 8, g * 8 + 8)
-                state = b[part] + c[part] * last
-                last = state[7:8]
-                pieces.append(state)
-            carry[0:1, cols] = last
-            h = jnp.concatenate(pieces, axis=0)
-            h_out[rows, cols] = h
-            gated[rows, cols] = (h * gelu(pre[rows, cols])).astype(jnp.bfloat16)
-        return 0
-
-    lax.fori_loop(0, CHUNK // BLOCK, scan_step, 0)
-
-
-def rec_fwd(lengths, pre, wg, par):
-    length, width = pre.shape[0], pre.shape[1] // 2
-    rows = lambda cols: pl.BlockSpec((CHUNK, cols), lambda i: (i, 0))
-    whole = lambda a: pl.BlockSpec(a.shape, lambda i: (0,) * a.ndim)
-    return pl.pallas_call(
-        rec_fwd_kernel,
-        grid=(length // CHUNK,),
-        out_shape=(
-            jax.ShapeDtypeStruct((length, SAVED * width), jnp.float32),
-            jax.ShapeDtypeStruct((length, width), jnp.bfloat16),
-        ),
-        in_specs=[IN_SMEM, rows(2 * width), whole(wg), whole(par)],
-        out_specs=[rows(SAVED * width), rows(width)],
-        scratch_shapes=[
-            pltpu.VMEM((CHUNK + HALO, width), jnp.float32),
-            pltpu.VMEM((CHUNK, 2 * width), jnp.float32),
-            pltpu.VMEM((8, width), jnp.float32),
-        ],
-        compiler_params=pltpu.CompilerParams(vmem_limit_bytes=40 * 2**20),
-        name="recurrence_forward",
-    )(lengths, pre, wg, par)
-
-
 def each(count, body):
     def step(i, _):
         body(i)
@@ -208,14 +115,49 @@
     return lax.axis_size(axis) - 1 - lax.axis_index(axis)
 
 
-def near_peers(axis):
-    n, me = lax.axis_size(axis), lax.axis_index(axis)
-    far = far_peer(axis)
+def far_copies(terms, far_terms, sems):
+    far = far_peer("dp")
+    return [
+        pltpu.make_async_remote_copy(
+            src_ref=terms.at[far, k],
+            dst_ref=far_terms.at[k],
+            send_sem=sems.at[0, k],
+            recv_sem=sems.at[1, k],
+            device_id={"dp": far},
+            device_id_type=pl.DeviceIdType.MESH,
+        )
+        for k in range(far_terms.shape[0])
+    ]
+
+
+def near_copies(terms, near_terms, last_terms, sems):
+    n, me, far = lax.axis_size("dp"), lax.axis_index("dp"), far_peer("dp")
     for k in range(n - 2):
         peer = k + jnp.where(k >= jnp.minimum(me, far), 1, 0)
         peer = peer + jnp.where(k + 1 >= jnp.maximum(me, far), 1, 0)
-        ahead = jnp.where(peer < me, 1, 0) + jnp.where(n - 1 - peer < me, 1, 0)
-        yield k, peer, me - ahead
+        slot = me - jnp.where(peer < me, 1, 0) - jnp.where(n - 1 - peer < me, 1, 0)
+        yield pltpu.make_async_remote_copy(
+            src_ref=terms.at[peer],
+            dst_ref=near_terms.at[slot],
+            send_sem=sems.at[0, k],
+            recv_sem=sems.at[1, slot],
+            device_id={"dp": peer},
+            device_id_type=pl.DeviceIdType.MESH,
+        )
+    yield pltpu.make_async_remote_copy(
+        src_ref=terms.at[far, 2],
+        dst_ref=last_terms,
+        send_sem=sems.at[0, n - 2],
+        recv_sem=sems.at[1, n - 2],
+        device_id={"dp": far},
+        device_id_type=pl.DeviceIdType.MESH,
+    )
+
+
+def near_arrive(near_terms, last_terms, sems):
+    for k in range(near_terms.shape[0]):
+        pltpu.make_async_copy(near_terms.at[k], near_terms.at[k], sems.at[1, k]).wait()
+    pltpu.make_async_copy(last_terms, last_terms, sems.at[1, near_terms.shape[0]]).wait()
 
 
 def peer_barrier(axes):
@@ -280,16 +222,16 @@
             block = self.j - side * t
             yield side, block, (block >= 0) & (block < self.n)
 
-    def start(self, source):
-        for s in range(PARTS):
+    def start(self, source, parts=range(PARTS)):
+        for s in parts:
             for side in (1, -1):
 
                 @pl.when(self.there(side))
                 def _():
                     self.copy(self.j, s, side, source).start()
 
-    def step(self, t):
-        for s in range(PARTS):
+    def step(self, t, parts=range(PARTS)):
+        for s in parts:
             for side, block, live in self.flows(t):
 
                 @pl.when(live)
@@ -352,8 +294,8 @@
             device_id_type=pl.DeviceIdType.MESH,
         )
 
-    def step(self, t):
-        for s in range(PARTS):
+    def step(self, t, parts=range(PARTS)):
+        for s in parts:
             for side, block, live in self.flows(t):
                 behind = (self.j - side >= 0) & (self.j - side < self.n)
 
@@ -517,30 +459,55 @@
     each(rows // STRIP, lambda i: body(pl.ds(pl.multiple_of(i * STRIP, STRIP), STRIP)))
 
 
-def project_kernel(
-    stream, gain, wbi, rows_out, pre, normed, rows, send, recv, keep_sem
+def front_kernel(
+    lengths, stream, premix, wb, wi, wo_in, wg, par, preffn, cot,
+    rows_out, pre_out, saved, gated_out, wbi_out, wo_out, cot_rows, hidden, low_out,
+    normed, rows, wbi, wo, pre, gated, stage, z, carry, own, held,
+    gsend, grecv, csend, crecv, send, recv, keep_sem, pre_sem, stage_sem, one_sem,
 ):
     j, n = line_place()
+    f32, bf16 = jnp.float32, jnp.bfloat16
+    local, depth = stream.shape
+    width, chans = gated.shape[1], wb.shape[0]
+    tiles = width // LANES
     line_barrier(j, n)
-    local = stream.shape[0]
 
     def norm(part):
-        _, unit = rms_parts(stream[part, :].astype(jnp.float32))
-        normed[part, :] = (unit * gain[...]).astype(jnp.bfloat16)
+        _, unit = rms_parts(stream[part, :].astype(f32))
+        normed[part, :] = (unit * premix[...]).astype(bf16)
 
     strips(local, norm)
-    gather = Gather(j, n, rows, send, recv)
+    gather = Gather(j, n, rows, gsend, grecv)
     gather.start(normed)
-
-    def project(block, source):
-        part = pl.ds(pl.multiple_of(block * local, local), local)
-        pre[part, :] = contract_cols(source, wbi[...])
+    for target, first, source in ((wbi, 0, wb), (wbi, width, wi), (wo, 0, wo_in)):
+        whole = chans // STRIP * STRIP
+        target[first + whole : first + width, :] = jnp.zeros((width - whole, depth), bf16)
+        target[first : first + chans, :] = source[...]
+    out_copies = [
+        pltpu.make_async_copy(wbi, wbi_out, one_sem.at[0]),
+        pltpu.make_async_copy(wo, wo_out, one_sem.at[1]),
+    ]
+    for copy in out_copies:
+        copy.start()
+
+    def span(block):
+        return pl.ds(pl.multiple_of(block * local, local), local)
+
+    def shifted(block):
+        return pl.ds(pl.multiple_of(block * local + HALO, HALO), local)
 
     def keep(source, block):
         return pltpu.make_async_copy(source, rows_out.at[block], keep_sem.at[block])
 
+    def keep_pre(block):
+        return pltpu.make_async_copy(
+            pre.at[shifted(block)], pre_out.at[span(block)], pre_sem.at[block]
+        )
+
+    pre[0:HALO, :] = jnp.zeros((HALO, 2 * width), f32)
     keep(normed, j).start()
-    project(j, normed[...])
+    pre[shifted(j), :] = contract_cols(normed[...], wbi[...])
+    keep_pre(j).start()
 
     def visit(v):
         t = v // 2 + 1
@@ -553,185 +520,278 @@
         @pl.when((block >= 0) & (block < n))
         def _():
             keep(rows.at[block], block).start()
-            project(block, rows[block])
+            pre[shifted(block), :] = contract_cols(rows[block], wbi[...])
+            keep_pre(block).start()
 
     each(2 * (n - 1), visit)
+    cots = Gather(j, n, cot_rows, csend, crecv)
+    cots.start(cot)
+    mine = pltpu.make_async_copy(cot, cot_rows.at[j], one_sem.at[2])
+    mine.start()
+
+    carry[...] = jnp.zeros_like(carry)
+    count = n * local // CHUNK
+
+    def keep_stage(i):
+        return pltpu.make_async_copy(
+            stage.at[lax.rem(i, 2)],
+            saved.at[pl.ds(pl.multiple_of(i * CHUNK, CHUNK), CHUNK)],
+            stage_sem.at[lax.rem(i, 2)],
+        )
+
+    def chunk(i):
+        first = i * CHUNK
+
+        @pl.when(i >= 2)
+        def _():
+            keep_stage(i - 2).wait()
+
+        u_out, r_out, e_out, h_out = (
+            stage.at[lax.rem(i, 2), :, k * width : (k + 1) * width] for k in range(SAVED)
+        )
+
+        def conv_step(b):
+            row = pl.multiple_of(b * BLOCK, BLOCK)
+            halo = pl.ds(pl.multiple_of(first + row, BLOCK), BLOCK + HALO)
+            place = doc_places(lengths, first + row, BLOCK)
+            for t in range(tiles):
+                cols = pl.ds(t * LANES, LANES)
+                xs = pre[halo, pl.ds(width + t * LANES, LANES)]
+                total = par[BIAS : BIAS + 1, cols] + par[TAP : TAP + 1, cols] * xs[HALO:]
+                for k in range(1, CONVW):
+                    term = par[TAP + k : TAP + k + 1, cols] * xs[HALO - k : HALO - k + BLOCK]
+                    total = total + jnp.where(place >= k, term, 0.0)
+                u_out[pl.ds(row, BLOCK), cols] = total
+
+        each(CHUNK // BLOCK, conv_step)
+        z[...] = jnp.dot(u_out[...].astype(bf16), wg[...], preferred_element_type=f32)
+
+        def scan_step(b):
+            row = pl.multiple_of(b * BLOCK, BLOCK)
+            part = pl.ds(row, BLOCK)
+            spot = pl.ds(pl.multiple_of(first + row, BLOCK), BLOCK)
+            here = pl.ds(pl.multiple_of(first + row + HALO, HALO), BLOCK)
+            fresh = doc_places(lengths, first + row, BLOCK) == 0
+            inner = lax.broadcasted_iota(jnp.int32, (BLOCK, LANES), 0) % 8
+            for t in range(tiles):
+                cols = pl.ds(t * LANES, LANES)
+                other = pl.ds(width + t * LANES, LANES)
+                r = jax.nn.sigmoid(z[part, cols] + par[RATE_B : RATE_B + 1, cols])
+                e = jax.nn.sigmoid(z[part, other] + par[ENTRY_B : ENTRY_B + 1, cols])
+                u = u_out[part, cols]
+                c, m, _ = decay_terms(r, par[DECAY : DECAY + 1, cols], fresh)
+                r_out[part, cols] = r
+                e_out[part, cols] = e
+                b_ = m * e * u
+                for d in (1, 2, 4):
+                    near = inner >= d
+                    b_ = b_ + c * jnp.where(near, pltpu.roll(b_, d, 0), 0.0)
+                    c = c * jnp.where(near, pltpu.roll(c, d, 0), 1.0)
+                last = carry[0:1, cols]
+                pieces = []
+                for g in range(BLOCK // 8):
+                    eight = slice(g * 8, g * 8 + 8)
+                    state = b_[eight] + c[eight] * last
+                    last = state[7:8]
+                    pieces.append(state)
+                carry[0:1, cols] = last
+                h = jnp.concatenate(pieces, axis=0)
+                h_out[part, cols] = h
+                gated[spot, cols] = (h * gelu(pre[here, cols])).astype(bf16)
+
+        each(CHUNK // BLOCK, scan_step)
+        keep_stage(i).start()
+
+        @pl.when(i == count * 5 // 8)
+        def _():
+            cots.step(1)
+
+    each(count, chunk)
+    keep_gated = pltpu.make_async_copy(gated, gated_out, one_sem.at[3])
+    keep_gated.start()
+
+    scatter = Scatter(j, n, own, held, send, recv)
+
+    def compute(block, slot):
+        own[slot] = jnp.dot(
+            gated[span(block), :], wo[...], preferred_element_type=f32
+        ).astype(bf16)
+
+    def ahead(t):
+        for side, block, live in scatter.flows(t):
+            pl.when(live)(functools.partial(compute, block, scatter.place(block, side)))
+
+    ahead(0)
+
+    def step(t):
+        scatter.step(t)
+        ahead(t + 1)
+
+        @pl.when(t == 0)
+        def _():
+            compute(j, 2)
+
+        @pl.when(t + 2 < n)
+        def _():
+            cots.step(t + 2)
+
+    each(n - 1, step)
+    scatter.arrive()
+
+    def settle(part):
+        total = stream[part, :].astype(f32) + scatter.result(part)
+        hidden[part, :] = total
+        _, unit = rms_parts(total)
+        low_out[part, :] = (unit * preffn[...]).astype(bf16)
+
+    strips(local, settle)
+    scatter.finish()
     gather.finish()
+    cots.finish()
+    mine.wait()
+    keep_gated.wait()
+    for copy in out_copies:
+        copy.wait()
     keep(normed, j).wait()
+    keep_pre(j).wait()
     for k in range(1, n):
         other = lax.rem(j + k, n)
         keep(rows.at[other], other).wait()
-
-
-def project(stream, gain, wbi):
+        keep_pre(other).wait()
+    for i in range(max(count - 2, 0), count):
+        keep_stage(i).wait()
+
+
+def mixer_front(lengths, stream, premix, wb, wi, wo, wg, par, preffn, cot):
     n = lax.axis_size("head")
     local, depth = stream.shape
+    width, tokens = wg.shape[0], n * local
+    f32, bf16 = jnp.float32, jnp.bfloat16
+    shape, vmem, dma = jax.ShapeDtypeStruct, pltpu.VMEM, pltpu.SemaphoreType.DMA
     return line_call(
-        project_kernel, 0, "gather_project",
+        front_kernel, 0, "mixer_front",
         (
-            jax.ShapeDtypeStruct((n, local, depth), jnp.bfloat16),
-            jax.ShapeDtypeStruct((n * local, wbi.shape[0]), jnp.float32),
+            shape((n, local, depth), bf16),
+            shape((tokens, 2 * width), f32),
+            shape((tokens, SAVED * width), f32),
+            shape((tokens, width), bf16),
+            shape((2 * width, depth), bf16),
+            shape((width, depth), bf16),
+            shape((n, local, depth), bf16),
+            shape((local, depth), f32),
+            shape((local, depth), bf16),
         ),
-        [IN_VMEM] * 3,
-        [IN_ANY, IN_VMEM],
+        [IN_SMEM] + [IN_VMEM] * 9,
+        [IN_ANY] * 7 + [IN_VMEM] * 2,
         [
-            pltpu.VMEM((local, depth), jnp.bfloat16),
-            pltpu.VMEM((n, local, depth), jnp.bfloat16),
+            vmem((local, depth), bf16),
+            vmem((n, local, depth), bf16),
+            vmem((2 * width, depth), bf16),
+            vmem((width, depth), bf16),
+            vmem((HALO + tokens, 2 * width), f32),
+            vmem((tokens, width), bf16),
+            vmem((2, CHUNK, SAVED * width), f32),
+            vmem((CHUNK, 2 * width), f32),
+            vmem((8, width), f32),
+            vmem((3, local, depth), bf16),
+            vmem((n + 1, local, depth), bf16),
             *gather_sems(n),
-            pltpu.SemaphoreType.DMA((n,)),
+            *gather_sems(n),
+            *scatter_sems(n),
+            dma((n,)),
+            dma((n,)),
+            dma((2,)),
+            dma((4,)),
         ],
-    )(stream, gain, wbi)
-
-
-def mixer_out_kernel(
-    gated, wo, stream, gain, cot, cot_rows, hidden, low_out, own, held,
-    send, recv, gsend, grecv, sem,
-):
-    j, n = line_place()
-    line_barrier(j, n)
-    local = stream.shape[0]
-    gather = Gather(j, n, cot_rows, gsend, grecv)
-    scatter = Scatter(j, n, own, held, send, recv)
-
-    def compute(block):
-        part = pl.ds(pl.multiple_of(block * local, local), local)
-        own[block] = jnp.dot(
-            gated[part, :], wo[...], preferred_element_type=jnp.float32
-        ).astype(jnp.bfloat16)
-
-    def ahead(t):
-        for _, block, live in scatter.flows(t):
-            pl.when(live)(lambda: compute(block))
-
-    ahead(0)
-    mine = pltpu.make_async_copy(cot, cot_rows.at[j], sem)
-    mine.start()
-
-    def step(t):
-        scatter.step(t)
-
-        @pl.when(t == 0)
-        def _():
-            gather.start(cot)
-
-        ahead(t + 1)
-
-        @pl.when(t == 0)
-        def _():
-            compute(j)
-
-        @pl.when(t > 0)
-        def _():
-            gather.step(t)
-
-    each(n - 1, step)
-    scatter.arrive()
-
-    def settle(part):
-        total = stream[part, :].astype(jnp.float32) + scatter.result(part)
-        hidden[part, :] = total
-        _, unit = rms_parts(total)
-        low_out[part, :] = (unit * gain[...]).astype(jnp.bfloat16)
-
-    strips(local, settle)
-    gather.step(n - 1)
-    scatter.finish()
-    gather.finish()
-    mine.wait()
-
-
-def mixer_out(gated, wo, stream, gain, cot):
-    n = lax.axis_size("head")
-    local, depth = stream.shape
-    return line_call(
-        mixer_out_kernel, 1, "mixer_out",
-        (
-            jax.ShapeDtypeStruct((n, local, depth), jnp.bfloat16),
-            jax.ShapeDtypeStruct((local, depth), jnp.float32),
-            jax.ShapeDtypeStruct((local, depth), jnp.bfloat16),
-        ),
-        [IN_VMEM] * 5,
-        [IN_ANY, IN_VMEM, IN_VMEM],
-        [
-            pltpu.VMEM((n, local, depth), jnp.bfloat16),
-            pltpu.VMEM((n + 1, local, depth), jnp.bfloat16),
-            *scatter_sems(n),
-            *gather_sems(n),
-            pltpu.SemaphoreType.DMA,
-        ],
-    )(gated, wo, stream, gain, cot)
+    )(lengths, stream, premix, wb, wi, wo, wg, par, preffn, cot)
 
 
 def ffn_kernel(
     low, cot_rows, cot, hidden, gain, wg, wu, wd,
     out_part, terms, far_terms, resid, resid_low, gain_grad,
-    rows, cot_unit, kept, own, held, stage, wstage, cot_cols,
-    gsend, grecv, send, recv, cot_sem, out_sem, col_sem, term_sem, fsend, frecv,
+    rows, cot_pair, kept, own, held, stage, wstage, cot_cols,
+    gsend, grecv, send, recv, cot_sem, out_sem, col_sem, term_sem, far_sem,
 ):
     j, n = line_place()
     peer_barrier(("head", "dp"))
     f32, bf16 = jnp.float32, jnp.bfloat16
     local, depth = low.shape
     units = wg.shape[1]
+    half = local // PARTS
     fstep = 256 if units % 256 == 0 else LANES
     dstep = 512
     gather = Gather(j, n, rows, gsend, grecv)
     scatter = Scatter(j, n, own, held, send, recv)
-    gather.start(low)
+    gather.start(low, [0])
     rows[j] = low[...]
 
-    def fetch(block):
-        return pltpu.make_async_copy(cot_rows.at[block], cot_unit, cot_sem)
-
-    def put(block):
-        return pltpu.make_async_copy(stage, out_part.at[block], out_sem)
-
-    def unit(block):
-        span = pl.ds(pl.multiple_of(block * local, local), local)
-        x = rows.at[block]
+    def pair(chip, q):
+        return pl.ds(pl.multiple_of(2 * chip, 2), 2), pl.ds(q * half, half)
+
+    def fetch(chip, q):
+        return pltpu.make_async_copy(cot_rows.at[pair(chip, q)], cot_pair, cot_sem)
+
+    def put(chip, q):
+        return pltpu.make_async_copy(stage, out_part.at[pair(chip, q)], out_sem)
+
+    def pair_work(chip, q):
+        spot = pair(chip, q)
+
+        def flat(v):
+            return v.reshape(2 * half, v.shape[-1])
+
+        def fold(v):
+            return v.astype(bf16).reshape(2, half, v.shape[-1])
+
         for f in range(0, units, fstep):
             cols = slice(f, f + fstep)
-            gate = jnp.dot(x[...], wg[:, cols], preferred_element_type=f32)
+            gate = jnp.dot(flat(rows[spot]), wg[:, cols], preferred_element_type=f32)
             act, slope = gelu_pair(gate)
-            up = jnp.dot(x[...], wu[:, cols], preferred_element_type=f32)
-            kept[2, span, cols] = (act * up).astype(bf16)
-            grad = jnp.dot(cot_unit[...], wd[:, cols], preferred_element_type=f32)
-            kept[0, span, cols] = (grad * up * slope).astype(bf16)
-            kept[1, span, cols] = (grad * act).astype(bf16)
+            up = jnp.dot(flat(rows[spot]), wu[:, cols], preferred_element_type=f32)
+            kept[2, *spot, cols] = fold(act * up)
+            grad = jnp.dot(flat(cot_pair[...]), wd[:, cols], preferred_element_type=f32)
+            kept[0, *spot, cols] = fold(grad * up * slope)
+            kept[1, *spot, cols] = fold(grad * act)
         for d in range(0, depth, dstep):
             cols = slice(d, d + dstep)
-            own[block, :, cols] = (
-                contract_cols(kept[0, span, :], wg[cols, :])
-                + contract_cols(kept[1, span, :], wu[cols, :])
-            ).astype(bf16)
-            stage[:, cols] = contract_cols(kept[2, span, :], wd[cols, :]).astype(bf16)
-
-    def visit(v):
-        t = (v + 1) // 2
-        block = jnp.where(v % 2 == 1, j - t, j + t)
-        live = (block >= 0) & (block < n)
-
-        @pl.when(live)
-        def _():
-            fetch(block).start()
-
-        @pl.when(v % 2 == 1)
-        def _():
-            gather.step(t)
-
-        @pl.when(live)
-        def _():
-            fetch(block).wait()
-
-            @pl.when(v > 0)
+            own[*spot, cols] = fold(
+                contract_cols(flat(kept[0, *spot]), wg[cols, :])
+                + contract_cols(flat(kept[1, *spot]), wu[cols, :])
+            )
+            stage[:, :, cols] = fold(contract_cols(flat(kept[2, *spot]), wd[cols, :]))
+
+    def gather_half(q):
+        def visit(i):
+            t = i + 1
+            reach = t // 2
+            chip = j // 2 + jnp.where((t + j) % 2 == 0, -reach, reach)
+            live = (chip >= 0) & (chip < n // 2)
+
+            @pl.when(live)
             def _():
-                put(block).wait()
-
-            unit(block)
-            put(block).start()
-
-    each(2 * n - 1, visit)
-    put(j).wait()
+                fetch(chip, q).start()
+
+            gather.step(t, [q])
+            if q:
+                scatter.step(t - 1, [0])
+
+            @pl.when(live)
+            def _():
+                fetch(chip, q).wait()
+
+                @pl.when((t > 1) | (q > 0))
+                def _():
+                    put(chip, q).wait()
+
+                pair_work(chip, q)
+                put(chip, q).start()
+
+        each(n - 1, visit)
+
+    gather_half(0)
+    gather.start(low, [1])
+    gather_half(1)
+    put(j // 2, 1).wait()
 
     width = depth // n
     per = depth // terms.shape[0] // width
@@ -749,19 +809,8 @@
         spot = pl.ds(pl.multiple_of(lax.rem(b, per) * width, width), width)
         return pltpu.make_async_copy(wstage, terms.at[owner, :, spot, :], term_sem)
 
-    def send_far():
-        return pltpu.make_async_remote_copy(
-            src_ref=terms.at[far],
-            dst_ref=far_terms,
-            send_sem=fsend,
-            recv_sem=frecv,
-            device_id={"dp": far},
-            device_id_type=pl.DeviceIdType.MESH,
-        )
-
     def weights(b):
-        cols = columns(b)
-        xs = rows[:, :, cols].reshape(n * local, width)
+        xs = rows[:, :, columns(b)].reshape(n * local, width)
         take(b).wait()
 
         @pl.when(b > 0)
@@ -770,13 +819,11 @@
 
         @pl.when(b == per)
         def _():
-            send_far().start()
-
-        wstage[0] = contract_rows(xs, kept[0]).astype(bf16)
-        wstage[1] = contract_rows(xs, kept[1]).astype(bf16)
-        wstage[2] = contract_rows(
-            cot_cols[...].reshape(n * local, width), kept[2]
-        ).astype(bf16)
+            for copy in far_copies(terms, far_terms, far_sem):
+                copy.start()
+
+        for k, lead in ((0, xs), (1, xs), (2, cot_cols[...].reshape(n * local, width))):
+            wstage[k] = contract_rows(lead, kept[k].reshape(n * local, units)).astype(bf16)
         give(b).start()
 
         @pl.when(b + 1 < n)
@@ -786,7 +833,7 @@
     take(0).start()
 
     def step(t):
-        pl.when(t < n - 1)(lambda: scatter.step(t))
+        pl.when(t < n - 1)(lambda: scatter.step(t, [1]))
         weights(t)
 
     each(n, step)
@@ -805,7 +852,8 @@
     give(0).wait()
     gather.finish()
     scatter.finish()
-    send_far().wait()
+    for copy in far_copies(terms, far_terms, far_sem):
+        copy.wait()
 
 
 def feed_forward(low, cot_rows, cot, hidden, gain, wg, wu, wd):
@@ -813,30 +861,33 @@
     local, depth = low.shape
     units = wg.shape[1]
     bf16 = jnp.bfloat16
+    shape, vmem = jax.ShapeDtypeStruct, pltpu.VMEM
+    pair = (2, local // PARTS, depth)
     return line_call(
         ffn_kernel, 2, "feed_forward",
         (
-            jax.ShapeDtypeStruct((n, local, depth), bf16),
-            jax.ShapeDtypeStruct((group, 3, depth // group, units), bf16),
-            jax.ShapeDtypeStruct((3, depth // group, units), bf16),
-            jax.ShapeDtypeStruct((local, depth), jnp.float32),
-            jax.ShapeDtypeStruct((local, depth), bf16),
-            jax.ShapeDtypeStruct((1, depth), jnp.float32),
+            shape((n, local, depth), bf16),
+            shape((group, 3, depth // group, units), bf16),
+            shape((FAR_TERMS, depth // group, units), bf16),
+            shape((local, depth), jnp.float32),
+            shape((local, depth), bf16),
+            shape((1, depth), jnp.float32),
         ),
         [IN_VMEM, IN_ANY] + [IN_VMEM] * 6,
         [IN_ANY, IN_ANY, IN_ANY, IN_VMEM, IN_VMEM, IN_VMEM],
         [
-            pltpu.VMEM((n, local, depth), bf16),
-            pltpu.VMEM((local, depth), bf16),
-            pltpu.VMEM((3, n * local, units), bf16),
-            pltpu.VMEM((n, local, depth), bf16),
-            pltpu.VMEM((n + 1, local, depth), bf16),
-            pltpu.VMEM((local, depth), bf16),
-            pltpu.VMEM((3, depth // n, units), bf16),
-            pltpu.VMEM((n, local, depth // n), bf16),
+            vmem((n, local, depth), bf16),
+            vmem(pair, bf16),
+            vmem((3, n, local, units), bf16),
+            vmem((n, local, depth), bf16),
+            vmem((n + 1, local, depth), bf16),
+            vmem(pair, bf16),
+            vmem((3, depth // n, units), bf16),
+            vmem((n, local, depth // n), bf16),
             *gather_sems(n),
             *scatter_sems(n),
-            *[pltpu.SemaphoreType.DMA] * 6,
+            *[pltpu.SemaphoreType.DMA] * 4,
+            pltpu.SemaphoreType.DMA((2, FAR_TERMS)),
         ],
     )(low, cot_rows, cot, hidden, gain, wg, wu, wd)
 
@@ -844,11 +895,11 @@
 def back_kernel(
     lengths, low, out_part, hidden, terms, gated, wo, wbi, wg, par, pre, saved,
     normed_rows, stream, gain, resid, preffn_grad,
-    layer_out, sums, stream_grad, ob_total, i_total, g_total, par_grad, gains,
+    layer_out, sums, last_terms, stream_grad, ob_total, i_total, g_total, par_grad, gains,
     rows, own, held, dh, dpre, acc, dgate, dz, du, carry, dpar, wide,
     unit_bp, unit_h, unit_gated, unit_normed,
     obterms, obslots, iterms, islots, gterms, gslots, pslots, dslots, hslots,
-    gsend, grecv, send4, recv4, send8, recv8, tsend, trecv, unit_sem, own_sem, chunk_sem,
+    gsend, grecv, send4, recv4, send8, recv8, tsems, unit_sem, own_sem, chunk_sem,
     row_sem, wide_sem, free, psend, precv, dsend, drecv, hsend, hrecv, *sems,
 ):
     j, n = line_place()
@@ -857,21 +908,9 @@
     width = dh.shape[1]
     tiles = width // LANES
     peer_barrier(("head", "dp"))
-
-    def near():
-        for k, peer, slot in near_peers("dp"):
-            yield pltpu.make_async_remote_copy(
-                src_ref=terms.at[peer],
-                dst_ref=sums.at[slot],
-                send_sem=tsend.at[k],
-                recv_sem=trecv.at[slot],
-                device_id={"dp": peer},
-                device_id_type=pl.DeviceIdType.MESH,
-            )
-
     gather = Gather(j, n, rows, gsend, grecv)
     gather.start(low)
-    for copy in near():
+    for copy in near_copies(terms, sums, last_terms, tsems):
         copy.start()
     rows[j] = low[...]
     outs = Scatter(j, n, own, held, send4, recv4)
@@ -1187,10 +1226,9 @@
     for one in (gsum, obsum, isum):
         one.finish()
     scatter.finish()
-    for copy in near():
+    for copy in near_copies(terms, sums, last_terms, tsems):
         copy.wait_send()
-    for k in range(sums.shape[0]):
-        pltpu.make_async_copy(sums.at[k], sums.at[k], trecv.at[k]).wait()
+    near_arrive(sums, last_terms, tsems)
 
 
 def mixer_back(
@@ -1211,6 +1249,7 @@
         (
             shape((local, depth), bf16),
             shape((group - 2, *terms.shape[1:]), bf16),
+            shape(terms.shape[2:], bf16),
             shape((local, depth), bf16),
             shape(ob, bf16),
             shape(one, bf16),
@@ -1222,7 +1261,7 @@
             IN_SMEM, IN_VMEM, IN_ANY, IN_ANY, IN_ANY, IN_ANY, *[IN_VMEM] * 4, IN_ANY, IN_ANY,
             IN_ANY, IN_VMEM, IN_VMEM, IN_ANY, IN_VMEM,
         ],
-        [IN_VMEM, IN_ANY, IN_VMEM, IN_ANY, IN_ANY, IN_ANY, IN_VMEM, IN_VMEM],
+        [IN_VMEM, IN_ANY, IN_ANY, IN_VMEM, IN_ANY, IN_ANY, IN_ANY, IN_VMEM, IN_VMEM],
         [
             pltpu.VMEM((n, local, depth), bf16),
             pltpu.VMEM((3, local, depth), bf16),
@@ -1252,8 +1291,7 @@
             *gather_sems(n),
             *scatter_sems(n),
             *scatter_sems(n),
-            dma((group,)),
-            dma((group,)),
+            dma((2, group)),
             dma((4,)),
             dma((3,)),
             dma((2, 4)),
@@ -1273,10 +1311,6 @@
     )
 
 
-def widen(values, width):
-    return jnp.pad(values, ((0, width - values.shape[0]), (0, 0)))
-
-
 def block_diagonal(weights, width):
     heads, size = weights.shape[0], weights.shape[1]
     placed = [
@@ -1286,9 +1320,8 @@
 
 
 def diagonal_blocks(dense, heads, size):
-    return jnp.stack(
-        [dense[i * size : (i + 1) * size, i * size : (i + 1) * size] for i in range(heads)]
-    )
+    blocks = [dense[i * size : (i + 1) * size, i * size : (i + 1) * size] for i in range(heads)]
+    return jnp.stack(blocks, axis=1).transpose(1, 0, 2)
 
 
 def shards(
@@ -1316,27 +1349,35 @@
     wg = jnp.concatenate(
         [block_diagonal(rate_weight, width), block_diagonal(entry_weight, width)], axis=1
     )
-    wbi = jnp.concatenate([widen(branch_weight.T, width), widen(input_weight.T, width)])
-    wo = widen(output_weight, width)
 
     premix = premix_gain.astype(f32)[None]
     preffn = preffn_gain.astype(f32)[None]
-    normed_rows, pre = project(stream, premix, wbi)
-    saved, gated = rec_fwd(doc_lengths, pre, wg, par)
-    cot_rows, hidden_in, ffn_low = mixer_out(gated, wo, stream, preffn, cotangent)
+    normed_rows, pre, saved, gated, wbi, wo, cot_rows, hidden_in, ffn_low = mixer_front(
+        doc_lengths, stream, premix, branch_weight.T, input_weight.T, output_weight, wg, par,
+        preffn, cotangent,
+    )
 
     out_part, terms, far_terms, resid_grad, resid_low, preffn_grad = feed_forward(
         ffn_low, cot_rows, cotangent, hidden_in, preffn, ffn_gate, ffn_upward, ffn_down
     )
 
-    layer_out, sums, stream_grad, ob_grad, input_grad, gate_grad, dpar, gains = mixer_back(
+    layer_out, sums, last_terms, stream_grad, ob_grad, input_grad, gate_grad, dpar, gains = mixer_back(
         doc_lengths, resid_low, out_part, hidden_in, terms, gated, wo, wbi, wg, par, pre, saved,
         normed_rows, stream, premix, resid_grad, preffn_grad,
     )
     mine = lax.dynamic_index_in_dim(terms, lax.axis_index("dp"), keepdims=False)
-    ffn_sums = mine.astype(f32) + far_terms.astype(f32) + jnp.sum(sums.astype(f32), axis=0)
-    ob_grad = ob_grad.reshape(2 * width, -1).astype(f32)
-    input_grad = input_grad.reshape(width, -1).astype(f32)
+    far = [far_terms[0], far_terms[1], last_terms]
+    ffn_sums = [
+        sum(
+            (sums[i, k].astype(f32) for i in range(sums.shape[0])),
+            mine[k].astype(f32) + far[k].astype(f32),
+        )
+        for k in range(3)
+    ]
+    ob_grad = ob_grad.reshape(2 * width, -1)
+    output_grad = ob_grad[:chans].astype(f32)
+    branch_grad = ob_grad[width : width + chans].astype(f32).T
+    input_grad = input_grad.reshape(width, -1)[:chans].astype(f32).T
     gate_grad = gate_grad.reshape(width, -1).astype(f32)
     dpar = dpar[:, :chans]
     decay_grad = dpar[G_DECAY] * (-DECAY_SCALE * jax.nn.sigmoid(decay_param.astype(f32)))
@@ -1344,8 +1385,8 @@
         layer_out,
         stream_grad,
         gains[0],
-        ob_grad[width : width + chans].T,
-        input_grad[:chans].T,
+        branch_grad,
+        input_grad,
         dpar[G_TAP : G_TAP + CONVW],
         dpar[G_BIAS],
         diagonal_blocks(gate_grad[:, :width], heads, size),
@@ -1353,7 +1394,7 @@
         diagonal_blocks(gate_grad[:, width:], heads, size),
         dpar[G_ENTRY].reshape(heads, size),
         decay_grad,
-        ob_grad[:chans],
+        output_grad,
         gains[1],
         ffn_sums[0],
         ffn_sums[1],

time: 643 us -> 576 us (0.90)
  Pallas kernels: 602 us -> 548 us
  local copies, waits for them, and re-layouts: 21.7 us -> 9.43 us
    pallas_call x4 -> x2, Pallas kernels: 375 us -> 329 us  [the longest x1 165 us: feed_forward(): line_call(ffn_kernel, 2, 'feed_forward', (shape((n, local, depth), bf16),...]
    pallas_call x1, Pallas kernels: 227 us -> 219 us  [mixer_back(): line_call(back_kernel, 3, 'mixer_back', (shape((local, depth), bf16), sha...]
where the time goes in v4:
time: 576 us; the launch traced here: 575 us
  Pallas kernels  548 us (95%)
  other arithmetic  16 us (3%)
  local copies, waits for them, and re-layouts  9.43 us (2%)
    pallas_call x1, Pallas kernels, mixer_back(): line_call(back_kernel, 3, 'mixer_back', (shape((local, depth), bf16), sha...  219 us
    pallas_call x1, Pallas kernels, feed_forward(): line_call(ffn_kernel, 2, 'feed_forward', (shape((n, local, depth), bf16),...  165 us
    pallas_call x1, Pallas kernels, mixer_front(): line_call(front_kernel, 0, 'mixer_front', (shape((n, local, depth), bf16)...  164 us

profile of v4, /device:TPU:0, one launch (start us, length us, event | category | flops | bytes accessed | tf_op | source)
XLA Modules:
  0.0 574.8 jit_solution(9990679743496664074)
XLA Ops:
  0.7 0.0 copy-start.5
  0.7 1.4 fusion.10
  2.0 0.0 copy-start.10
  2.1 0.0 copy-start.12
  2.1 0.0 copy-start.13
  2.1 0.0 copy-start.14
  2.1 0.0 copy-start.11
  2.1 0.1 pad_add_fusion.1
  2.2 0.0 copy-done.5
  2.2 0.0 copy-start.8
  2.2 0.0 copy-start.9
  2.3 0.2 fusion.11
  2.5 0.1 pad_add_fusion
  2.6 0.9 pad_maximum_fusion.wg
  3.5 0.0 copy-done.10
  3.5 0.0 copy-done.12
  3.6 0.0 copy-done.13
  3.6 0.1 reshape.117
  3.7 0.0 copy-done.14
  3.7 0.1 reshape.118
  3.7 0.0 copy-done.11
  3.8 0.7 pad_select_fusion.par
  4.5 0.0 copy-done.8
  4.5 0.6 broadcast_in_dim.26
  5.1 0.0 copy-done.9
  5.1 0.6 broadcast_in_dim.27
  5.7 164.2 %mixer_front.1 = (bf16[8,256,2048]{2,1,0:T(8,128)(2,1)}, f32[2048,768]{1,0:T(8,128)}, f32[2048,1536]{1,0:T(8,128)}, bf16[2048,384]{1,0:T(8,128)(2,1)}, bf16[768,...) custom-call(s32[1,8]{1,0:T(1,128)} %lengths.3, ...), custom_call_target="tpu_custom_call" | custom-call | tf_op jit(solution)/shard_map/mixer_front/pallas_call | solution.py:671
  169.9 165.1 %feed_forward.1 = (bf16[8,256,2048]{2,1,0:T(8,128)(2,1)}, bf16[4,3,512,768]{3,2,1,0:T(8,128)(2,1)}, bf16[2,512,768]{2,1,0:T(8,128)(2,1)}, f32[256,2048]{1,0:T(8,...) custom-call(bf16[256,2048]{1,0:T(8,128)(2,1)} %get-tuple-element.41.low, ...), custom_call_target="tpu_custom_call" | custom-call | tf_op jit(solution)/shard_map/feed_forward/pallas_call | solution.py:866
  335.0 0.0 copy-start.1
  335.0 219.2 %mixer_back.1 = (bf16[256,2048]{1,0:T(8,128)(2,1)}, bf16[2,3,512,768]{3,2,1,0:T(8,128)(2,1)}, bf16[512,768]{1,0:T(8,128)(2,1)}, bf16[256,2048]{1,0:T(8,128)(2,1)...) custom-call(s32[1,8]{1,0:T(1,128)} %lengths.3, ...), custom_call_target="tpu_custom_call" | custom-call | tf_op jit(solution)/shard_map/mixer_back/pallas_call | solution.py:1247
  554.2 0.0 copy-done.1
  554.2 0.0 copy-start.6
  554.2 6.0 %convert_add_fusion.3 = (f32[512,768]{1,0:T(8,128)}, f32[512,768]{1,0:T(8,128)}, f32[512,768]{1,0:T(8,128)}) fusion(bf16[4,3,512,768]{3,2,1,0:T(8,128)(2,1)} %get-tuple-element.46.terms, s32[]{:T(128)S(6)} %select_n.14, s32[]{:T(128)S(6)} %add.72, bf16[2,3,512,768]{3,2,1,0:T(8,128)(2,1)} %get-tuple-element.63, bf16[2,512,768]{2,1,0:T(8,128)(2,1)S(1)} %copy-done.1, ...), kind=kLoop, calls=%fused_computation.5 | loop fusion | flops 8257536 | bytes 14155788 | tf_op jit(solution)/shard_map/add | solution.py:1371
  560.2 0.0 copy-done.6
  560.2 0.1 bitcast_convert_fusion
  560.4 0.0 copy-start
  560.4 0.2 slice_bitcast_fusion
  560.5 0.2 copy.39
  560.7 0.1 stack.22
  560.8 1.1 maximum_bitcast_fusion.1
  562.0 1.0 copy.40
  563.0 0.0 copy-done
  563.0 0.0 copy-start.2
  563.0 3.2 slice_convert_fusion
  566.2 0.0 copy-done.2
  566.2 0.0 copy-start.7
  566.2 0.0 copy-start.4
  566.2 1.9 convert_bitcast_fusion
  568.1 0.0 copy-start.3
  568.1 1.6 fusion.12
  569.7 0.0 copy-done.7
  569.7 0.6 slice_reduce_fusion
  570.3 0.6 fusion.4
  570.9 0.7 reshape_squeeze.6
  571.6 0.7 reshape_squeeze.7
  572.2 0.6 slice.109
  572.8 0.0 copy-done.4
  572.8 1.0 copy.51
  573.8 0.0 copy-done.3
  573.8 1.0 copy.52
  (9 shorter events, 0.1 us)
Async XLA Ops:
  0.7 1.6 copy-start.5
  2.0 1.5 copy-start.10
  2.1 1.5 copy-start.12
  2.1 1.5 copy-start.13
  2.1 1.6 copy-start.14
  2.1 1.6 copy-start.11
  2.2 2.2 copy-start.8
  2.2 2.8 copy-start.9
  335.0 219.2 %copy-start.1 = (bf16[2,512,768]{2,1,0:T(8,128)(2,1)S(1)}, bf16[2,512,768]{2,1,0:T(8,128)(2,1)}, u32[]{:S(2)}) copy-start(bf16[2,512,768]{2,1,0:T(8,128)(2,1)} %get-tuple-element.62) | copy-start | bytes 4718596
  554.2 6.0 %copy-start.6 = (bf16[4,96,768]{2,1,0:T(8,128)(2,1)S(1)}, bf16[4,96,768]{2,1,0:T(8,128)(2,1)}, u32[]{:S(2)}) copy-start(bf16[4,96,768]{2,1,0:T(8,128)(2,1)} %get-tuple-element.61) | copy-start | bytes 1769476
  560.4 2.6 copy-start
  563.0 3.2 copy-start.2
  566.2 3.5 copy-start.7
  566.2 6.6 %copy-start.4 = (bf16[256,2048]{1,0:T(8,128)(2,1)S(1)}, bf16[256,2048]{1,0:T(8,128)(2,1)}, u32[]{:S(2)}) copy-start(bf16[256,2048]{1,0:T(8,128)(2,1)} %get-tuple-element.122) | copy-start | bytes 3145732
  568.1 5.7 copy-start.3

commit v5 on v4

--- a/solution.py
+++ b/solution.py
@@ -15,7 +15,8 @@
 LANES = 128
 HALO = 8
 PARTS = 2
-LAG = 1
+LAG = 2
+OUT_AT = 2
 FAR_TERMS = 2
 VMEM_BYTES = 62 * 2**20
 IN_VMEM = pl.BlockSpec(memory_space=pltpu.VMEM)
@@ -242,9 +243,9 @@
                 def _():
                     self.copy(block, s, side).start()
 
-    def finish(self):
+    def finish(self, parts=range(PARTS)):
         def drain(t):
-            for s in range(PARTS):
+            for s in parts:
                 for side, block, live in self.flows(t):
 
                     @pl.when(live & self.there(side))
@@ -255,16 +256,18 @@
 
 
 class Scatter:
-    def __init__(self, j, n, own, held, send, recv):
+    def __init__(self, j, n, own, held, send, recv, last=2):
         self.j, self.n, self.own, self.held, self.send, self.recv = j, n, own, held, send, recv
         self.span = own.shape[1] // PARTS
+        self.ends = (j, n)
+        self.spot = last
         self.compact = own.shape[0] != n
 
     def place(self, block, side):
         return block if not self.compact else (1 - side) // 2
 
     def last(self):
-        return self.j if not self.compact else 2
+        return self.j if not self.compact else self.spot
 
     def rows(self, s):
         return pl.ds(s * self.span, self.span)
@@ -325,21 +328,21 @@
 
         each(self.span // STRIP, add_rows)
 
-    def arrive(self):
-        for s in range(PARTS):
+    def arrive(self, parts=range(PARTS)):
+        for s in parts:
 
             @pl.when(self.j > 0)
             def _():
-                self.arrival(self.j, s).wait()
+                self.arrival(self.ends[0], s).wait()
 
             @pl.when(self.j < self.n - 1)
             def _():
-                self.arrival(self.n, s).wait()
+                self.arrival(self.ends[1], s).wait()
 
     def result(self, rows):
         total = self.own[self.last(), rows, :].astype(jnp.float32)
-        left = self.held[self.j, rows, :].astype(jnp.float32)
-        right = self.held[self.n, rows, :].astype(jnp.float32)
+        left = self.held[self.ends[0], rows, :].astype(jnp.float32)
+        right = self.held[self.ends[1], rows, :].astype(jnp.float32)
         total = total + jnp.where(self.j > 0, left, 0.0)
         return total + jnp.where(self.j < self.n - 1, right, 0.0)
 
@@ -455,21 +458,27 @@
 STRIP = 16
 
 
-def strips(rows, body):
-    each(rows // STRIP, lambda i: body(pl.ds(pl.multiple_of(i * STRIP, STRIP), STRIP)))
+def strips(rows, body, first=0):
+    each(rows // STRIP, lambda i: body(pl.ds(pl.multiple_of(first + i * STRIP, STRIP), STRIP)))
 
 
 def front_kernel(
     lengths, stream, premix, wb, wi, wo_in, wg, par, preffn, cot,
     rows_out, pre_out, saved, gated_out, wbi_out, wo_out, cot_rows, hidden, low_out,
-    normed, rows, wbi, wo, pre, gated, stage, z, carry, own, held,
-    gsend, grecv, csend, crecv, send, recv, keep_sem, pre_sem, stage_sem, one_sem,
+    normed, rows, wbi, wo, pre, gated, stage, z, carry, own, held, raw,
+    gsend, grecv, csend, crecv, send, recv, keep_sem, pre_sem, stage_sem, one_sem, raw_sem,
 ):
     j, n = line_place()
     f32, bf16 = jnp.float32, jnp.bfloat16
     local, depth = stream.shape
     width, chans = gated.shape[1], wb.shape[0]
     tiles = width // LANES
+    loads = [
+        pltpu.make_async_copy(source, raw.at[k], raw_sem.at[k])
+        for k, source in enumerate((wb, wi, wo_in))
+    ]
+    for load in loads:
+        load.start()
     line_barrier(j, n)
 
     def norm(part):
@@ -479,10 +488,11 @@
     strips(local, norm)
     gather = Gather(j, n, rows, gsend, grecv)
     gather.start(normed)
-    for target, first, source in ((wbi, 0, wb), (wbi, width, wi), (wo, 0, wo_in)):
+    for k, (target, first) in enumerate(((wbi, 0), (wbi, width), (wo, 0))):
+        loads[k].wait()
         whole = chans // STRIP * STRIP
         target[first + whole : first + width, :] = jnp.zeros((width - whole, depth), bf16)
-        target[first : first + chans, :] = source[...]
+        target[first : first + chans, :] = raw[k]
     out_copies = [
         pltpu.make_async_copy(wbi, wbi_out, one_sem.at[0]),
         pltpu.make_async_copy(wo, wo_out, one_sem.at[1]),
@@ -681,7 +691,7 @@
             shape((local, depth), f32),
             shape((local, depth), bf16),
         ),
-        [IN_SMEM] + [IN_VMEM] * 9,
+        [IN_SMEM, IN_VMEM, IN_VMEM, IN_ANY, IN_ANY, IN_ANY, *[IN_VMEM] * 4],
         [IN_ANY] * 7 + [IN_VMEM] * 2,
         [
             vmem((local, depth), bf16),
@@ -695,6 +705,7 @@
             vmem((8, width), f32),
             vmem((3, local, depth), bf16),
             vmem((n + 1, local, depth), bf16),
+            vmem((3, wb.shape[0], depth), bf16),
             *gather_sems(n),
             *gather_sems(n),
             *scatter_sems(n),
@@ -702,15 +713,16 @@
             dma((n,)),
             dma((2,)),
             dma((4,)),
+            dma((3,)),
         ],
     )(lengths, stream, premix, wb, wi, wo, wg, par, preffn, cot)
 
 
 def ffn_kernel(
-    low, cot_rows, cot, hidden, gain, wg, wu, wd,
+    low, cot_rows, cot_in, hidden_in, gain, wg_in, wu_in, wd_in,
     out_part, terms, far_terms, resid, resid_low, gain_grad,
-    rows, cot_pair, kept, own, held, stage, wstage, cot_cols,
-    gsend, grecv, send, recv, cot_sem, out_sem, col_sem, term_sem, far_sem,
+    rows, cot_pair, kept, own, held, stage, wstage, cot_cols, wg, wu, wd, cot, hidden,
+    gsend, grecv, send, recv, cot_sem, out_sem, col_sem, term_sem, far_sem, load_sem,
 ):
     j, n = line_place()
     peer_barrier(("head", "dp"))
@@ -723,7 +735,17 @@
     gather = Gather(j, n, rows, gsend, grecv)
     scatter = Scatter(j, n, own, held, send, recv)
     gather.start(low, [0])
+    loads = [
+        pltpu.make_async_copy(a, b, load_sem.at[k])
+        for k, (a, b) in enumerate(
+            ((wg_in, wg), (wu_in, wu), (wd_in, wd), (cot_in, cot), (hidden_in, hidden))
+        )
+    ]
+    for load in loads:
+        load.start()
     rows[j] = low[...]
+    for load in loads:
+        load.wait()
 
     def pair(chip, q):
         return pl.ds(pl.multiple_of(2 * chip, 2), 2), pl.ds(q * half, half)
@@ -873,7 +895,7 @@
             shape((local, depth), bf16),
             shape((1, depth), jnp.float32),
         ),
-        [IN_VMEM, IN_ANY] + [IN_VMEM] * 6,
+        [IN_VMEM, IN_ANY, IN_ANY, IN_ANY, IN_VMEM, IN_ANY, IN_ANY, IN_ANY],
         [IN_ANY, IN_ANY, IN_ANY, IN_VMEM, IN_VMEM, IN_VMEM],
         [
             vmem((n, local, depth), bf16),
@@ -884,29 +906,40 @@
             vmem(pair, bf16),
             vmem((3, depth // n, units), bf16),
             vmem((n, local, depth // n), bf16),
+            *[vmem(wg.shape, bf16)] * 3,
+            vmem((local, depth), bf16),
+            vmem((local, depth), jnp.float32),
             *gather_sems(n),
             *scatter_sems(n),
             *[pltpu.SemaphoreType.DMA] * 4,
             pltpu.SemaphoreType.DMA((2, FAR_TERMS)),
+            pltpu.SemaphoreType.DMA((5,)),
         ],
     )(low, cot_rows, cot, hidden, gain, wg, wu, wd)
 
 
 def back_kernel(
-    lengths, low, out_part, hidden, terms, gated, wo, wbi, wg, par, pre, saved,
-    normed_rows, stream, gain, resid, preffn_grad,
+    lengths, low, out_part, hidden, terms, gated, wo_in, wbi_in, wg, par, pre, saved,
+    normed_rows, stream_in, gain, resid, preffn_grad,
     layer_out, sums, last_terms, stream_grad, ob_total, i_total, g_total, par_grad, gains,
-    rows, own, held, dh, dpre, acc, dgate, dz, du, carry, dpar, wide,
+    rows, own, held, wo, wbi, dh, dpre, acc, dgate, dz, du, carry, dpar,
     unit_bp, unit_h, unit_gated, unit_normed,
     obterms, obslots, iterms, islots, gterms, gslots, pslots, dslots, hslots,
     gsend, grecv, send4, recv4, send8, recv8, tsems, unit_sem, own_sem, chunk_sem,
-    row_sem, wide_sem, free, psend, precv, dsend, drecv, hsend, hrecv, *sems,
+    row_sem, wide_sem, load_sem, free, psend, precv, dsend, drecv, hsend, hrecv, *sems,
 ):
     j, n = line_place()
     f32, bf16 = jnp.float32, jnp.bfloat16
-    local, depth = stream.shape
+    local, depth = low.shape
     width = dh.shape[1]
     tiles = width // LANES
+    stream, wide = unit_normed, acc.at[width : width + local]
+    loads = [
+        pltpu.make_async_copy(a, b, load_sem.at[k])
+        for k, (a, b) in enumerate(((wo_in, wo), (wbi_in, wbi), (stream_in, stream)))
+    ]
+    for load in loads[:2]:
+        load.start()
     peer_barrier(("head", "dp"))
     gather = Gather(j, n, rows, gsend, grecv)
     gather.start(low)
@@ -926,10 +959,15 @@
                 pl.when(live)(copy.start if start else copy.wait)
 
     def outs_step(t):
+        outs.step(t)
+        outs_ahead(t + 1)
+
+    def outs_slot(slot):
+        t = slot - 1 - LAG
+
         @pl.when((t >= 0) & (t < n - 1))
         def _():
-            outs.step(t)
-            outs_ahead(t + 1)
+            outs_step(t)
 
     outs_ahead(0)
     fetch_out(j, 2).start()
@@ -977,7 +1015,7 @@
         @pl.when(v % 2 == 1)
         def _():
             gather.step(t)
-            outs_step(t - 1 - LAG)
+            outs_slot(t)
 
         @pl.when(live)
         def _():
@@ -985,8 +1023,16 @@
                 copy.wait()
             unit(block)
 
+    loads[0].wait()
     each(2 * n - 1, visit)
     gather.finish()
+    for side in (-1, 1):
+
+        @pl.when((j + side >= 0) & (j + side < n))
+        def _():
+            pl.semaphore_signal(
+                free, inc=1, device_id={"head": j + side}, device_id_type=pl.DeviceIdType.MESH
+            )
 
     def pack(target, source, count):
         span = target.shape[1]
@@ -1004,10 +1050,7 @@
     gsum = Sum(gterms, gslots, g_total, sems[10:15])
     pack(obterms, acc, 2 * width)
     obsum.start()
-    load = pltpu.make_async_copy(normed_rows, rows, row_sem)
-    load.start()
-    load_hidden = pltpu.make_async_copy(hidden, wide, wide_sem.at[0])
-    load_hidden.start()
+    loads[2].start()
 
     count = n * local // CHUNK
 
@@ -1126,39 +1169,21 @@
                 dpre[spot, pl.ds(width + t * LANES, LANES)] = dx.astype(bf16)
 
         each(CHUNK // BLOCK, conv_step)
-        if LAG:
-            late = n - 1 - LAG
-
-            @pl.when((k % 2 == 1) & (k // 2 < LAG))
-            def _():
-                outs_step(late + k // 2)
+        pl.when(k % 2 == 0)(lambda: outs_slot(n + k // 2))
 
     each(count, chunk)
-
+    for t in range(n - 1 - max(0, LAG - (count + 1) // 2), n - 1):
+        outs_step(jnp.int32(t))
     pack(gterms, dgate, width)
     gsum.start()
     pshare = Share("dp", pslots, psend, precv)
     pslots[pshare.me] = dpar[...]
     pshare.start()
-    outs.arrive()
-    load_hidden.wait()
-
-    def settle_out(part):
-        layer_out[part, :] = (wide[part, :] + outs.result(part)).astype(bf16)
-
-    strips(local, settle_out)
-    outs.finish()
-    load_resid = pltpu.make_async_copy(resid, wide, wide_sem.at[1])
-    load_resid.start()
-    for side in (-1, 1):
-
-        @pl.when((j + side >= 0) & (j + side < n))
-        def _():
-            pl.semaphore_signal(
-                free, inc=1, device_id={"head": j + side}, device_id_type=pl.DeviceIdType.MESH
-            )
-
-    scatter = Scatter(j, n, own, held, send8, recv8)
+    load_hidden = pltpu.make_async_copy(hidden, wide, wide_sem.at[0])
+    load_hidden.start()
+    scatter = Scatter(j, n, own, rows, send8, recv8, last=3)
+    loads[1].wait()
+    loads[2].wait()
 
     def compute(block, slot):
         span = pl.ds(pl.multiple_of(block * local, local), local)
@@ -1172,26 +1197,45 @@
     wait_neighbours(free, j, n)
     scatter.step(0)
     ahead(1)
-    load.wait()
-    for c in range(0, width, LANES):
-        acc[c : c + LANES, :] = contract_rows(
-            dpre[:, width + c : width + c + LANES], rows[...].reshape(n * local, depth)
-        )
-    pack(iterms, acc, width)
-    isum.start()
-    compute(j, 2)
     obsum.spread()
+
+    def settle_out(part):
+        layer_out[part, :] = (wide[part, :] + outs.result(part)).astype(bf16)
+
+    load_resid = pltpu.make_async_copy(resid, wide, wide_sem.at[1])
 
     def step(t):
         scatter.step(t)
         ahead(t + 1)
 
-        @pl.when(t == n // 2)
+        @pl.when(t == OUT_AT)
+        def _():
+            outs.arrive()
+            load_hidden.wait()
+            strips(local, settle_out)
+            outs.finish()
+            load_resid.start()
+            load.start()
+            compute(j, 3)
+
+        @pl.when(t == OUT_AT + 1)
+        def _():
+            load.wait()
+            for c in range(0, width, LANES):
+                acc[c : c + LANES, :] = contract_rows(
+                    dpre[:, width + c : width + c + LANES],
+                    held[0:n].reshape(n * local, depth),
+                )
+            pack(iterms, acc, width)
+            isum.start()
+
+        @pl.when(t == OUT_AT + 2)
         def _():
             gsum.spread()
-            isum.spread()
-
+
+    load = pltpu.make_async_copy(normed_rows, held.at[pl.ds(0, n)], row_sem)
     lax.fori_loop(1, n - 1, lambda t, _: (step(t), 0)[1], 0)
+    isum.spread()
     scatter.arrive()
     load_resid.wait()
     gains[...] = jnp.zeros_like(gains)
@@ -1258,14 +1302,16 @@
             shape((8, depth), f32),
         ),
         [
-            IN_SMEM, IN_VMEM, IN_ANY, IN_ANY, IN_ANY, IN_ANY, *[IN_VMEM] * 4, IN_ANY, IN_ANY,
-            IN_ANY, IN_VMEM, IN_VMEM, IN_ANY, IN_VMEM,
+            IN_SMEM, IN_VMEM, *[IN_ANY] * 6, IN_VMEM, IN_VMEM, *[IN_ANY] * 4, IN_VMEM, IN_ANY,
+            IN_VMEM,
         ],
         [IN_VMEM, IN_ANY, IN_ANY, IN_VMEM, IN_ANY, IN_ANY, IN_ANY, IN_VMEM, IN_VMEM],
         [
-            pltpu.VMEM((n, local, depth), bf16),
-            pltpu.VMEM((3, local, depth), bf16),
             pltpu.VMEM((n + 1, local, depth), bf16),
+            pltpu.VMEM((4, local, depth), bf16),
+            pltpu.VMEM((n + 1, local, depth), bf16),
+            pltpu.VMEM(wo.shape, bf16),
+            pltpu.VMEM(wbi.shape, bf16),
             pltpu.VMEM((tokens, width), f32),
             pltpu.VMEM((tokens, 2 * width), bf16),
             pltpu.VMEM((max(2 * width, 2 * (CHUNK + HALO)), depth), f32),
@@ -1274,7 +1320,6 @@
             pltpu.VMEM((CHUNK + HALO, width), f32),
             pltpu.VMEM((8, width), f32),
             pltpu.VMEM((PARAMS, width), f32),
-            pltpu.VMEM((local, depth), f32),
             pltpu.VMEM((local, width), f32),
             pltpu.VMEM((local, width), f32),
             pltpu.VMEM((local, width), bf16),
@@ -1297,6 +1342,7 @@
             dma((2, 4)),
             dma,
             dma((2,)),
+            dma((3,)),
             pltpu.SemaphoreType.REGULAR,
             *share_sems("dp"),
             *share_sems("dp"),

time: 576 us -> 568 us (0.986)
  Pallas kernels: 548 us -> 539 us
where the time goes in v5:
time: 568 us; the launch traced here: 565 us
  Pallas kernels  539 us (95%)
  other arithmetic  16 us (3%)
  local copies, waits for them, and re-layouts  9.43 us (2%)
    pallas_call x1, Pallas kernels, mixer_back(): line_call(back_kernel, 3, 'mixer_back', (shape((local, depth), bf16), sha...  215 us
    pallas_call x1, Pallas kernels, mixer_front(): line_call(front_kernel, 0, 'mixer_front', (shape((n, local, depth), bf16)...  163 us
    pallas_call x1, Pallas kernels, feed_forward(): line_call(ffn_kernel, 2, 'feed_forward', (shape((n, local, depth), bf16),...  161 us

profile of v5, /device:TPU:0, one launch (start us, length us, event | category | flops | bytes accessed | tf_op | source)
XLA Modules:
  0.0 565.5 jit_solution(3921466297838913535)
XLA Ops:
  0.7 0.0 copy-start.5
  0.7 1.4 fusion.10
  2.0 0.0 copy-start.10
  2.1 0.0 copy-start.12
  2.1 0.0 copy-start.13
  2.1 0.0 copy-start.14
  2.1 0.0 copy-start.11
  2.1 0.1 pad_add_fusion.1
  2.2 0.0 copy-done.5
  2.2 0.0 copy-start.8
  2.2 0.0 copy-start.9
  2.3 0.2 fusion.11
  2.5 0.1 pad_add_fusion
  2.6 0.9 pad_maximum_fusion.wg
  3.5 0.0 copy-done.10
  3.5 0.0 copy-done.12
  3.6 0.0 copy-done.13
  3.6 0.1 reshape.117
  3.7 0.0 copy-done.14
  3.7 0.1 reshape.118
  3.7 0.0 copy-done.11
  3.8 0.7 pad_select_fusion.par
  4.5 0.0 copy-done.8
  4.5 0.6 broadcast_in_dim.26
  5.1 0.0 copy-done.9
  5.1 0.6 broadcast_in_dim.27
  5.7 163.0 %mixer_front.1 = (bf16[8,256,2048]{2,1,0:T(8,128)(2,1)}, f32[2048,768]{1,0:T(8,128)}, f32[2048,1536]{1,0:T(8,128)}, bf16[2048,384]{1,0:T(8,128)(2,1)}, bf16[768,...) custom-call(s32[1,8]{1,0:T(1,128)} %lengths.3, ...), custom_call_target="tpu_custom_call" | custom-call | tf_op jit(solution)/shard_map/mixer_front/pallas_call | solution.py:681
  168.7 161.3 %feed_forward.1 = (bf16[8,256,2048]{2,1,0:T(8,128)(2,1)}, bf16[4,3,512,768]{3,2,1,0:T(8,128)(2,1)}, bf16[2,512,768]{2,1,0:T(8,128)(2,1)}, f32[256,2048]{1,0:T(8,...) custom-call(bf16[256,2048]{1,0:T(8,128)(2,1)} %get-tuple-element.41.low, ...), custom_call_target="tpu_custom_call" | custom-call | tf_op jit(solution)/shard_map/feed_forward/pallas_call | solution.py:888
  330.0 0.0 copy-start.1
  330.0 214.9 %mixer_back.1 = (bf16[256,2048]{1,0:T(8,128)(2,1)}, bf16[2,3,512,768]{3,2,1,0:T(8,128)(2,1)}, bf16[512,768]{1,0:T(8,128)(2,1)}, bf16[256,2048]{1,0:T(8,128)(2,1)...) custom-call(s32[1,8]{1,0:T(1,128)} %lengths.3, ...), custom_call_target="tpu_custom_call" | custom-call | tf_op jit(solution)/shard_map/mixer_back/pallas_call | solution.py:1291
  544.9 0.0 copy-done.1
  544.9 0.0 copy-start.6
  544.9 6.0 %convert_add_fusion.3 = (f32[512,768]{1,0:T(8,128)}, f32[512,768]{1,0:T(8,128)}, f32[512,768]{1,0:T(8,128)}) fusion(bf16[4,3,512,768]{3,2,1,0:T(8,128)(2,1)} %get-tuple-element.46.terms, s32[]{:T(128)S(6)} %select_n.14, s32[]{:T(128)S(6)} %add.72, bf16[2,3,512,768]{3,2,1,0:T(8,128)(2,1)} %get-tuple-element.63, bf16[2,512,768]{2,1,0:T(8,128)(2,1)S(1)} %copy-done.1, ...), kind=kLoop, calls=%fused_computation.5 | loop fusion | flops 8257536 | bytes 14155788 | tf_op jit(solution)/shard_map/add | solution.py:1417
  550.9 0.0 copy-done.6
  550.9 0.1 bitcast_convert_fusion
  551.1 0.0 copy-start
  551.1 0.2 slice_bitcast_fusion
  551.2 0.2 copy.39
  551.4 0.1 stack.22
  551.5 1.1 maximum_bitcast_fusion.1
  552.7 1.0 copy.40
  553.7 0.0 copy-done
  553.7 0.0 copy-start.2
  553.7 3.2 slice_convert_fusion
  556.9 0.0 copy-done.2
  556.9 0.0 copy-start.7
  556.9 0.0 copy-start.4
  556.9 1.9 convert_bitcast_fusion
  558.8 0.0 copy-start.3
  558.8 1.6 fusion.12
  560.4 0.0 copy-done.7
  560.4 0.6 slice_reduce_fusion
  561.0 0.6 fusion.4
  561.6 0.7 reshape_squeeze.6
  562.3 0.7 reshape_squeeze.7
  562.9 0.6 slice.109
  563.5 0.0 copy-done.4
  563.5 1.0 copy.51
  564.5 0.0 copy-done.3
  564.5 1.0 copy.52
  (9 shorter events, 0.1 us)
Async XLA Ops:
  0.7 1.6 copy-start.5
  2.0 1.5 copy-start.10
  2.1 1.5 copy-start.12
  2.1 1.5 copy-start.13
  2.1 1.6 copy-start.14
  2.1 1.6 copy-start.11
  2.2 2.2 copy-start.8
  2.2 2.8 copy-start.9
  330.0 214.9 %copy-start.1 = (bf16[2,512,768]{2,1,0:T(8,128)(2,1)S(1)}, bf16[2,512,768]{2,1,0:T(8,128)(2,1)}, u32[]{:S(2)}) copy-start(bf16[2,512,768]{2,1,0:T(8,128)(2,1)} %get-tuple-element.62) | copy-start | bytes 4718596
  544.9 6.0 %copy-start.6 = (bf16[4,96,768]{2,1,0:T(8,128)(2,1)S(1)}, bf16[4,96,768]{2,1,0:T(8,128)(2,1)}, u32[]{:S(2)}) copy-start(bf16[4,96,768]{2,1,0:T(8,128)(2,1)} %get-tuple-element.61) | copy-start | bytes 1769476
  551.1 2.6 copy-start
  553.7 3.2 copy-start.2
  556.9 3.5 copy-start.7
  556.9 6.6 %copy-start.4 = (bf16[256,2048]{1,0:T(8,128)(2,1)S(1)}, bf16[256,2048]{1,0:T(8,128)(2,1)}, u32[]{:S(2)}) copy-start(bf16[256,2048]{1,0:T(8,128)(2,1)} %get-tuple-element.122) | copy-start | bytes 3145732
  558.8 5.7 %copy-start.3 = (bf16[256,2048]{1,0:T(8,128)(2,1)S(1)}, bf16[256,2048]{1,0:T(8,128)(2,1)}, u32[]{:S(2)}) copy-start(bf16[256,2048]{1,0:T(8,128)(2,1)} %get-tuple-element.123) | copy-start | bytes 3145732

commit v6 on v5

--- a/solution.py
+++ b/solution.py
@@ -14,7 +14,7 @@
 BLOCK = 64
 LANES = 128
 HALO = 8
-PARTS = 2
+PARTS = 4
 LAG = 2
 OUT_AT = 2
 FAR_TERMS = 2
@@ -101,6 +101,10 @@
         return 0
 
     lax.fori_loop(0, count, step, 0)
+
+
+def half_parts(q):
+    return range(q * PARTS // 2, (q + 1) * PARTS // 2)
 
 
 def line_place():
@@ -729,12 +733,12 @@
     f32, bf16 = jnp.float32, jnp.bfloat16
     local, depth = low.shape
     units = wg.shape[1]
-    half = local // PARTS
+    half = local // 2
     fstep = 256 if units % 256 == 0 else LANES
     dstep = 512
     gather = Gather(j, n, rows, gsend, grecv)
     scatter = Scatter(j, n, own, held, send, recv)
-    gather.start(low, [0])
+    gather.start(low, half_parts(0))
     loads = [
         pltpu.make_async_copy(a, b, load_sem.at[k])
         for k, (a, b) in enumerate(
@@ -793,9 +797,9 @@
             def _():
                 fetch(chip, q).start()
 
-            gather.step(t, [q])
+            gather.step(t, half_parts(q))
             if q:
-                scatter.step(t - 1, [0])
+                scatter.step(t - 1, half_parts(0))
 
             @pl.when(live)
             def _():
@@ -811,7 +815,7 @@
         each(n - 1, visit)
 
     gather_half(0)
-    gather.start(low, [1])
+    gather.start(low, half_parts(1))
     gather_half(1)
     put(j // 2, 1).wait()
 
@@ -855,7 +859,7 @@
     take(0).start()
 
     def step(t):
-        pl.when(t < n - 1)(lambda: scatter.step(t, [1]))
+        pl.when(t < n - 1)(lambda: scatter.step(t, half_parts(1)))
         weights(t)
 
     each(n, step)
@@ -884,7 +888,7 @@
     units = wg.shape[1]
     bf16 = jnp.bfloat16
     shape, vmem = jax.ShapeDtypeStruct, pltpu.VMEM
-    pair = (2, local // PARTS, depth)
+    pair = (2, local // 2, depth)
     return line_call(
         ffn_kernel, 2, "feed_forward",
         (
@@ -1299,7 +1303,7 @@
             shape(one, bf16),
             shape(gate, bf16),
             shape((PARAMS, width), f32),
-            shape((8, depth), f32),
+            shape((2, depth), f32),
         ),
         [
             IN_SMEM, IN_VMEM, *[IN_ANY] * 6, IN_VMEM, IN_VMEM, *[IN_ANY] * 4, IN_VMEM, IN_ANY,
@@ -1331,8 +1335,8 @@
             pltpu.VMEM(gate, bf16),
             pltpu.VMEM(gate, bf16),
             pltpu.VMEM((group, PARAMS, width), f32),
-            pltpu.VMEM((group, 8, depth), f32),
-            pltpu.VMEM((n, 8, depth), f32),
+            pltpu.VMEM((group, 2, depth), f32),
+            pltpu.VMEM((n, 2, depth), f32),
             *gather_sems(n),
             *scatter_sems(n),
             *scatter_sems(n),

time: 568 us -> 564 us (level)
  Pallas kernels: 539 us -> 533 us
    pallas_call x1, Pallas kernels: 215 us -> 208 us  [mixer_back(): line_call(back_kernel, 3, 'mixer_back', (shape((local, depth), bf16), sha...]
where the time goes in v6:
time: 564 us; the launch traced here: 559 us
  Pallas kernels  533 us (95%)
  other arithmetic  16 us (3%)
  local copies, waits for them, and re-layouts  8.48 us (2%)
    pallas_call x1, Pallas kernels, mixer_back(): line_call(back_kernel, 3, 'mixer_back', (shape((local, depth), bf16), sha...  208 us
    pallas_call x1, Pallas kernels, feed_forward(): line_call(ffn_kernel, 2, 'feed_forward', (shape((n, local, depth), bf16),...  163 us
    pallas_call x1, Pallas kernels, mixer_front(): line_call(front_kernel, 0, 'mixer_front', (shape((n, local, depth), bf16)...  162 us

profile of v6, /device:TPU:0, one launch (start us, length us, event | category | flops | bytes accessed | tf_op | source)
XLA Modules:
  0.0 559.1 jit_solution(3138638257424894569)
XLA Ops:
  0.7 0.0 copy-start.5
  0.7 1.4 fusion.10
  2.0 0.0 copy-start.11
  2.1 0.0 copy-start.13
  2.1 0.0 copy-start.14
  2.1 0.0 copy-start.15
  2.1 0.0 copy-start.12
  2.1 0.1 pad_add_fusion.1
  2.2 0.0 copy-done.5
  2.2 0.0 copy-start.9
  2.2 0.0 copy-start.10
  2.3 0.2 fusion.11
  2.5 0.1 pad_add_fusion
  2.6 0.9 pad_maximum_fusion.wg
  3.5 0.0 copy-done.11
  3.5 0.0 copy-done.13
  3.6 0.0 copy-done.14
  3.6 0.1 reshape.117
  3.7 0.0 copy-done.15
  3.7 0.1 reshape.118
  3.7 0.0 copy-done.12
  3.8 0.7 pad_select_fusion.par
  4.5 0.0 copy-done.9
  4.5 0.6 broadcast_in_dim.26
  5.1 0.0 copy-done.10
  5.1 0.6 broadcast_in_dim.27
  5.7 162.3 %mixer_front.1 = (bf16[8,256,2048]{2,1,0:T(8,128)(2,1)}, f32[2048,768]{1,0:T(8,128)}, f32[2048,1536]{1,0:T(8,128)}, bf16[2048,384]{1,0:T(8,128)(2,1)}, bf16[768,...) custom-call(s32[1,8]{1,0:T(1,128)} %lengths.3, ...), custom_call_target="tpu_custom_call" | custom-call | tf_op jit(solution)/shard_map/mixer_front/pallas_call | solution.py:685
  168.0 162.7 %feed_forward.1 = (bf16[8,256,2048]{2,1,0:T(8,128)(2,1)}, bf16[4,3,512,768]{3,2,1,0:T(8,128)(2,1)}, bf16[2,512,768]{2,1,0:T(8,128)(2,1)}, f32[256,2048]{1,0:T(8,...) custom-call(bf16[256,2048]{1,0:T(8,128)(2,1)} %get-tuple-element.41.low, ...), custom_call_target="tpu_custom_call" | custom-call | tf_op jit(solution)/shard_map/feed_forward/pallas_call | solution.py:892
  330.7 0.0 copy-start.1
  330.8 208.2 %mixer_back.1 = (bf16[256,2048]{1,0:T(8,128)(2,1)}, bf16[2,3,512,768]{3,2,1,0:T(8,128)(2,1)}, bf16[512,768]{1,0:T(8,128)(2,1)}, bf16[256,2048]{1,0:T(8,128)(2,1)...) custom-call(s32[1,8]{1,0:T(1,128)} %lengths.3, ...), custom_call_target="tpu_custom_call" | custom-call | tf_op jit(solution)/shard_map/mixer_back/pallas_call | solution.py:1295
  539.0 0.0 copy-done.1
  539.0 0.0 copy-start.6
  539.0 6.0 %convert_add_fusion.3 = (f32[512,768]{1,0:T(8,128)}, f32[512,768]{1,0:T(8,128)}, f32[512,768]{1,0:T(8,128)}) fusion(bf16[4,3,512,768]{3,2,1,0:T(8,128)(2,1)} %get-tuple-element.46.terms, s32[]{:T(128)S(6)} %select_n.14, s32[]{:T(128)S(6)} %add.72, bf16[2,3,512,768]{3,2,1,0:T(8,128)(2,1)} %get-tuple-element.63, bf16[2,512,768]{2,1,0:T(8,128)(2,1)S(1)} %copy-done.1, ...), kind=kLoop, calls=%fused_computation.5 | loop fusion | flops 8257536 | bytes 14155788 | tf_op jit(solution)/shard_map/add | solution.py:1421
  545.0 0.0 copy-done.6
  545.0 0.1 bitcast_convert_fusion
  545.2 0.0 copy-start
  545.2 0.2 slice_bitcast_fusion
  545.3 0.2 copy.39
  545.5 0.1 stack.22
  545.7 1.1 maximum_bitcast_fusion.1
  546.8 1.0 copy.40
  547.8 0.0 copy-done
  547.8 0.0 copy-start.2
  547.8 3.2 slice_convert_fusion
  551.0 0.0 copy-done.2
  551.0 0.0 copy-start.7
  551.0 0.0 copy-start.8
  551.0 0.0 copy-start.4
  551.0 1.9 convert_bitcast_fusion
  552.9 0.0 copy-start.3
  552.9 0.0 copy-done.7
  552.9 0.6 fusion.12
  553.5 0.0 copy-done.8
  553.6 0.6 slice_reduce_fusion
  554.2 0.6 fusion.4
  554.8 0.7 reshape_squeeze.6
  555.4 0.7 reshape_squeeze.7
  556.1 0.6 slice.109
  556.7 0.0 copy-done.4
  556.7 1.0 copy.51
  557.6 0.0 copy-done.3
  557.6 1.0 copy.52
  (9 shorter events, 0.1 us)
Async XLA Ops:
  0.7 1.6 copy-start.5
  2.0 1.5 copy-start.11
  2.1 1.5 copy-start.13
  2.1 1.5 copy-start.14
  2.1 1.6 copy-start.15
  2.1 1.6 copy-start.12
  2.2 2.2 copy-start.9
  2.2 2.8 copy-start.10
  330.7 208.2 %copy-start.1 = (bf16[2,512,768]{2,1,0:T(8,128)(2,1)S(1)}, bf16[2,512,768]{2,1,0:T(8,128)(2,1)}, u32[]{:S(2)}) copy-start(bf16[2,512,768]{2,1,0:T(8,128)(2,1)} %get-tuple-element.62) | copy-start | bytes 4718596
  539.0 6.0 %copy-start.6 = (bf16[4,96,768]{2,1,0:T(8,128)(2,1)S(1)}, bf16[4,96,768]{2,1,0:T(8,128)(2,1)}, u32[]{:S(2)}) copy-start(bf16[4,96,768]{2,1,0:T(8,128)(2,1)} %get-tuple-element.61) | copy-start | bytes 1769476
  545.2 2.6 copy-start
  547.8 3.2 copy-start.2
  551.0 1.9 copy-start.7
  551.0 2.5 copy-start.8
  551.0 5.6 %copy-start.4 = (bf16[256,2048]{1,0:T(8,128)(2,1)S(1)}, bf16[256,2048]{1,0:T(8,128)(2,1)}, u32[]{:S(2)}) copy-start(bf16[256,2048]{1,0:T(8,128)(2,1)} %get-tuple-element.122) | copy-start | bytes 3145732
  552.9 4.7 copy-start.3

commit v7 on v6

--- a/solution.py
+++ b/solution.py
@@ -1209,19 +1209,6 @@
     load_resid = pltpu.make_async_copy(resid, wide, wide_sem.at[1])
 
     def step(t):
-        scatter.step(t)
-        ahead(t + 1)
-
-        @pl.when(t == OUT_AT)
-        def _():
-            outs.arrive()
-            load_hidden.wait()
-            strips(local, settle_out)
-            outs.finish()
-            load_resid.start()
-            load.start()
-            compute(j, 3)
-
         @pl.when(t == OUT_AT + 1)
         def _():
             load.wait()
@@ -1232,6 +1219,19 @@
                 )
             pack(iterms, acc, width)
             isum.start()
+
+        scatter.step(t)
+        ahead(t + 1)
+
+        @pl.when(t == OUT_AT)
+        def _():
+            outs.arrive()
+            load_hidden.wait()
+            strips(local, settle_out)
+            outs.finish()
+            load_resid.start()
+            load.start()
+            compute(j, 3)
 
         @pl.when(t == OUT_AT + 2)
         def _():

time: 564 us -> 564 us (level)
  no operation moved by 1% of the time
where the time goes in v7:
time: 564 us; the launch traced here: 559 us
  Pallas kernels  533 us (95%)
  other arithmetic  16 us (3%)
  local copies, waits for them, and re-layouts  8.48 us (2%)
    pallas_call x1, Pallas kernels, mixer_back(): line_call(back_kernel, 3, 'mixer_back', (shape((local, depth), bf16), sha...  208 us
    pallas_call x1, Pallas kernels, feed_forward(): line_call(ffn_kernel, 2, 'feed_forward', (shape((n, local, depth), bf16),...  163 us
    pallas_call x1, Pallas kernels, mixer_front(): line_call(front_kernel, 0, 'mixer_front', (shape((n, local, depth), bf16)...  162 us

profile of v7, /device:TPU:0, one launch (start us, length us, event | category | flops | bytes accessed | tf_op | source)
XLA Modules:
  0.0 559.1 jit_solution(12776957984931170205)
XLA Ops:
  0.7 0.0 copy-start.5
  0.7 1.4 fusion.10
  2.0 0.0 copy-start.11
  2.1 0.0 copy-start.13
  2.1 0.0 copy-start.14
  2.1 0.0 copy-start.15
  2.1 0.0 copy-start.12
  2.1 0.1 pad_add_fusion.1
  2.2 0.0 copy-done.5
  2.2 0.0 copy-start.9
  2.2 0.0 copy-start.10
  2.3 0.2 fusion.11
  2.5 0.1 pad_add_fusion
  2.6 0.9 pad_maximum_fusion.wg
  3.5 0.0 copy-done.11
  3.5 0.0 copy-done.13
  3.6 0.0 copy-done.14
  3.6 0.1 reshape.117
  3.7 0.0 copy-done.15
  3.7 0.1 reshape.118
  3.7 0.0 copy-done.12
  3.8 0.7 pad_select_fusion.par
  4.5 0.0 copy-done.9
  4.5 0.6 broadcast_in_dim.26
  5.1 0.0 copy-done.10
  5.1 0.6 broadcast_in_dim.27
  5.7 162.3 %mixer_front.1 = (bf16[8,256,2048]{2,1,0:T(8,128)(2,1)}, f32[2048,768]{1,0:T(8,128)}, f32[2048,1536]{1,0:T(8,128)}, bf16[2048,384]{1,0:T(8,128)(2,1)}, bf16[768,...) custom-call(s32[1,8]{1,0:T(1,128)} %lengths.3, ...), custom_call_target="tpu_custom_call" | custom-call | tf_op jit(solution)/shard_map/mixer_front/pallas_call | solution.py:685
  168.0 162.7 %feed_forward.1 = (bf16[8,256,2048]{2,1,0:T(8,128)(2,1)}, bf16[4,3,512,768]{3,2,1,0:T(8,128)(2,1)}, bf16[2,512,768]{2,1,0:T(8,128)(2,1)}, f32[256,2048]{1,0:T(8,...) custom-call(bf16[256,2048]{1,0:T(8,128)(2,1)} %get-tuple-element.41.low, ...), custom_call_target="tpu_custom_call" | custom-call | tf_op jit(solution)/shard_map/feed_forward/pallas_call | solution.py:892
  330.7 0.0 copy-start.1
  330.8 208.2 %mixer_back.1 = (bf16[256,2048]{1,0:T(8,128)(2,1)}, bf16[2,3,512,768]{3,2,1,0:T(8,128)(2,1)}, bf16[512,768]{1,0:T(8,128)(2,1)}, bf16[256,2048]{1,0:T(8,128)(2,1)...) custom-call(s32[1,8]{1,0:T(1,128)} %lengths.3, ...), custom_call_target="tpu_custom_call" | custom-call | tf_op jit(solution)/shard_map/mixer_back/pallas_call | solution.py:1295
  539.0 0.0 copy-done.1
  539.0 0.0 copy-start.6
  539.0 6.0 %convert_add_fusion.3 = (f32[512,768]{1,0:T(8,128)}, f32[512,768]{1,0:T(8,128)}, f32[512,768]{1,0:T(8,128)}) fusion(bf16[4,3,512,768]{3,2,1,0:T(8,128)(2,1)} %get-tuple-element.46.terms, s32[]{:T(128)S(6)} %select_n.14, s32[]{:T(128)S(6)} %add.72, bf16[2,3,512,768]{3,2,1,0:T(8,128)(2,1)} %get-tuple-element.63, bf16[2,512,768]{2,1,0:T(8,128)(2,1)S(1)} %copy-done.1, ...), kind=kLoop, calls=%fused_computation.5 | loop fusion | flops 8257536 | bytes 14155788 | tf_op jit(solution)/shard_map/add | solution.py:1421
  545.0 0.0 copy-done.6
  545.0 0.1 bitcast_convert_fusion
  545.2 0.0 copy-start
  545.2 0.2 slice_bitcast_fusion
  545.3 0.2 copy.39
  545.5 0.1 stack.22
  545.7 1.1 maximum_bitcast_fusion.1
  546.8 1.0 copy.40
  547.8 0.0 copy-done
  547.8 0.0 copy-start.2
  547.8 3.2 slice_convert_fusion
  551.0 0.0 copy-done.2
  551.0 0.0 copy-start.7
  551.0 0.0 copy-start.8
  551.0 0.0 copy-start.4
  551.0 1.9 convert_bitcast_fusion
  552.9 0.0 copy-start.3
  552.9 0.0 copy-done.7
  552.9 0.6 fusion.12
  553.6 0.0 copy-done.8
  553.6 0.6 slice_reduce_fusion
  554.2 0.6 fusion.4
  554.8 0.7 reshape_squeeze.6
  555.4 0.7 reshape_squeeze.7
  556.1 0.6 slice.109
  556.7 0.0 copy-done.4
  556.7 1.0 copy.51
  557.6 0.0 copy-done.3
  557.7 1.0 copy.52
  (9 shorter events, 0.1 us)
Async XLA Ops:
  0.7 1.6 copy-start.5
  2.0 1.5 copy-start.11
  2.1 1.5 copy-start.13
  2.1 1.5 copy-start.14
  2.1 1.6 copy-start.15
  2.1 1.6 copy-start.12
  2.2 2.2 copy-start.9
  2.2 2.8 copy-start.10
  330.7 208.3 %copy-start.1 = (bf16[2,512,768]{2,1,0:T(8,128)(2,1)S(1)}, bf16[2,512,768]{2,1,0:T(8,128)(2,1)}, u32[]{:S(2)}) copy-start(bf16[2,512,768]{2,1,0:T(8,128)(2,1)} %get-tuple-element.62) | copy-start | bytes 4718596
  539.0 6.0 %copy-start.6 = (bf16[4,96,768]{2,1,0:T(8,128)(2,1)S(1)}, bf16[4,96,768]{2,1,0:T(8,128)(2,1)}, u32[]{:S(2)}) copy-start(bf16[4,96,768]{2,1,0:T(8,128)(2,1)} %get-tuple-element.61) | copy-start | bytes 1769476
  545.2 2.6 copy-start
  547.8 3.2 copy-start.2
  551.0 1.9 copy-start.7
  551.0 2.5 copy-start.8
  551.0 5.6 %copy-start.4 = (bf16[256,2048]{1,0:T(8,128)(2,1)S(1)}, bf16[256,2048]{1,0:T(8,128)(2,1)}, u32[]{:S(2)}) copy-start(bf16[256,2048]{1,0:T(8,128)(2,1)} %get-tuple-element.122) | copy-start | bytes 3145732
  552.9 4.7 copy-start.3
